TPU v7x, 128 devices: a whole 4x4x4 slice. The times are simulated.
128 devices in a mesh: wide: 32 (over y, x, core), quad: 4 (over z).
Axes of the slice: x: 4, y: 4, z: 4, core: 2. Of those that a mesh axis runs over, the one named last changes fastest.
Arguments:
- basis: float32 [16, 8388608], P(None, ('wide', 'quad')), may hold values from -6 to 6
- target: float32 [8388608], P(('wide', 'quad')), may hold values from -6 to 6
- sign_bits: int32 [8388608], P(('wide', 'quad')), may hold values from 0 to 1
- samples: int32 [32768], replicated, may hold values from 0 to 8388607
- owners: int32 [32768], replicated, may hold values from 0 to 7
Outputs:
- sketch: float32 [32768, 17], P(('wide', 'quad'))
- gram: float32 [8, 16, 17], P('quad')
Inputs may be any that keep to these rules, and one draw needn't show every extreme that they name: `samples`: sampled scenarios may repeat.
All inputs are finite; a program needn't handle non-finite values.
Results may differ from a plain program's by a relative error of at most 0.0003.
Values sent between devices are 32-bit elements; how exact they have to be, the bound alone decides.
No kernel may reach another device: no remote copies, remote signals or barrier semaphores. Data moves between devices by JAX's collectives and lax.ppermute only.
A program may use at most 128 MiB of HBM per device.

v0:
```python
import math

import jax
import jax.numpy as jnp
from jax import lax
from jax.sharding import PartitionSpec as P

GROUPS = 8


def parity_sign(first, second, nbits):
    count = jnp.zeros_like(first)
    for bit in range(nbits):
        count = count + ((first & second) >> bit) & 1
    return (1 - 2 * (count & 1)).astype(jnp.float32)


def walsh_table(order):
    nbits = order.bit_length() - 1
    line = jnp.arange(order, dtype=jnp.int32)
    return parity_sign(line[:, None], line[None, :], nbits)


def shards(basis, target, sign_bits, samples, owners):
    rows = basis.shape[1]
    block = math.isqrt(rows)
    n_wide = lax.axis_size("wide")
    n_quad = lax.axis_size("quad")
    devices = n_wide * n_quad
    my_wide = lax.axis_index("wide")
    my_quad = lax.axis_index("quad")
    my_device = my_wide * n_quad + my_quad
    total_samples = samples.shape[0]
    per_dev = total_samples // devices
    scale = 1.0 / math.sqrt(rows * devices)
    flip = (1 - 2 * sign_bits).astype(jnp.float32)
    signed = jnp.concatenate([basis, target[None, :]], axis=0) * flip[None, :]
    width = signed.shape[0]
    table = walsh_table(block)
    cube = signed.reshape(width, block, block)
    cube = jnp.einsum("kab,ac->kcb", cube, table, precision=lax.Precision.HIGHEST)
    cube = jnp.einsum("kcb,bd->kcd", cube, table, precision=lax.Precision.HIGHEST)
    local = cube.reshape(width, rows)
    all_bits = devices.bit_length() - 1
    slots = jnp.arange(total_samples, dtype=jnp.int32)
    number = samples[slots]
    values = jnp.take(local, number % rows, axis=1)
    source, values = (number // rows, values)
    sign = parity_sign(source, jnp.full_like(source, my_device), all_bits)
    term = values * (scale * sign)[None, :]
    columns = lax.psum_scatter(term, ("wide", "quad"), scatter_dimension=1, tiled=True)
    sketch = columns.T
    own_groups = lax.dynamic_slice_in_dim(owners, my_device * per_dev, per_dev, 0)
    onehot = (own_groups[:, None] == jnp.arange(GROUPS, dtype=jnp.int32)[None, :]).astype(
        jnp.float32
    )
    partial_gram = jnp.einsum(
        "rg,ri,rj->gij", onehot, sketch[:, : width - 1], sketch, precision=lax.Precision.HIGHEST
    )
    partial_gram = partial_gram * (GROUPS / total_samples)
    owned = GROUPS // n_quad
    summed = lax.psum(partial_gram, ("wide", "quad"))
    gram = lax.dynamic_slice_in_dim(summed, my_quad * owned, owned, 0)
    return (sketch, gram)


def solution(mesh):
    placed = (P(None, ("wide", "quad")), P(("wide", "quad")), P(("wide", "quad")), P(), P())
    return jax.shard_map(
        shards,
        mesh=mesh,
        in_specs=placed,
        out_specs=(P(("wide", "quad"), None), P("quad", None, None)),
        check_vma=False,
    )
```

profile of v0, /device:TPU:1, one launch (start us, length us, event | category | flops | bytes accessed | tf_op | source)
XLA Modules:
  0.0 1103.3 jit_solution(5172128148363246547)
XLA Ops:
  7.2 0.0 copy-start
  7.2 0.0 reduce-scatter.2.cloned.1.call-start
  7.2 0.0 copy-start.2
  7.3 1.1 concatenate.9
  8.3 5.4 copy.20
  13.7 0.0 copy-done.2
  13.7 0.1 mul.68
  13.8 6.7 fusion
  20.6 5.7 fusion.3
  26.2 18.3 %copy.18 = f32[17,256,256]{0,2,1:T(8,128)} copy(f32[17,256,256]{2,1,0:T(8,128)} %fusion.3) | data formatting | bytes 8912896 | tf_op jit(solution)/shard_map/reshape | solution.py:43
  44.5 0.0 copy-done
  44.5 180.5 %gather_fusion = s32[32768]{0:T(1024)S(1)} fusion(s32[32768]{0:T(1024)S(1)} %copy-done, s32[32768]{0:T(1024)S(1)} %iota_clamp_fusion), kind=kCustom, calls=%fused_computation | custom fusion | bytes 393216 | tf_op jit(solution)/shard_map/gather | solution.py:46
  225.1 0.1 compare_and_fusion
  225.2 0.5 compare_select_fusion
  225.7 0.2 convert_multiply_fusion
  225.9 119.5 %gather_fusion.1 = f32[32768,17]{1,0:T(8,128)} fusion(f32[17,65536]{0,1:T(8,128)} %bitcast.22, s32[32768]{0:T(1024)S(1)} %broadcast_clamp_fusion), kind=kCustom, calls=%fused_computation.1 | custom fusion | bytes 4587520 | tf_op jit(solution)/shard_map/jit(_take)/gather | solution.py:47
  345.3 13.2 %multiply_bitcast_fusion = f32[17,32768]{0,1:T(8,128)} fusion(f32[32768,17]{1,0:T(8,128)} %gather_fusion.1, f32[32768]{0:T(1024)S(1)} %convert_multiply_fusion, pred[32768]{0:T(1024)(128)(4,1)S(1)} %compare_and_fusion), kind=kLoop, calls=%fused_computation.2 | loop fusion | flops 1114112 | bytes 4620288 | tf_op jit(solution)/shard_map/mul | solution.py:50
  358.6 0.0 reduce-scatter.2.cloned.1.call-update
  358.6 0.0 copy-start.1
  358.6 0.8 dynamic_slice.6
  359.4 662.1 %reduce-scatter.2.cloned.1.call-done = f32[17,256]{0,1:T(8,128)} async-done(((f32[17,32768]{0,1:T(8,128)}), f32[17,256]{0,1:T(8,128)}) %reduce-scatter.2.cloned.1.call-update) | async-done | bytes 17424 | tf_op jit(solution)/shard_map/reduce_scatter | solution.py:51
  1021.5 1.6 copy.15
  1023.1 1.0 copy.13
  1024.1 1.2 fusion.6
  1025.3 70.5 %psum.7 = f32[8,16,17]{2,0,1:T(8,128)S(1)} all-reduce(f32[8,16,17]{2,0,1:T(8,128)S(1)} %fusion.6), channel_id=1, replica_groups=mesh['wide'=32,'quad'=4] {'wide','quad'}, use_global_device_ids=true, to_apply=%region_1.2 | all-reduce | flops 2176 | bytes 17408 | tf_op jit(solution)/shard_map/psum | solution.py:62
  1095.8 0.6 copy.16
  1096.4 0.0 copy-done.1
  (5 shorter events, 0.1 us)
Async XLA Ops:
  7.2 37.4 %copy-start = (s32[32768]{0:T(1024)S(1)}, s32[32768]{0:T(1024)}, u32[]{:S(2)}) copy-start(s32[32768]{0:T(1024)} %param.8) | copy-start | bytes 393220
  7.2 1014.4 %reduce-scatter.2.cloned.1.call-start = ((), (), s32[]{:S(2)}) async-start(), calls=%async_computation.1 | async-start | bytes 16908288 | tf_op jit(solution)/shard_map/reduce_scatter | solution.py:51
  7.2 6.5 copy-start.2
  358.6 737.8 %copy-start.1 = (s32[32768]{0:T(1024)S(1)}, s32[32768]{0:T(1024)}, u32[]{:S(2)}) copy-start(s32[32768]{0:T(1024)} %param.8) | copy-start | bytes 393220
Sparse Core Ops, SparseCore 0:
  358.7 662.7 reduce-scatter.1
where the time goes:
time: 1100 us
  waiting for transfers between devices  662 us (60%)
  local copies, waits for them, and re-layouts  329 us (30%)
  blocking collectives  70.5 us (6%)
  between operations  14.1 us (1%)
  other arithmetic  14 us (1%)
  matrix products  13.6 us (1%)
    reduce_scatter x1, waiting for transfers between devices, shards(): lax.psum_scatter(term, ('wide', 'quad'), scatter_dimension=1, tiled=True)  662 us
    gather x1, local copies, waits for them, and re-layouts, shards(): number = samples[slots]  181 us
    gather x1, local copies, waits for them, and re-layouts, shards(): values = jnp.take(local, number % rows, axis=1)  119 us
    psum x1, blocking collectives, shards(): summed = lax.psum(partial_gram, ('wide', 'quad'))  70.5 us
  transfers between devices with their start and end apart: 1, of which 1 were waited for; matrix products, arithmetic and copies ran while one was open for 0% of the time, Pallas kernels for 0%

commit v1 on v0

v1 whole, which is shorter than its diff:
```python
import math

import jax
import jax.numpy as jnp
from jax import lax
from jax.experimental import pallas as pl
from jax.experimental.pallas import tpu as pltpu
from jax.sharding import PartitionSpec as P

GROUPS = 8
AXES = ("wide", "quad")
LANES = 128
COLS = 17
PAD = 24
SIDE = 256
ORDERS = (("y", "x", "z"), ("z", "y", "x"))
PEEL = 6
STEP = 4


def number(y, x, c, z):
    return ((y * 4 + x) * 2 + c) * 4 + z


def shift(axis, off):
    pairs = []
    for y in range(4):
        for x in range(4):
            for c in range(2):
                for z in range(4):
                    at = {"y": y, "x": x, "c": c, "z": z}
                    size = 2 if axis == "c" else 4
                    to = dict(at)
                    to[axis] = (at[axis] + off) % size
                    pairs.append((number(**at), number(**to)))
    return pairs


def fold(v):
    v = v ^ (v >> 8)
    v = v ^ (v >> 4)
    v = v ^ (v >> 2)
    v = v ^ (v >> 1)
    return v & 1


def lane_take(tile, index):
    return jnp.take_along_axis(tile, index, axis=1)


def sort_kernel(pos_ref, samples_ref, keys_ref, ends_ref, scratch):
    me = pos_ref[0]
    sub = lax.broadcasted_iota(jnp.int32, (8, LANES), 0)
    lane = lax.broadcasted_iota(jnp.int32, (8, LANES), 1)
    for c in range(2):
        v = []
        for i in range(16):
            s = samples_ref[i, c]
            p = s & 65535
            place = (((p >> 7) & 1) << 15) | ((p >> 8) << 7) | (p & 127)
            odd = fold((s >> 16) & me)
            r = i * 1024 + sub * LANES + lane
            v.append((place << 15) | (r << 1) | odd)
        for k in range(1, 15):
            for b in (k - 1, k):
                if b == 0 or b == 14:
                    continue
                if b < 4:
                    v = [~t if (i >> b) & 1 else t for i, t in enumerate(v)]
                else:
                    bit = (sub >> (b - 4)) if b < 7 else (lane >> (b - 7))
                    m = -(bit & 1)
                    v = [t ^ m for t in v]
            for j in range(k - 1, -1, -1):
                if j < 4:
                    new = list(v)
                    for i in range(16):
                        if not (i >> j) & 1:
                            a, b = v[i], v[i | (1 << j)]
                            new[i] = jnp.minimum(a, b)
                            new[i | (1 << j)] = jnp.maximum(a, b)
                    v = new
                elif j < 7:
                    d = 1 << (j - 4)
                    up = (sub & d) != 0
                    new = []
                    for t in v:
                        prev = pltpu.roll(t, d, 0)
                        nxt = prev if d == 4 else pltpu.roll(t, 8 - d, 0)
                        new.append(jnp.where(up, jnp.maximum(t, prev), jnp.minimum(t, nxt)))
                    v = new
                else:
                    d = 1 << (j - 7)
                    up = (lane & d) != 0
                    other = lane ^ d
                    new = []
                    for t in v:
                        o = lane_take(t, other)
                        new.append(jnp.where(up, jnp.maximum(t, o), jnp.minimum(t, o)))
                    v = new
        for i in range(16):
            scratch[pl.ds(i, 8, stride=16), :] = v[i]
        ends_ref[2 * c : 2 * c + 1, :] = scratch[0:1, :] >> 22
        ends_ref[2 * c + 1 : 2 * c + 2, :] = scratch[127:128, :] >> 22
        keys_ref[c * LANES : (c + 1) * LANES, :] = scratch[...].T


def sort_call(pos, samples):
    return pl.pallas_call(
        sort_kernel,
        out_shape=(
            jax.ShapeDtypeStruct((256, LANES), jnp.int32),
            jax.ShapeDtypeStruct((4, LANES), jnp.int32),
        ),
        in_specs=[pl.BlockSpec(memory_space=pltpu.SMEM), pl.BlockSpec(memory_space=pltpu.VMEM)],
        out_specs=(pl.BlockSpec(memory_space=pltpu.VMEM),) * 2,
        scratch_shapes=[pltpu.VMEM((LANES, LANES), jnp.int32)],
        name="sort_slots",
    )(pos, samples)


def split(x):
    hi = x.astype(jnp.bfloat16)
    lo = (x - hi.astype(jnp.float32)).astype(jnp.bfloat16)
    return hi, lo


def table256():
    a = lax.broadcasted_iota(jnp.int32, (SIDE, SIDE), 0)
    b = lax.broadcasted_iota(jnp.int32, (SIDE, SIDE), 1)
    return (1 - 2 * fold(a & b)).astype(jnp.float32).astype(jnp.bfloat16)


def dot(a, b):
    return lax.dot_general(a, b, (((1,), (0,)), ((), ())), preferred_element_type=jnp.float32)


def mix_kernel(scale, pos_ref, ends_ref, basis_ref, target_ref, bits_ref, keys_ref, k0, s0, k1, s1, tab):
    walsh = table256()
    flips = [(1 - 2 * bits_ref[pl.ds(bh, SIDE, stride=2), :]).astype(jnp.float32) for bh in range(2)]
    flip = jnp.concatenate(flips, axis=1)
    for k in range(COLS):
        if k < 16:
            base = (k // 8) * 4096 + k % 8
            halves = [basis_ref[pl.ds(base + 8 * bh, SIDE, stride=16), :] for bh in range(2)]
        else:
            halves = [target_ref[pl.ds(bh, SIDE, stride=2), :] for bh in range(2)]
        x = jnp.concatenate(halves, axis=1) * flip
        hi, lo = split(x)
        y = dot(hi, walsh) + dot(lo, walsh)
        hi, lo = split(y)
        z = dot(walsh, hi) + dot(walsh, lo)
        for bh in range(2):
            tab[pl.ds(bh * SIDE * PAD + k, SIDE, stride=PAD), :] = z[:, bh * LANES : (bh + 1) * LANES]

    core = pos_ref[1]
    for b, outs in ((0, (k0, s0)), (1, (k1, s1))):
        m1, m2, m3 = (pos_ref[2 + "yxz".index(a)] for a in ORDERS[b])
        for rel_core, out in enumerate(outs):
            c = core ^ rel_core

            def group(it, _, b=b, c=c, out=out, m1=m1, m2=m2, m3=m3):
                s12 = (((it >> 2) + m1) & 3) * 4 + (((it & 3) + m2) & 3)
                lows, spans, lanes_of, rows_of, weights = [], [], [], [], []
                for r3 in range(4):
                    j = b * 64 + s12 * 4 + ((r3 + m3) & 3)
                    key = jnp.broadcast_to(keys_ref[pl.ds(c * LANES + j, 1), :], (8, LANES))
                    low = ends_ref[2 * c, j]
                    lows.append(low)
                    spans.append(ends_ref[2 * c + 1, j] - low + 1)
                    lanes_of.append((key >> 15) & 127)
                    rows_of.append((key >> 22) - low)
                    weights.append(jnp.where((key & 1) != 0, -scale, scale))
                most = jnp.maximum(jnp.maximum(spans[0], spans[1]), jnp.maximum(spans[2], spans[3]))

                def add_rows(first, count, acc):
                    acc = list(acc)
                    for u in range(count):
                        for q in range(4):
                            row = jnp.minimum(lows[q] + first + u, 511)
                            hit = rows_of[q] == first + u
                            for t in range(3):
                                tile = tab[pl.ds(pl.multiple_of(row * PAD + 8 * t, 8), 8), :]
                                acc[q * 3 + t] = jnp.where(hit, lane_take(tile, lanes_of[q]), acc[q * 3 + t])
                    return tuple(acc)

                acc = tuple(jnp.zeros((8, LANES), jnp.float32) for _ in range(12))
                acc = add_rows(0, PEEL, acc)
                more = (jnp.maximum(most - PEEL, 0) + STEP - 1) // STEP
                acc = lax.fori_loop(0, more, lambda n, a: add_rows(PEEL + n * STEP, STEP, a), acc)
                base = it * (4 * COLS)
                for r3 in range(4):
                    for t in range(2):
                        out[pl.ds(base + r3 + 32 * t, 8, stride=4), :] = acc[r3 * 3 + t] * weights[r3]
                    out[pl.ds(base + r3 + 64, 1), :] = acc[r3 * 3 + 2][0:1] * weights[r3][0:1]
                return 0

            lax.fori_loop(0, 16, group, 0)


def mix_call(scale, pos, ends, basis, target, bits, keys):
    vmem = pl.BlockSpec(memory_space=pltpu.VMEM)
    smem = pl.BlockSpec(memory_space=pltpu.SMEM)
    part = jax.ShapeDtypeStruct((16 * 4 * COLS, LANES), jnp.float32)
    return pl.pallas_call(
        lambda *refs: mix_kernel(scale, *refs),
        out_shape=(part,) * 4,
        in_specs=[smem, smem, vmem, vmem, vmem, vmem],
        out_specs=(vmem,) * 4,
        scratch_shapes=[pltpu.VMEM((512 * PAD, LANES), jnp.float32)],
        compiler_params=pltpu.CompilerParams(vmem_limit_bytes=48 * 2**20),
        name="mix_and_pick",
    )(pos, ends, basis, target, bits, keys)


def own_block(pos_ref, b):
    m1, m2, m3 = (pos_ref[2 + "yxz".index(a)] for a in ORDERS[b])
    return b * 64 + (m1 * 4 + m2) * 4 + m3


def gram_kernel(factor, pos_ref, v0_ref, v1_ref, keys_ref, owners_ref, o0, o1, o2, o3):
    core, quad = pos_ref[1], pos_ref[4]
    sub = lax.broadcasted_iota(jnp.int32, (8, LANES), 0)
    values = jnp.concatenate([v0_ref[...], v1_ref[...]], axis=1)
    owner = []
    for b in range(2):
        row = core * LANES + own_block(pos_ref, b)
        r = (jnp.broadcast_to(keys_ref[pl.ds(row, 1), :], (8, LANES)) >> 1) & 16383
        found = jnp.zeros((8, LANES), jnp.int32)
        for i in range(16):
            tile = owners_ref[i, core]
            found = jnp.where((r >> 10) == i, lane_take(tile, r & 127), found)
        found = jnp.where(((r >> 7) & 7) == sub, found, 0)
        owner.append(jnp.sum(found, axis=0, keepdims=True))
    owner = jnp.concatenate(owner, axis=1)
    for rel, out in enumerate((o0, o1, o2, o3)):
        first = 2 * ((rel + quad) & 3)
        left = jnp.concatenate(
            [jnp.where(owner == first + g, values[:16], 0.0) for g in range(2)], axis=0
        )
        out[...] = factor * lax.dot_general(
            left, values, (((1,), (1,)), ((), ())),
            precision=lax.Precision.HIGHEST, preferred_element_type=jnp.float32,
        )


def gram_call(factor, pos, v0, v1, keys, owners):
    vmem = pl.BlockSpec(memory_space=pltpu.VMEM)
    smem = pl.BlockSpec(memory_space=pltpu.SMEM)
    return pl.pallas_call(
        lambda *refs: gram_kernel(factor, *refs),
        out_shape=(jax.ShapeDtypeStruct((32, COLS), jnp.float32),) * 4,
        in_specs=[smem] + [vmem] * 4,
        out_specs=(vmem,) * 4,
        name="slot_gram",
    )(pos, v0, v1, keys, owners)


def rank_kernel(pos_ref, keys_ref, rank_ref, acc):
    core = pos_ref[1]
    first = ((pos_ref[2] * 4 + pos_ref[3]) * 4 + pos_ref[4]) * 256
    sub = lax.broadcasted_iota(jnp.int32, (SIDE, LANES), 0)
    lane = lax.broadcasted_iota(jnp.int32, (1, LANES), 1)
    acc[...] = jnp.zeros_like(acc)

    def step(n, _):
        total = acc[...]
        for u in range(8):
            j = n * 8 + u
            r = ((keys_ref[pl.ds(core * LANES + j, 1), :] >> 1) & 16383) - first
            slot = j * LANES + lane
            total = jnp.where(sub == r, slot, total)
        acc[...] = total
        return 0

    lax.fori_loop(0, LANES // 8, step, 0)
    ones = jnp.ones((8, LANES), jnp.float32)
    rank_ref[...] = lax.dot_general(
        ones, acc[...].astype(jnp.float32), (((1,), (1,)), ((), ())),
        precision=lax.Precision.HIGHEST, preferred_element_type=jnp.float32,
    ).astype(jnp.int32)


def rank_call(pos, keys):
    vmem = pl.BlockSpec(memory_space=pltpu.VMEM)
    smem = pl.BlockSpec(memory_space=pltpu.SMEM)
    return pl.pallas_call(
        rank_kernel,
        out_shape=jax.ShapeDtypeStruct((8, SIDE), jnp.int32),
        in_specs=[smem, vmem],
        out_specs=vmem,
        scratch_shapes=[pltpu.VMEM((SIDE, LANES), jnp.int32)],
        name="row_rank",
    )(pos, keys)


def pick_kernel(pos_ref, rank_ref, *refs):
    parts, out = refs[:8], refs[8]
    rows = 16 * COLS
    at = lax.broadcasted_iota(jnp.int32, (rows, LANES), 0)
    code_row = (at // (4 * COLS)) * 4 + (at & 3)
    er = lax.broadcasted_iota(jnp.int32, (rows, COLS), 0)
    ek = lax.broadcasted_iota(jnp.int32, (rows, COLS), 1)
    collect = jnp.where((er % (4 * COLS)) // 4 == ek, 1.0, 0.0)
    for h in range(2):
        slot = rank_ref[:, h * LANES : (h + 1) * LANES]
        block = slot >> 7
        b = block >> 6
        rel = []
        for n in range(3):
            mine = [pos_ref[2 + "yxz".index(ORDERS[q][n])] for q in range(2)]
            mine = jnp.where(b == 0, mine[0], mine[1])
            rel.append((((block >> (4 - 2 * n)) & 3) - mine) & 3)
        index = slot & 127
        first = b * 4 + rel[0]
        acc = [jnp.zeros((8, LANES), jnp.float32)] * (rows // 8)
        for n, part in enumerate(parts):
            hit = first == n
            for t in range(rows // 8):
                acc[t] = jnp.where(hit, lane_take(part[8 * t : 8 * t + 8, :], index), acc[t])
        code = (rel[1] * 4 + rel[2])[0:1]
        chosen = jnp.where(code_row == code, jnp.concatenate(acc, axis=0), 0.0)
        out[h * LANES : (h + 1) * LANES, :] = lax.dot_general(
            chosen, collect, (((0,), (0,)), ((), ())),
            precision=lax.Precision.HIGHEST, preferred_element_type=jnp.float32,
        )


def pick_call(pos, rank, parts):
    vmem = pl.BlockSpec(memory_space=pltpu.VMEM)
    smem = pl.BlockSpec(memory_space=pltpu.SMEM)
    return pl.pallas_call(
        pick_kernel,
        out_shape=jax.ShapeDtypeStruct((SIDE, COLS), jnp.float32),
        in_specs=[smem] + [vmem] * 9,
        out_specs=vmem,
        name="pick_rows",
    )(pos, rank, *parts)


def send(v, axis, off):
    return lax.ppermute(v, AXES, shift(axis, off))


def shards(basis, target, sign_bits, samples, owners):
    rows = basis.shape[1]
    total_samples = samples.shape[0]
    scale = 1.0 / math.sqrt(rows * 128)
    wide = lax.axis_index("wide")
    z = lax.axis_index("quad")
    core, x, y = wide & 1, (wide >> 1) & 3, wide >> 3
    pos = jnp.stack([wide * 4 + z, core, y, x, z, z, z, z]).astype(jnp.int32)

    keys, ends = sort_call(pos, samples.reshape(16, 2, 8, LANES))
    tiles = basis.reshape(2, 8, 512, LANES).transpose(0, 2, 1, 3).reshape(8192, LANES)
    k0, s0, k1, s1 = mix_call(
        scale, pos, ends, tiles, target.reshape(512, LANES), sign_bits.reshape(512, LANES), keys
    )
    rank = rank_call(pos, keys)
    vals = [k0 + send(s0, "c", 1), k1 + send(s1, "c", 1)]
    for n in range(2):
        got = []
        for b in range(2):
            quarter = vals[b].reshape(4, -1, LANES)
            got.append([quarter[0]] + [send(quarter[o], ORDERS[b][n], o) for o in (2, 1, 3)])
        vals = [(g[0] + g[1]) + (g[2] + g[3]) for g in got]
    got = []
    for b in range(2):
        quarter = vals[b].reshape(COLS, 4, LANES)
        got.append([quarter[:, 0]] + [send(quarter[:, o], ORDERS[b][2], o) for o in (2, 1, 3)])
    vals = [(g[0] + g[1]) + (g[2] + g[3]) for g in got]

    grams = gram_call(GROUPS / total_samples, pos, vals[0], vals[1], keys, owners.reshape(16, 2, 8, LANES))
    gram = sum([send(grams[o], "z", o) for o in (1, 2, 3)], grams[0])
    for axis in ("y", "x"):
        gram = sum([send(gram, axis, o) for o in (1, 2, 3)], gram)
    gram = gram + send(gram, "c", 1)

    full = []
    for b in range(2):
        own = vals[b]
        axis = ORDERS[b][2]
        own = jnp.stack([own] + [send(own, axis, -o) for o in (1, 2, 3)], axis=1).reshape(4 * COLS, LANES)
        axis = ORDERS[b][1]
        own = jnp.concatenate([own] + [send(own, axis, -o) for o in (1, 2, 3)], axis=0)
        axis = ORDERS[b][0]
        full += [own] + [send(own, axis, -o) for o in (1, 2, 3)]
    sketch = pick_call(pos, rank, full)
    return sketch, gram.reshape(2, 16, COLS)


def solution(mesh):
    placed = (P(None, AXES), P(AXES), P(AXES), P(), P())
    return jax.shard_map(
        shards,
        mesh=mesh,
        in_specs=placed,
        out_specs=(P(AXES, None), P("quad", None, None)),
        check_vma=False,
    )
```

time: 1100 us -> 128 us (0.12)
  waiting for transfers between devices: 662 us -> 9.74 us
  local copies, waits for them, and re-layouts: 329 us -> 7.32 us
  starting transfers between devices: 0.04 us -> 71.2 us
  blocking collectives: 70.5 us -> 0 us
  Pallas kernels: 0 us -> 33.2 us
  matrix products: 13.6 us -> 0 us
  between operations: 14.1 us -> 0.95 us
    reduce_scatter x1 -> x0, waiting for transfers between devices: 662 us -> none  [shards(): lax.psum_scatter(term, ('wide', 'quad'), scatter_dimension=1, tiled=True)]
    gather x2 -> x0, local copies, waits for them, and re-layouts: 300 us -> none  [the longest x1 181 us: shards(): number = samples[slots]]
    ppermute x0 -> x48, starting transfers between devices: none -> 71.2 us  [send(): return lax.ppermute(v, AXES, shift(axis, off))]
    psum x1 -> x0, blocking collectives: 70.5 us -> none  [shards(): summed = lax.psum(partial_gram, ('wide', 'quad'))]
    pallas_call x0 -> x5, Pallas kernels: none -> 33.2 us  [the longest x1 20.2 us: mix_call(): pl.pallas_call(lambda *refs: mix_kernel(scale, *refs), out_shape=(part,)...]
    reshape x1 -> x4, local copies, waits for them, and re-layouts: 18.3 us -> 0.06 us  [the longest x2 0.03 us: shards(): jnp.stack([own] + [send(own, axis, -o) for o in (1, 2, 3)], axis=1)]
    dot_general x3 -> x0, matrix products: 13.6 us -> none  [the longest x1 6.72 us: shards(): jnp.einsum('kab,ac->kcb', cube, table, precision=lax.Precision.HIGHEST)]
    mul x2 -> x0, other arithmetic: 13.4 us -> none  [shards(): term = values * (scale * sign)[None, :]]
  transfers between devices with their start and end apart: 1 -> 48, of which waited for: 1 -> 9; matrix products, arithmetic and copies ran while one was open for 0% -> 2% of each run, Pallas kernels for 0% -> 2%
where the time goes in v1:
time: 128 us; the launch traced here: 127 us
  starting transfers between devices  71.2 us (56%)
  Pallas kernels  33.2 us (26%)
  waiting for transfers between devices  9.74 us (8%)
  local copies, waits for them, and re-layouts  7.32 us (6%)
  other arithmetic  4.22 us (3%)
    ppermute x48, starting transfers between devices, send(): return lax.ppermute(v, AXES, shift(axis, off))  71.2 us
    pallas_call x1, Pallas kernels, mix_call(): pl.pallas_call(lambda *refs: mix_kernel(scale, *refs), out_shape=(part,)...  20.2 us
    ppermute x48, waiting for transfers between devices, send(): return lax.ppermute(v, AXES, shift(axis, off))  9.74 us
    unnamed x33, local copies, waits for them, and re-layouts  6.43 us
    pallas_call x1, Pallas kernels, sort_call(): pl.pallas_call(sort_kernel, out_shape=(jax.ShapeDtypeStruct((256, LANES),...  4.77 us
    pallas_call x1, Pallas kernels, pick_call(): pl.pallas_call(pick_kernel, out_shape=jax.ShapeDtypeStruct((SIDE, COLS),...  3.3 us
    pallas_call x1, Pallas kernels, rank_call(): pl.pallas_call(rank_kernel, out_shape=jax.ShapeDtypeStruct((8, SIDE), jnp...  2.99 us
  transfers between devices with their start and end apart: 48, of which 9 were waited for; matrix products, arithmetic and copies ran while one was open for 2% of the time, Pallas kernels for 2%

profile of v1, /device:TPU:1, one launch (start us, length us, event | category | flops | bytes accessed | tf_op | source)
XLA Modules:
  0.0 126.6 jit_solution(16837947616617477783)
XLA Ops:
  1.3 4.8 %sort_slots.1 = (s32[256,128]{1,0:T(8,128)}, s32[4,128]{1,0:T(4,128)}) custom-call(s32[8]{0:T(128)} %stack.56.pos_ref.refs_0_, s32[16,2,8,128]{3,2,1,0:T(8,128)} %bitcast.56), custom_call_target="tpu_custom_call" | custom-call | tf_op jit(solution)/shard_map/sort_slots/pallas_call | solution.py:109
  6.1 0.9 copy-done
  7.0 0.9 copy-done.1
  7.9 0.9 copy-done.2
  10.2 20.2 %mix_and_pick.1 = (f32[1088,128]{1,0:T(8,128)S(1)}, f32[1088,128]{1,0:T(8,128)S(1)}, f32[1088,128]{1,0:T(8,128)S(1)}, f32[1088,128]{1,0:T(8,128)S(1)}) custom-call(s32[8]{0:T(128)S(1)} %copy-done.3, s32[4,128]{1,0:T(4,128)S(1)} %copy-done.4, f32[8192,128]{1,0:T(8,128)} %bitcast.55, f32[512,128]{1,0:T(8,128)S(1)} %bitcast.53, s32[512,128]{1,0:T(8,128)S(1)} %bitcast.54, ...), custom_call_target="tpu_custom_call" | custom-call | tf_op jit(solution)/shard_map/mix_and_pick/pallas_call | solution.py:205
  30.4 1.5 %collective-permute-start.19 = (f32[1088,128]{1,0:T(8,128)S(1)}, f32[1088,128]{1,0:T(8,128)S(1)}, u32[]{:S(2)}, u32[]{:S(2)}) collective-permute-start(f32[1088,128]{1,0:T(8,128)S(1)} %get-tuple-element.17), channel_id=1, source_target_pairs={{0,4},{1,5},{2,6},{3,7},{4,0},{5,1},{6,2},{7,3},{8,12},{9,13},{10,... | collective-permute-start | bytes 1671176 | tf_op jit(solution)/shard_map/ppermute | solution.py:342
  32.0 1.5 %collective-permute-done.19 = f32[1088,128]{1,0:T(8,128)S(1)} collective-permute-done((f32[1088,128]{1,0:T(8,128)S(1)}, f32[1088,128]{1,0:T(8,128)S(1)}, u32[]{:S(2)}, u32[]{:S(2)}) %collective-permute-start.19) | collective-permute-done | bytes 557088 | tf_op jit(solution)/shard_map/ppermute | solution.py:342
  33.6 3.8 %collective-permute-start.20 = (f32[272,128]{1,0:T(8,128)S(1)}, f32[272,128]{1,0:T(8,128)S(1)}, u32[]{:S(2)}, u32[]{:S(2)}) collective-permute-start(f32[272,128]{1,0:T(8,128)S(1)} %get-tuple-element.28), channel_id=1, source_target_pairs={{0,2},{1,3},{2,0},{3,1},{4,6},{5,7},{6,4},{7,5},{8,10},{9,11},{10,... | collective-permute-start | bytes 417800 | tf_op jit(solution)/shard_map/ppermute | solution.py:342
  37.4 0.7 collective-permute-start.21
  38.1 1.9 %collective-permute-start.22 = (f32[272,128]{1,0:T(8,128)S(1)}, f32[272,128]{1,0:T(8,128)S(1)}, u32[]{:S(2)}, u32[]{:S(2)}) collective-permute-start(f32[272,128]{1,0:T(8,128)S(1)} %get-tuple-element.26), channel_id=1, source_target_pairs={{0,3},{1,0},{2,1},{3,2},{4,7},{5,4},{6,5},{7,6},{8,11},{9,8},{10,9... | collective-permute-start | bytes 417800 | tf_op jit(solution)/shard_map/ppermute | solution.py:342
  40.2 3.0 %collective-permute-start.1 = (f32[272,128]{1,0:T(8,128)S(1)}, f32[272,128]{1,0:T(8,128)S(1)}, u32[]{:S(2)}, u32[]{:S(2)}) collective-permute-start(f32[272,128]{1,0:T(8,128)S(1)} %get-tuple-element.31), channel_id=1, source_target_pairs={{0,64},{1,65},{2,66},{3,67},{4,68},{5,69},{6,70},{7,71},{8,72},{9,... | collective-permute-start | bytes 417800 | tf_op jit(solution)/shard_map/ppermute | solution.py:342
  43.6 2.3 %collective-permute-start.3 = (f32[272,128]{1,0:T(8,128)S(1)}, f32[272,128]{1,0:T(8,128)S(1)}, u32[]{:S(2)}, u32[]{:S(2)}) collective-permute-start(f32[272,128]{1,0:T(8,128)S(1)} %get-tuple-element.29), channel_id=1, source_target_pairs={{0,96},{1,97},{2,98},{3,99},{4,100},{5,101},{6,102},{7,103},{8,104... | collective-permute-start | bytes 417800 | tf_op jit(solution)/shard_map/ppermute | solution.py:342
  45.9 1.7 %collective-permute-start.23 = (f32[68,128]{1,0:T(8,128)S(1)}, f32[68,128]{1,0:T(8,128)S(1)}, u32[]{:S(2)}, u32[]{:S(2)}) collective-permute-start(f32[68,128]{1,0:T(8,128)S(1)} %get-tuple-element.34), channel_id=1, source_target_pairs={{0,64},{1,65},{2,66},{3,67},{4,68},{5,69},{6,70},{7,71},{8,72},{9,... | collective-permute-start | bytes 104456 | tf_op jit(solution)/shard_map/ppermute | solution.py:342
  48.0 2.3 %collective-permute-start.25 = (f32[68,128]{1,0:T(8,128)S(1)}, f32[68,128]{1,0:T(8,128)S(1)}, u32[]{:S(2)}, u32[]{:S(2)}) collective-permute-start(f32[68,128]{1,0:T(8,128)S(1)} %get-tuple-element.32), channel_id=1, source_target_pairs={{0,96},{1,97},{2,98},{3,99},{4,100},{5,101},{6,102},{7,103},{8,104... | collective-permute-start | bytes 104456 | tf_op jit(solution)/shard_map/ppermute | solution.py:342
  50.3 2.8 %collective-permute-start.4 = (f32[68,128]{1,0:T(8,128)S(1)}, f32[68,128]{1,0:T(8,128)S(1)}, u32[]{:S(2)}, u32[]{:S(2)}) collective-permute-start(f32[68,128]{1,0:T(8,128)S(1)} %get-tuple-element.37), channel_id=1, source_target_pairs={{0,16},{1,17},{2,18},{3,19},{4,20},{5,21},{6,22},{7,23},{8,24},{9,... | collective-permute-start | bytes 104456 | tf_op jit(solution)/shard_map/ppermute | solution.py:342
  53.5 2.4 %collective-permute-start.6 = (f32[68,128]{1,0:T(8,128)S(1)}, f32[68,128]{1,0:T(8,128)S(1)}, u32[]{:S(2)}, u32[]{:S(2)}) collective-permute-start(f32[68,128]{1,0:T(8,128)S(1)} %get-tuple-element.35), channel_id=1, source_target_pairs={{0,24},{1,25},{2,26},{3,27},{4,28},{5,29},{6,30},{7,31},{8,0},{9,1... | collective-permute-start | bytes 104456 | tf_op jit(solution)/shard_map/ppermute | solution.py:342
  56.6 2.2 %collective-permute-start.28 = (f32[17,128]{1,0:T(8,128)S(1)}, f32[17,128]{1,0:T(8,128)S(1)}, u32[]{:S(2)}, u32[]{:S(2)}) collective-permute-start(f32[17,128]{1,0:T(8,128)S(1)} %bitcast.69), channel_id=1, source_target_pairs={{0,24},{1,25},{2,26},{3,27},{4,28},{5,29},{6,30},{7,31},{8,0},{9,1... | collective-permute-start | bytes 26120 | tf_op jit(solution)/shard_map/ppermute | solution.py:342
  58.9 2.2 %collective-permute-start.7 = (f32[17,128]{1,0:T(8,128)S(1)}, f32[17,128]{1,0:T(8,128)S(1)}, u32[]{:S(2)}, u32[]{:S(2)}) collective-permute-start(f32[17,128]{1,0:T(8,128)S(1)} %bitcast.70), channel_id=1, source_target_pairs={{0,2},{1,3},{2,0},{3,1},{4,6},{5,7},{6,4},{7,5},{8,10},{9,11},{10,... | collective-permute-start | bytes 26120 | tf_op jit(solution)/shard_map/ppermute | solution.py:342
  61.0 1.0 collective-permute-start.8
  62.0 1.7 %collective-permute-start.9 = (f32[17,128]{1,0:T(8,128)S(1)}, f32[17,128]{1,0:T(8,128)S(1)}, u32[]{:S(2)}, u32[]{:S(2)}) collective-permute-start(f32[17,128]{1,0:T(8,128)S(1)} %bitcast.72), channel_id=1, source_target_pairs={{0,3},{1,0},{2,1},{3,2},{4,7},{5,4},{6,5},{7,6},{8,11},{9,8},{10,9... | collective-permute-start | bytes 26120 | tf_op jit(solution)/shard_map/ppermute | solution.py:342
  65.4 2.0 %slot_gram.1 = (f32[32,17]{1,0:T(8,128)}, f32[32,17]{1,0:T(8,128)}, f32[32,17]{1,0:T(8,128)}, f32[32,17]{1,0:T(8,128)}) custom-call(s32[8]{0:T(128)} %stack.56.pos_ref.refs_0_, f32[17,128]{1,0:T(8,128)} %fusion.7.refs_1_, f32[17,128]{1,0:T(8,128)} %fusion.5.refs_2_, s32[256,128]{1,0:T(8,128)} %get-tuple-element.12.keys_ref.refs_5_.refs_3_, ...), custom_call_target="tpu_custom_call" | custom-call | tf_op jit(solution)/shard_map/slot_gram/pallas_call | solution.py:250
  67.4 3.9 %collective-permute-start.39 = (f32[32,17]{1,0:T(8,128)}, f32[32,17]{1,0:T(8,128)S(1)}, u32[]{:S(2)}, u32[]{:S(2)}) collective-permute-start(f32[32,17]{1,0:T(8,128)} %get-tuple-element.20), channel_id=1, source_target_pairs={{0,2},{1,3},{2,0},{3,1},{4,6},{5,7},{6,4},{7,5},{8,10},{9,11},{10,... | collective-permute-start | bytes 6536 | tf_op jit(solution)/shard_map/ppermute | solution.py:342
  71.4 1.4 %collective-permute-done.39 = f32[32,17]{1,0:T(8,128)S(1)} collective-permute-done((f32[32,17]{1,0:T(8,128)}, f32[32,17]{1,0:T(8,128)S(1)}, u32[]{:S(2)}, u32[]{:S(2)}) %collective-permute-start.39) | collective-permute-done | bytes 2208 | tf_op jit(solution)/shard_map/ppermute | solution.py:342
  72.8 1.3 %collective-permute-done.40 = f32[32,17]{1,0:T(8,128)S(1)} collective-permute-done((f32[32,17]{1,0:T(8,128)}, f32[32,17]{1,0:T(8,128)S(1)}, u32[]{:S(2)}, u32[]{:S(2)}) %collective-permute-start.40) | collective-permute-done | bytes 2208 | tf_op jit(solution)/shard_map/ppermute | solution.py:342
  74.0 0.7 add_add_fusion.2
  74.8 2.3 %collective-permute-start.42 = (f32[32,17]{1,0:T(8,128)S(1)}, f32[32,17]{1,0:T(8,128)S(1)}, u32[]{:S(2)}, u32[]{:S(2)}) collective-permute-start(f32[32,17]{1,0:T(8,128)S(1)} %add_add_fusion.2), channel_id=1, source_target_pairs={{0,64},{1,65},{2,66},{3,67},{4,68},{5,69},{6,70},{7,71},{8,72},{9,... | collective-permute-start | bytes 6536 | tf_op jit(solution)/shard_map/ppermute | solution.py:342
  77.5 1.4 %collective-permute-start.29 = (f32[17,128]{1,0:T(8,128)}, f32[17,128]{1,0:T(8,128)S(1)}, u32[]{:S(2)}, u32[]{:S(2)}) collective-permute-start(f32[17,128]{1,0:T(8,128)} %fusion.5.refs_2_), channel_id=1, source_target_pairs={{0,24},{1,25},{2,26},{3,27},{4,28},{5,29},{6,30},{7,31},{8,0},{9,1... | collective-permute-start | bytes 26120 | tf_op jit(solution)/shard_map/ppermute | solution.py:342
  79.2 0.8 collective-permute-start.31
  80.0 1.2 collective-permute-start.10
  81.6 0.8 collective-permute-start.12
  83.1 0.8 collective-permute-start.44
  83.9 1.5 %collective-permute-start.45 = (f32[32,17]{1,0:T(8,128)S(1)}, f32[32,17]{1,0:T(8,128)S(1)}, u32[]{:S(2)}, u32[]{:S(2)}) collective-permute-start(f32[32,17]{1,0:T(8,128)S(1)} %add_add_fusion.1), channel_id=1, source_target_pairs={{0,16},{1,17},{2,18},{3,19},{4,20},{5,21},{6,22},{7,23},{8,24},{9,... | collective-permute-start | bytes 6536 | tf_op jit(solution)/shard_map/ppermute | solution.py:342
  86.2 1.1 collective-permute-start.32
  87.4 1.6 %collective-permute-start.33 = (f32[68,128]{1,0:T(8,128)S(1)}, f32[68,128]{1,0:T(8,128)S(1)}, u32[]{:S(2)}, u32[]{:S(2)}) collective-permute-start(f32[68,128]{1,0:T(8,128)S(1)} %reshape.81), channel_id=1, source_target_pairs={{0,64},{1,65},{2,66},{3,67},{4,68},{5,69},{6,70},{7,71},{8,72},{9,... | collective-permute-start | bytes 104456 | tf_op jit(solution)/shard_map/ppermute | solution.py:342
  89.5 0.7 pad_maximum_fusion.2
  90.3 1.6 %collective-permute-start.46 = (f32[32,17]{1,0:T(8,128)S(1)}, f32[32,17]{1,0:T(8,128)S(1)}, u32[]{:S(2)}, u32[]{:S(2)}) collective-permute-start(f32[32,17]{1,0:T(8,128)S(1)} %add_add_fusion.1), channel_id=1, source_target_pairs={{0,24},{1,25},{2,26},{3,27},{4,28},{5,29},{6,30},{7,31},{8,0},{9,1... | collective-permute-start | bytes 6536 | tf_op jit(solution)/shard_map/ppermute | solution.py:342
  91.9 1.0 collective-permute-start.13
  93.0 1.4 %collective-permute-start.14 = (f32[68,128]{1,0:T(8,128)S(1)}, f32[68,128]{1,0:T(8,128)S(1)}, u32[]{:S(2)}, u32[]{:S(2)}) collective-permute-start(f32[68,128]{1,0:T(8,128)S(1)} %reshape.79), channel_id=1, source_target_pairs={{0,16},{1,17},{2,18},{3,19},{4,20},{5,21},{6,22},{7,23},{8,24},{9,... | collective-permute-start | bytes 104456 | tf_op jit(solution)/shard_map/ppermute | solution.py:342
  94.4 1.0 collective-permute-start.15
  95.4 1.9 %collective-permute-start.35 = (f32[272,128]{1,0:T(8,128)S(1)}, f32[272,128]{1,0:T(8,128)S(1)}, u32[]{:S(2)}, u32[]{:S(2)}) collective-permute-start(f32[272,128]{1,0:T(8,128)S(1)} %pad_maximum_fusion.1.refs_4_), channel_id=1, source_target_pairs={{0,3},{1,0},{2,1},{3,2},{4,7},{5,4},{6,5},{7,6},{8,11},{9,8},{10,9... | collective-permute-start | bytes 417800 | tf_op jit(solution)/shard_map/ppermute | solution.py:342
  97.4 12.2 %collective-permute-start.47 = (f32[32,17]{1,0:T(8,128)S(1)}, f32[32,17]{1,0:T(8,128)S(1)}, u32[]{:S(2)}, u32[]{:S(2)}) collective-permute-start(f32[32,17]{1,0:T(8,128)S(1)} %add_add_fusion), channel_id=1, source_target_pairs={{0,4},{1,5},{2,6},{3,7},{4,0},{5,1},{6,2},{7,3},{8,12},{9,13},{10,... | collective-permute-start | bytes 6536 | tf_op jit(solution)/shard_map/ppermute | solution.py:342
  109.6 1.5 %collective-permute-start.36 = (f32[272,128]{1,0:T(8,128)S(1)}, f32[272,128]{1,0:T(8,128)S(1)}, u32[]{:S(2)}, u32[]{:S(2)}) collective-permute-start(f32[272,128]{1,0:T(8,128)S(1)} %pad_maximum_fusion.1.refs_4_), channel_id=1, source_target_pairs={{0,2},{1,3},{2,0},{3,1},{4,6},{5,7},{6,4},{7,5},{8,10},{9,11},{10,... | collective-permute-start | bytes 417800 | tf_op jit(solution)/shard_map/ppermute | solution.py:342
  112.4 0.9 collective-permute-start.18
  113.2 3.0 %row_rank.1.rank_ref = s32[8,256]{1,0:T(8,128)} custom-call(s32[8]{0:T(128)} %stack.56.pos_ref.refs_0_, s32[256,128]{1,0:T(8,128)} %get-tuple-element.12.keys_ref.refs_5_.refs_3_), custom_call_target="tpu_custom_call" | custom-call | tf_op jit(solution)/shard_map/row_rank/pallas_call | solution.py:287
  116.9 2.9 %collective-permute-done.37.refs_7_ = f32[272,128]{1,0:T(8,128)S(1)} collective-permute-done((f32[272,128]{1,0:T(8,128)S(1)}, f32[272,128]{1,0:T(8,128)S(1)}, u32[]{:S(2)}, u32[]{:S(2)}) %collective-permute-start.37) | collective-permute-done | bytes 139296 | tf_op jit(solution)/shard_map/ppermute | solution.py:342
  119.7 1.3 %collective-permute-done.18.refs_3_ = f32[272,128]{1,0:T(8,128)S(1)} collective-permute-done((f32[272,128]{1,0:T(8,128)S(1)}, f32[272,128]{1,0:T(8,128)S(1)}, u32[]{:S(2)}, u32[]{:S(2)}) %collective-permute-start.18) | collective-permute-done | bytes 139296 | tf_op jit(solution)/shard_map/ppermute | solution.py:342
  121.8 3.3 %pick_rows.1 = f32[256,17]{1,0:T(8,128)} custom-call(s32[8]{0:T(128)} %stack.56.pos_ref.refs_0_, s32[8,256]{1,0:T(8,128)} %row_rank.1.rank_ref, f32[272,128]{1,0:T(8,128)} %copy-done.6, f32[272,128]{1,0:T(8,128)} %copy-done.10, f32[272,128]{1,0:T(8,128)} %copy-done.11, f32[272,128]{1,0:T(8,128)} %copy-done.12, f32[272,128]{1,0:T(8,128)} %copy-done.5, ...), custom_call_target="tpu_custom_call" | custom-call | tf_op jit(solution)/shard_map/pick_rows/pallas_call | solution.py:332
  125.0 1.6 %copy.18 = f32[256,17]{0,1:T(8,128)} copy(f32[256,17]{1,0:T(8,128)} %pick_rows.1) | data formatting | bytes 34816
  (115 shorter events, 12.0 us)
Async XLA Ops:
  30.4 3.1 %collective-permute-start.19 = (f32[1088,128]{1,0:T(8,128)S(1)}, f32[1088,128]{1,0:T(8,128)S(1)}, u32[]{:S(2)}, u32[]{:S(2)}) collective-permute-start(f32[1088,128]{1,0:T(8,128)S(1)} %get-tuple-element.17), channel_id=1, source_target_pairs={{0,4},{1,5},{2,6},{3,7},{4,0},{5,1},{6,2},{7,3},{8,12},{9,13},{10,... | collective-permute-start | bytes 1671176 | tf_op jit(solution)/shard_map/ppermute | solution.py:342
  31.9 8.1 %collective-permute-start = (f32[1088,128]{1,0:T(8,128)S(1)}, f32[1088,128]{1,0:T(8,128)S(1)}, u32[]{:S(2)}, u32[]{:S(2)}) collective-permute-start(f32[1088,128]{1,0:T(8,128)S(1)} %get-tuple-element.15), channel_id=1, source_target_pairs={{0,4},{1,5},{2,6},{3,7},{4,0},{5,1},{6,2},{7,3},{8,12},{9,13},{10,... | collective-permute-start | bytes 1671176 | tf_op jit(solution)/shard_map/ppermute | solution.py:342
  33.6 9.9 %collective-permute-start.20 = (f32[272,128]{1,0:T(8,128)S(1)}, f32[272,128]{1,0:T(8,128)S(1)}, u32[]{:S(2)}, u32[]{:S(2)}) collective-permute-start(f32[272,128]{1,0:T(8,128)S(1)} %get-tuple-element.28), channel_id=1, source_target_pairs={{0,2},{1,3},{2,0},{3,1},{4,6},{5,7},{6,4},{7,5},{8,10},{9,11},{10,... | collective-permute-start | bytes 417800 | tf_op jit(solution)/shard_map/ppermute | solution.py:342
  37.4 8.5 %collective-permute-start.21 = (f32[272,128]{1,0:T(8,128)S(1)}, f32[272,128]{1,0:T(8,128)S(1)}, u32[]{:S(2)}, u32[]{:S(2)}) collective-permute-start(f32[272,128]{1,0:T(8,128)S(1)} %get-tuple-element.27), channel_id=1, source_target_pairs={{0,1},{1,2},{2,3},{3,0},{4,5},{5,6},{6,7},{7,4},{8,9},{9,10},{10,1... | collective-permute-start | bytes 417800 | tf_op jit(solution)/shard_map/ppermute | solution.py:342
  38.1 7.7 %collective-permute-start.22 = (f32[272,128]{1,0:T(8,128)S(1)}, f32[272,128]{1,0:T(8,128)S(1)}, u32[]{:S(2)}, u32[]{:S(2)}) collective-permute-start(f32[272,128]{1,0:T(8,128)S(1)} %get-tuple-element.26), channel_id=1, source_target_pairs={{0,3},{1,0},{2,1},{3,2},{4,7},{5,4},{6,5},{7,6},{8,11},{9,8},{10,9... | collective-permute-start | bytes 417800 | tf_op jit(solution)/shard_map/ppermute | solution.py:342
  40.2 7.8 %collective-permute-start.1 = (f32[272,128]{1,0:T(8,128)S(1)}, f32[272,128]{1,0:T(8,128)S(1)}, u32[]{:S(2)}, u32[]{:S(2)}) collective-permute-start(f32[272,128]{1,0:T(8,128)S(1)} %get-tuple-element.31), channel_id=1, source_target_pairs={{0,64},{1,65},{2,66},{3,67},{4,68},{5,69},{6,70},{7,71},{8,72},{9,... | collective-permute-start | bytes 417800 | tf_op jit(solution)/shard_map/ppermute | solution.py:342
  43.2 7.1 %collective-permute-start.2 = (f32[272,128]{1,0:T(8,128)S(1)}, f32[272,128]{1,0:T(8,128)S(1)}, u32[]{:S(2)}, u32[]{:S(2)}) collective-permute-start(f32[272,128]{1,0:T(8,128)S(1)} %get-tuple-element.30), channel_id=1, source_target_pairs={{0,32},{1,33},{2,34},{3,35},{4,36},{5,37},{6,38},{7,39},{8,40},{9,... | collective-permute-start | bytes 417800 | tf_op jit(solution)/shard_map/ppermute | solution.py:342
  43.6 6.7 %collective-permute-start.3 = (f32[272,128]{1,0:T(8,128)S(1)}, f32[272,128]{1,0:T(8,128)S(1)}, u32[]{:S(2)}, u32[]{:S(2)}) collective-permute-start(f32[272,128]{1,0:T(8,128)S(1)} %get-tuple-element.29), channel_id=1, source_target_pairs={{0,96},{1,97},{2,98},{3,99},{4,100},{5,101},{6,102},{7,103},{8,104... | collective-permute-start | bytes 417800 | tf_op jit(solution)/shard_map/ppermute | solution.py:342
  45.9 7.6 %collective-permute-start.23 = (f32[68,128]{1,0:T(8,128)S(1)}, f32[68,128]{1,0:T(8,128)S(1)}, u32[]{:S(2)}, u32[]{:S(2)}) collective-permute-start(f32[68,128]{1,0:T(8,128)S(1)} %get-tuple-element.34), channel_id=1, source_target_pairs={{0,64},{1,65},{2,66},{3,67},{4,68},{5,69},{6,70},{7,71},{8,72},{9,... | collective-permute-start | bytes 104456 | tf_op jit(solution)/shard_map/ppermute | solution.py:342
  47.6 8.3 %collective-permute-start.24 = (f32[68,128]{1,0:T(8,128)S(1)}, f32[68,128]{1,0:T(8,128)S(1)}, u32[]{:S(2)}, u32[]{:S(2)}) collective-permute-start(f32[68,128]{1,0:T(8,128)S(1)} %get-tuple-element.33), channel_id=1, source_target_pairs={{0,32},{1,33},{2,34},{3,35},{4,36},{5,37},{6,38},{7,39},{8,40},{9,... | collective-permute-start | bytes 104456 | tf_op jit(solution)/shard_map/ppermute | solution.py:342
  48.0 7.9 %collective-permute-start.25 = (f32[68,128]{1,0:T(8,128)S(1)}, f32[68,128]{1,0:T(8,128)S(1)}, u32[]{:S(2)}, u32[]{:S(2)}) collective-permute-start(f32[68,128]{1,0:T(8,128)S(1)} %get-tuple-element.32), channel_id=1, source_target_pairs={{0,96},{1,97},{2,98},{3,99},{4,100},{5,101},{6,102},{7,103},{8,104... | collective-permute-start | bytes 104456 | tf_op jit(solution)/shard_map/ppermute | solution.py:342
  50.3 6.3 %collective-permute-start.4 = (f32[68,128]{1,0:T(8,128)S(1)}, f32[68,128]{1,0:T(8,128)S(1)}, u32[]{:S(2)}, u32[]{:S(2)}) collective-permute-start(f32[68,128]{1,0:T(8,128)S(1)} %get-tuple-element.37), channel_id=1, source_target_pairs={{0,16},{1,17},{2,18},{3,19},{4,20},{5,21},{6,22},{7,23},{8,24},{9,... | collective-permute-start | bytes 104456 | tf_op jit(solution)/shard_map/ppermute | solution.py:342
  53.2 5.6 %collective-permute-start.5 = (f32[68,128]{1,0:T(8,128)S(1)}, f32[68,128]{1,0:T(8,128)S(1)}, u32[]{:S(2)}, u32[]{:S(2)}) collective-permute-start(f32[68,128]{1,0:T(8,128)S(1)} %get-tuple-element.36), channel_id=1, source_target_pairs={{0,8},{1,9},{2,10},{3,11},{4,12},{5,13},{6,14},{7,15},{8,16},{9,17... | collective-permute-start | bytes 104456 | tf_op jit(solution)/shard_map/ppermute | solution.py:342
  53.5 5.3 %collective-permute-start.6 = (f32[68,128]{1,0:T(8,128)S(1)}, f32[68,128]{1,0:T(8,128)S(1)}, u32[]{:S(2)}, u32[]{:S(2)}) collective-permute-start(f32[68,128]{1,0:T(8,128)S(1)} %get-tuple-element.35), channel_id=1, source_target_pairs={{0,24},{1,25},{2,26},{3,27},{4,28},{5,29},{6,30},{7,31},{8,0},{9,1... | collective-permute-start | bytes 104456 | tf_op jit(solution)/shard_map/ppermute | solution.py:342
  55.9 6.1 %collective-permute-start.26 = (f32[17,128]{1,0:T(8,128)S(1)}, f32[17,128]{1,0:T(8,128)S(1)}, u32[]{:S(2)}, u32[]{:S(2)}) collective-permute-start(f32[17,128]{1,0:T(8,128)S(1)} %bitcast.68), channel_id=1, source_target_pairs={{0,16},{1,17},{2,18},{3,19},{4,20},{5,21},{6,22},{7,23},{8,24},{9,... | collective-permute-start | bytes 26120 | tf_op jit(solution)/shard_map/ppermute | solution.py:342
  56.0 7.7 %collective-permute-start.27 = (f32[17,128]{1,0:T(8,128)S(1)}, f32[17,128]{1,0:T(8,128)S(1)}, u32[]{:S(2)}, u32[]{:S(2)}) collective-permute-start(f32[17,128]{1,0:T(8,128)S(1)} %bitcast.67), channel_id=1, source_target_pairs={{0,8},{1,9},{2,10},{3,11},{4,12},{5,13},{6,14},{7,15},{8,16},{9,17... | collective-permute-start | bytes 26120 | tf_op jit(solution)/shard_map/ppermute | solution.py:342
  56.6 7.1 %collective-permute-start.28 = (f32[17,128]{1,0:T(8,128)S(1)}, f32[17,128]{1,0:T(8,128)S(1)}, u32[]{:S(2)}, u32[]{:S(2)}) collective-permute-start(f32[17,128]{1,0:T(8,128)S(1)} %bitcast.69), channel_id=1, source_target_pairs={{0,24},{1,25},{2,26},{3,27},{4,28},{5,29},{6,30},{7,31},{8,0},{9,1... | collective-permute-start | bytes 26120 | tf_op jit(solution)/shard_map/ppermute | solution.py:342
  58.9 5.5 %collective-permute-start.7 = (f32[17,128]{1,0:T(8,128)S(1)}, f32[17,128]{1,0:T(8,128)S(1)}, u32[]{:S(2)}, u32[]{:S(2)}) collective-permute-start(f32[17,128]{1,0:T(8,128)S(1)} %bitcast.70), channel_id=1, source_target_pairs={{0,2},{1,3},{2,0},{3,1},{4,6},{5,7},{6,4},{7,5},{8,10},{9,11},{10,... | collective-permute-start | bytes 26120 | tf_op jit(solution)/shard_map/ppermute | solution.py:342
  61.0 3.8 %collective-permute-start.8 = (f32[17,128]{1,0:T(8,128)S(1)}, f32[17,128]{1,0:T(8,128)S(1)}, u32[]{:S(2)}, u32[]{:S(2)}) collective-permute-start(f32[17,128]{1,0:T(8,128)S(1)} %bitcast.71), channel_id=1, source_target_pairs={{0,1},{1,2},{2,3},{3,0},{4,5},{5,6},{6,7},{7,4},{8,9},{9,10},{10,1... | collective-permute-start | bytes 26120 | tf_op jit(solution)/shard_map/ppermute | solution.py:342
  62.0 2.8 %collective-permute-start.9 = (f32[17,128]{1,0:T(8,128)S(1)}, f32[17,128]{1,0:T(8,128)S(1)}, u32[]{:S(2)}, u32[]{:S(2)}) collective-permute-start(f32[17,128]{1,0:T(8,128)S(1)} %bitcast.72), channel_id=1, source_target_pairs={{0,3},{1,0},{2,1},{3,2},{4,7},{5,4},{6,5},{7,6},{8,11},{9,8},{10,9... | collective-permute-start | bytes 26120 | tf_op jit(solution)/shard_map/ppermute | solution.py:342
  67.4 4.0 %collective-permute-start.38 = (f32[32,17]{1,0:T(8,128)}, f32[32,17]{1,0:T(8,128)S(1)}, u32[]{:S(2)}, u32[]{:S(2)}) collective-permute-start(f32[32,17]{1,0:T(8,128)} %get-tuple-element.19), channel_id=1, source_target_pairs={{0,1},{1,2},{2,3},{3,0},{4,5},{5,6},{6,7},{7,4},{8,9},{9,10},{10,1... | collective-permute-start | bytes 6536 | tf_op jit(solution)/shard_map/ppermute | solution.py:342
  67.4 5.4 %collective-permute-start.39 = (f32[32,17]{1,0:T(8,128)}, f32[32,17]{1,0:T(8,128)S(1)}, u32[]{:S(2)}, u32[]{:S(2)}) collective-permute-start(f32[32,17]{1,0:T(8,128)} %get-tuple-element.20), channel_id=1, source_target_pairs={{0,2},{1,3},{2,0},{3,1},{4,6},{5,7},{6,4},{7,5},{8,10},{9,11},{10,... | collective-permute-start | bytes 6536 | tf_op jit(solution)/shard_map/ppermute | solution.py:342
  71.2 2.8 %collective-permute-start.40 = (f32[32,17]{1,0:T(8,128)}, f32[32,17]{1,0:T(8,128)S(1)}, u32[]{:S(2)}, u32[]{:S(2)}) collective-permute-start(f32[32,17]{1,0:T(8,128)} %get-tuple-element.21), channel_id=1, source_target_pairs={{0,3},{1,0},{2,1},{3,2},{4,7},{5,4},{6,5},{7,6},{8,11},{9,8},{10,9... | collective-permute-start | bytes 6536 | tf_op jit(solution)/shard_map/ppermute | solution.py:342
  74.8 4.4 %collective-permute-start.41 = (f32[32,17]{1,0:T(8,128)S(1)}, f32[32,17]{1,0:T(8,128)S(1)}, u32[]{:S(2)}, u32[]{:S(2)}) collective-permute-start(f32[32,17]{1,0:T(8,128)S(1)} %add_add_fusion.2), channel_id=1, source_target_pairs={{0,32},{1,33},{2,34},{3,35},{4,36},{5,37},{6,38},{7,39},{8,40},{9,... | collective-permute-start | bytes 6536 | tf_op jit(solution)/shard_map/ppermute | solution.py:342
  74.8 5.2 %collective-permute-start.42 = (f32[32,17]{1,0:T(8,128)S(1)}, f32[32,17]{1,0:T(8,128)S(1)}, u32[]{:S(2)}, u32[]{:S(2)}) collective-permute-start(f32[32,17]{1,0:T(8,128)S(1)} %add_add_fusion.2), channel_id=1, source_target_pairs={{0,64},{1,65},{2,66},{3,67},{4,68},{5,69},{6,70},{7,71},{8,72},{9,... | collective-permute-start | bytes 6536 | tf_op jit(solution)/shard_map/ppermute | solution.py:342
  77.0 4.2 %collective-permute-start.43 = (f32[32,17]{1,0:T(8,128)S(1)}, f32[32,17]{1,0:T(8,128)S(1)}, u32[]{:S(2)}, u32[]{:S(2)}) collective-permute-start(f32[32,17]{1,0:T(8,128)S(1)} %add_add_fusion.2), channel_id=1, source_target_pairs={{0,96},{1,97},{2,98},{3,99},{4,100},{5,101},{6,102},{7,103},{8,104... | collective-permute-start | bytes 6536 | tf_op jit(solution)/shard_map/ppermute | solution.py:342
  77.5 4.1 %collective-permute-start.29 = (f32[17,128]{1,0:T(8,128)}, f32[17,128]{1,0:T(8,128)S(1)}, u32[]{:S(2)}, u32[]{:S(2)}) collective-permute-start(f32[17,128]{1,0:T(8,128)} %fusion.5.refs_2_), channel_id=1, source_target_pairs={{0,24},{1,25},{2,26},{3,27},{4,28},{5,29},{6,30},{7,31},{8,0},{9,1... | collective-permute-start | bytes 26120 | tf_op jit(solution)/shard_map/ppermute | solution.py:342
  78.8 4.3 %collective-permute-start.30 = (f32[17,128]{1,0:T(8,128)}, f32[17,128]{1,0:T(8,128)S(1)}, u32[]{:S(2)}, u32[]{:S(2)}) collective-permute-start(f32[17,128]{1,0:T(8,128)} %fusion.5.refs_2_), channel_id=1, source_target_pairs={{0,16},{1,17},{2,18},{3,19},{4,20},{5,21},{6,22},{7,23},{8,24},{9,... | collective-permute-start | bytes 26120 | tf_op jit(solution)/shard_map/ppermute | solution.py:342
  79.2 4.8 %collective-permute-start.31 = (f32[17,128]{1,0:T(8,128)}, f32[17,128]{1,0:T(8,128)S(1)}, u32[]{:S(2)}, u32[]{:S(2)}) collective-permute-start(f32[17,128]{1,0:T(8,128)} %fusion.5.refs_2_), channel_id=1, source_target_pairs={{0,8},{1,9},{2,10},{3,11},{4,12},{5,13},{6,14},{7,15},{8,16},{9,17... | collective-permute-start | bytes 26120 | tf_op jit(solution)/shard_map/ppermute | solution.py:342
  80.0 6.2 %collective-permute-start.10 = (f32[17,128]{1,0:T(8,128)}, f32[17,128]{1,0:T(8,128)S(1)}, u32[]{:S(2)}, u32[]{:S(2)}) collective-permute-start(f32[17,128]{1,0:T(8,128)} %fusion.7.refs_1_), channel_id=1, source_target_pairs={{0,3},{1,0},{2,1},{3,2},{4,7},{5,4},{6,5},{7,6},{8,11},{9,8},{10,9... | collective-permute-start | bytes 26120 | tf_op jit(solution)/shard_map/ppermute | solution.py:342
  81.2 6.2 %collective-permute-start.11 = (f32[17,128]{1,0:T(8,128)}, f32[17,128]{1,0:T(8,128)S(1)}, u32[]{:S(2)}, u32[]{:S(2)}) collective-permute-start(f32[17,128]{1,0:T(8,128)} %fusion.7.refs_1_), channel_id=1, source_target_pairs={{0,2},{1,3},{2,0},{3,1},{4,6},{5,7},{6,4},{7,5},{8,10},{9,11},{10,... | collective-permute-start | bytes 26120 | tf_op jit(solution)/shard_map/ppermute | solution.py:342
  81.6 7.4 %collective-permute-start.12 = (f32[17,128]{1,0:T(8,128)}, f32[17,128]{1,0:T(8,128)S(1)}, u32[]{:S(2)}, u32[]{:S(2)}) collective-permute-start(f32[17,128]{1,0:T(8,128)} %fusion.7.refs_1_), channel_id=1, source_target_pairs={{0,1},{1,2},{2,3},{3,0},{4,5},{5,6},{6,7},{7,4},{8,9},{9,10},{10,1... | collective-permute-start | bytes 26120 | tf_op jit(solution)/shard_map/ppermute | solution.py:342
  83.1 11.3 %collective-permute-start.44 = (f32[32,17]{1,0:T(8,128)S(1)}, f32[32,17]{1,0:T(8,128)S(1)}, u32[]{:S(2)}, u32[]{:S(2)}) collective-permute-start(f32[32,17]{1,0:T(8,128)S(1)} %add_add_fusion.1), channel_id=1, source_target_pairs={{0,8},{1,9},{2,10},{3,11},{4,12},{5,13},{6,14},{7,15},{8,16},{9,17... | collective-permute-start | bytes 6536 | tf_op jit(solution)/shard_map/ppermute | solution.py:342
  83.9 11.5 %collective-permute-start.45 = (f32[32,17]{1,0:T(8,128)S(1)}, f32[32,17]{1,0:T(8,128)S(1)}, u32[]{:S(2)}, u32[]{:S(2)}) collective-permute-start(f32[32,17]{1,0:T(8,128)S(1)} %add_add_fusion.1), channel_id=1, source_target_pairs={{0,16},{1,17},{2,18},{3,19},{4,20},{5,21},{6,22},{7,23},{8,24},{9,... | collective-permute-start | bytes 6536 | tf_op jit(solution)/shard_map/ppermute | solution.py:342
  86.2 4.1 %collective-permute-start.32 = (f32[68,128]{1,0:T(8,128)S(1)}, f32[68,128]{1,0:T(8,128)S(1)}, u32[]{:S(2)}, u32[]{:S(2)}) collective-permute-start(f32[68,128]{1,0:T(8,128)S(1)} %reshape.81), channel_id=1, source_target_pairs={{0,96},{1,97},{2,98},{3,99},{4,100},{5,101},{6,102},{7,103},{8,104... | collective-permute-start | bytes 104456 | tf_op jit(solution)/shard_map/ppermute | solution.py:342
  87.4 4.5 %collective-permute-start.33 = (f32[68,128]{1,0:T(8,128)S(1)}, f32[68,128]{1,0:T(8,128)S(1)}, u32[]{:S(2)}, u32[]{:S(2)}) collective-permute-start(f32[68,128]{1,0:T(8,128)S(1)} %reshape.81), channel_id=1, source_target_pairs={{0,64},{1,65},{2,66},{3,67},{4,68},{5,69},{6,70},{7,71},{8,72},{9,... | collective-permute-start | bytes 104456 | tf_op jit(solution)/shard_map/ppermute | solution.py:342
  89.0 4.0 %collective-permute-start.34 = (f32[68,128]{1,0:T(8,128)S(1)}, f32[68,128]{1,0:T(8,128)S(1)}, u32[]{:S(2)}, u32[]{:S(2)}) collective-permute-start(f32[68,128]{1,0:T(8,128)S(1)} %reshape.81), channel_id=1, source_target_pairs={{0,32},{1,33},{2,34},{3,35},{4,36},{5,37},{6,38},{7,39},{8,40},{9,... | collective-permute-start | bytes 104456 | tf_op jit(solution)/shard_map/ppermute | solution.py:342
  90.3 7.1 %collective-permute-start.46 = (f32[32,17]{1,0:T(8,128)S(1)}, f32[32,17]{1,0:T(8,128)S(1)}, u32[]{:S(2)}, u32[]{:S(2)}) collective-permute-start(f32[32,17]{1,0:T(8,128)S(1)} %add_add_fusion.1), channel_id=1, source_target_pairs={{0,24},{1,25},{2,26},{3,27},{4,28},{5,29},{6,30},{7,31},{8,0},{9,1... | collective-permute-start | bytes 6536 | tf_op jit(solution)/shard_map/ppermute | solution.py:342
  91.9 17.7 %collective-permute-start.13 = (f32[68,128]{1,0:T(8,128)S(1)}, f32[68,128]{1,0:T(8,128)S(1)}, u32[]{:S(2)}, u32[]{:S(2)}) collective-permute-start(f32[68,128]{1,0:T(8,128)S(1)} %reshape.79), channel_id=1, source_target_pairs={{0,24},{1,25},{2,26},{3,27},{4,28},{5,29},{6,30},{7,31},{8,0},{9,1... | collective-permute-start | bytes 104456 | tf_op jit(solution)/shard_map/ppermute | solution.py:342
  93.0 18.1 %collective-permute-start.14 = (f32[68,128]{1,0:T(8,128)S(1)}, f32[68,128]{1,0:T(8,128)S(1)}, u32[]{:S(2)}, u32[]{:S(2)}) collective-permute-start(f32[68,128]{1,0:T(8,128)S(1)} %reshape.79), channel_id=1, source_target_pairs={{0,16},{1,17},{2,18},{3,19},{4,20},{5,21},{6,22},{7,23},{8,24},{9,... | collective-permute-start | bytes 104456 | tf_op jit(solution)/shard_map/ppermute | solution.py:342
  94.4 17.2 %collective-permute-start.15 = (f32[68,128]{1,0:T(8,128)S(1)}, f32[68,128]{1,0:T(8,128)S(1)}, u32[]{:S(2)}, u32[]{:S(2)}) collective-permute-start(f32[68,128]{1,0:T(8,128)S(1)} %reshape.79), channel_id=1, source_target_pairs={{0,8},{1,9},{2,10},{3,11},{4,12},{5,13},{6,14},{7,15},{8,16},{9,17... | collective-permute-start | bytes 104456 | tf_op jit(solution)/shard_map/ppermute | solution.py:342
  95.4 17.0 %collective-permute-start.35 = (f32[272,128]{1,0:T(8,128)S(1)}, f32[272,128]{1,0:T(8,128)S(1)}, u32[]{:S(2)}, u32[]{:S(2)}) collective-permute-start(f32[272,128]{1,0:T(8,128)S(1)} %pad_maximum_fusion.1.refs_4_), channel_id=1, source_target_pairs={{0,3},{1,0},{2,1},{3,2},{4,7},{5,4},{6,5},{7,6},{8,11},{9,8},{10,9... | collective-permute-start | bytes 417800 | tf_op jit(solution)/shard_map/ppermute | solution.py:342
  97.4 14.4 %collective-permute-start.47 = (f32[32,17]{1,0:T(8,128)S(1)}, f32[32,17]{1,0:T(8,128)S(1)}, u32[]{:S(2)}, u32[]{:S(2)}) collective-permute-start(f32[32,17]{1,0:T(8,128)S(1)} %add_add_fusion), channel_id=1, source_target_pairs={{0,4},{1,5},{2,6},{3,7},{4,0},{5,1},{6,2},{7,3},{8,12},{9,13},{10,... | collective-permute-start | bytes 6536 | tf_op jit(solution)/shard_map/ppermute | solution.py:342
  109.6 7.3 %collective-permute-start.36 = (f32[272,128]{1,0:T(8,128)S(1)}, f32[272,128]{1,0:T(8,128)S(1)}, u32[]{:S(2)}, u32[]{:S(2)}) collective-permute-start(f32[272,128]{1,0:T(8,128)S(1)} %pad_maximum_fusion.1.refs_4_), channel_id=1, source_target_pairs={{0,2},{1,3},{2,0},{3,1},{4,6},{5,7},{6,4},{7,5},{8,10},{9,11},{10,... | collective-permute-start | bytes 417800 | tf_op jit(solution)/shard_map/ppermute | solution.py:342
  111.1 8.6 %collective-permute-start.37 = (f32[272,128]{1,0:T(8,128)S(1)}, f32[272,128]{1,0:T(8,128)S(1)}, u32[]{:S(2)}, u32[]{:S(2)}) collective-permute-start(f32[272,128]{1,0:T(8,128)S(1)} %pad_maximum_fusion.1.refs_4_), channel_id=1, source_target_pairs={{0,1},{1,2},{2,3},{3,0},{4,5},{5,6},{6,7},{7,4},{8,9},{9,10},{10,1... | collective-permute-start | bytes 417800 | tf_op jit(solution)/shard_map/ppermute | solution.py:342
  111.6 8.1 %collective-permute-start.16 = (f32[272,128]{1,0:T(8,128)S(1)}, f32[272,128]{1,0:T(8,128)S(1)}, u32[]{:S(2)}, u32[]{:S(2)}) collective-permute-start(f32[272,128]{1,0:T(8,128)S(1)} %pad_maximum_fusion.refs_0_), channel_id=1, source_target_pairs={{0,96},{1,97},{2,98},{3,99},{4,100},{5,101},{6,102},{7,103},{8,104... | collective-permute-start | bytes 417800 | tf_op jit(solution)/shard_map/ppermute | solution.py:342
  111.8 7.9 %collective-permute-start.17 = (f32[272,128]{1,0:T(8,128)S(1)}, f32[272,128]{1,0:T(8,128)S(1)}, u32[]{:S(2)}, u32[]{:S(2)}) collective-permute-start(f32[272,128]{1,0:T(8,128)S(1)} %pad_maximum_fusion.refs_0_), channel_id=1, source_target_pairs={{0,64},{1,65},{2,66},{3,67},{4,68},{5,69},{6,70},{7,71},{8,72},{9,... | collective-permute-start | bytes 417800 | tf_op jit(solution)/shard_map/ppermute | solution.py:342
  112.4 8.7 %collective-permute-start.18 = (f32[272,128]{1,0:T(8,128)S(1)}, f32[272,128]{1,0:T(8,128)S(1)}, u32[]{:S(2)}, u32[]{:S(2)}) collective-permute-start(f32[272,128]{1,0:T(8,128)S(1)} %pad_maximum_fusion.refs_0_), channel_id=1, source_target_pairs={{0,32},{1,33},{2,34},{3,35},{4,36},{5,37},{6,38},{7,39},{8,40},{9,... | collective-permute-start | bytes 417800 | tf_op jit(solution)/shard_map/ppermute | solution.py:342
  (13 other events, 57.8 us)

commit v2 on v0

v2 whole, which is shorter than its diff:
```python
import math

import jax
import jax.numpy as jnp
from jax import lax
from jax.experimental import pallas as pl
from jax.experimental.pallas import tpu as pltpu
from jax.sharding import PartitionSpec as P

GROUPS = 8
AXES = ("wide", "quad")
LANES = 128
COLS = 17
SIDE = 256
PEEL = 20
STEP = 4


def number(y, x, c, z):
    return ((y * 4 + x) * 2 + c) * 4 + z


def shift(axis, off):
    pairs = []
    for y in range(4):
        for x in range(4):
            for c in range(2):
                for z in range(4):
                    at = {"y": y, "x": x, "c": c, "z": z}
                    size = 2 if axis == "c" else 4
                    to = dict(at)
                    to[axis] = (at[axis] + off) % size
                    pairs.append((number(**at), number(**to)))
    return pairs


def fold(v):
    v = v ^ (v >> 8)
    v = v ^ (v >> 4)
    v = v ^ (v >> 2)
    v = v ^ (v >> 1)
    return v & 1


def lane_take(tile, index):
    return jnp.take_along_axis(tile, index, axis=1)


def bitonic(v, sub, lane):
    for k in range(1, 13):
        for b in (k - 1, k):
            if b == 0 or b == 12:
                continue
            if b < 4:
                v = [~t if (i >> b) & 1 else t for i, t in enumerate(v)]
            else:
                bit = (sub >> (b - 4)) if b < 7 else (lane >> (b - 7))
                m = -(bit & 1)
                v = [t ^ m for t in v]
        for j in range(k - 1, -1, -1):
            if j < 4:
                new = list(v)
                for i in range(16):
                    if not (i >> j) & 1:
                        a, b = v[i], v[i | (1 << j)]
                        new[i] = jnp.minimum(a, b)
                        new[i | (1 << j)] = jnp.maximum(a, b)
                v = new
            elif j < 7:
                d = 1 << (j - 4)
                up = (sub & d) != 0
                new = []
                for t in v:
                    prev = pltpu.roll(t, d, 0)
                    nxt = prev if d == 4 else pltpu.roll(t, 8 - d, 0)
                    new.append(jnp.where(up, jnp.maximum(t, prev), jnp.minimum(t, nxt)))
                v = new
            else:
                d = 1 << (j - 7)
                up = (lane & d) != 0
                other = lane ^ d
                new = []
                for t in v:
                    o = lane_take(t, other)
                    new.append(jnp.where(up, jnp.maximum(t, o), jnp.minimum(t, o)))
                v = new
    return v


def sort_kernel(pos_ref, samples_ref, keys_ref, ends_ref, rank_ref, scratch):
    me, core = pos_ref[0], pos_ref[1]
    sub = lax.broadcasted_iota(jnp.int32, (8, LANES), 0)
    lane = lax.broadcasted_iota(jnp.int32, (8, LANES), 1)
    both = []
    for c in range(2):
        v = []
        for i in range(16):
            s = samples_ref[i, c]
            p = s & 65535
            place = (((p >> 7) & 1) << 15) | ((p >> 8) << 7) | (p & 127)
            odd = fold((s >> 16) & me)
            r = i * 256 + sub * 32 + (lane & 31)
            v.append((place << 13) | (r << 1) | odd)
        v = bitonic(v, sub, lane)
        both.append(v)
        for i in range(16):
            scratch[pl.ds(i, 8, stride=16), :] = v[i]
        ends_ref[2 * c : 2 * c + 1, :] = scratch[0:1, :] >> 20
        ends_ref[2 * c + 1 : 2 * c + 2, :] = scratch[127:128, :] >> 20
        keys_ref[c * LANES : (c + 1) * LANES, :] = scratch[...].T
    v = []
    for i in range(16):
        key = jnp.where(core == 0, both[0][i], both[1][i])
        slot = (lane & 31) * LANES + sub * 16 + i
        v.append((((key >> 1) & 4095) << 12) | slot)
    v = bitonic(v, sub, lane)
    for i in range(16):
        scratch[pl.ds(i, 8, stride=16), :] = v[i] & 4095
    rank_ref[...] = scratch[...].T


VMEM = pl.BlockSpec(memory_space=pltpu.VMEM)
SMEM = pl.BlockSpec(memory_space=pltpu.SMEM)


def sort_call(pos, samples):
    return pl.pallas_call(
        sort_kernel,
        out_shape=(
            jax.ShapeDtypeStruct((256, LANES), jnp.int32),
            jax.ShapeDtypeStruct((4, LANES), jnp.int32),
            jax.ShapeDtypeStruct((LANES, LANES), jnp.int32),
        ),
        in_specs=[SMEM, VMEM],
        out_specs=(VMEM,) * 3,
        scratch_shapes=[pltpu.VMEM((LANES, LANES), jnp.int32)],
        compiler_params=pltpu.CompilerParams(vmem_limit_bytes=8 * 2**20),
        cost_estimate=pl.CostEstimate(flops=20_000_000, bytes_accessed=20_000_000, transcendentals=0),
        name="sort_slots",
    )(pos, samples)


def split(x):
    hi = x.astype(jnp.bfloat16)
    lo = (x - hi.astype(jnp.float32)).astype(jnp.bfloat16)
    return hi, lo


def dot(a, b):
    return lax.dot_general(a, b, (((1,), (0,)), ((), ())), preferred_element_type=jnp.float32)


def mix_kernel(basis_ref, target_ref, bits_ref, tab, last):
    a = lax.broadcasted_iota(jnp.int32, (SIDE, SIDE), 0)
    b = lax.broadcasted_iota(jnp.int32, (SIDE, SIDE), 1)
    walsh = (1 - 2 * fold(a & b)).astype(jnp.float32).astype(jnp.bfloat16)
    flips = [(1 - 2 * bits_ref[pl.ds(bh, SIDE, stride=2), :]).astype(jnp.float32) for bh in range(2)]
    flip = jnp.concatenate(flips, axis=1)
    for k in range(COLS):
        if k < 16:
            base = (k // 8) * 4096 + k % 8
            halves = [basis_ref[pl.ds(base + 8 * bh, SIDE, stride=16), :] for bh in range(2)]
        else:
            halves = [target_ref[pl.ds(bh, SIDE, stride=2), :] for bh in range(2)]
        x = jnp.concatenate(halves, axis=1) * flip
        hi, lo = split(x)
        y = dot(hi, walsh) + dot(lo, walsh)
        hi, lo = split(y)
        z = dot(walsh, hi) + dot(walsh, lo)
        for bh in range(2):
            half = z[:, bh * LANES : (bh + 1) * LANES]
            if k < 16:
                tab[pl.ds(bh * SIDE * 16 + k, SIDE, stride=16), :] = half
            else:
                last[bh * SIDE : (bh + 1) * SIDE, :] = half


def mix_call(basis, target, bits):
    return pl.pallas_call(
        mix_kernel,
        out_shape=(
            jax.ShapeDtypeStruct((512 * 16, LANES), jnp.float32),
            jax.ShapeDtypeStruct((512, LANES), jnp.float32),
        ),
        in_specs=[VMEM] * 3,
        out_specs=(VMEM,) * 2,
        compiler_params=pltpu.CompilerParams(vmem_limit_bytes=16 * 2**20),
        cost_estimate=pl.CostEstimate(flops=2 * 2**31, bytes_accessed=20_000_000, transcendentals=0),
        name="local_walsh",
    )(basis, target, bits)


def slots_kernel(scale, off, pos_ref, ends_ref, tab, last, keys_ref, keep, give):
    core = pos_ref[1]
    z = (pos_ref[4] + off) & 3
    sub = lax.broadcasted_iota(jnp.int32, (8, LANES), 0)
    for rel_core, out in enumerate((keep, give)):
        c = core ^ rel_core

        def group(it, _, c=c, out=out):
            lows, tiles, lanes_of, rows_of, subrows, weights = [], [], [], [], [], []
            most, many = jnp.int32(0), jnp.int32(0)
            for q in range(4):
                j = z * 32 + it * 4 + q
                key = jnp.broadcast_to(keys_ref[pl.ds(c * LANES + j, 1), :], (8, LANES))
                low, high = ends_ref[2 * c, j], ends_ref[2 * c + 1, j]
                lows.append(low)
                tiles.append(low >> 3)
                most = jnp.maximum(most, high - low + 1)
                many = jnp.maximum(many, (high >> 3) - (low >> 3) + 1)
                lanes_of.append((key >> 13) & 127)
                rows_of.append((key >> 20) - low)
                subrows.append((key >> 20) - (low >> 3) * 8 - sub)
                weights.append(jnp.where((key & 1) != 0, -scale, scale))

            def add_rows(first, count, acc):
                acc = list(acc)
                for u in range(count):
                    for q in range(4):
                        row = jnp.minimum(lows[q] + first + u, 511)
                        hit = rows_of[q] == first + u
                        for t in range(2):
                            tile = tab[pl.ds(pl.multiple_of(row * 16 + 8 * t, 8), 8), :]
                            acc[q * 2 + t] = jnp.where(hit, lane_take(tile, lanes_of[q]), acc[q * 2 + t])
                return tuple(acc)

            def add_last(first, count, acc):
                acc = list(acc)
                for u in range(count):
                    for q in range(4):
                        row = jnp.minimum(tiles[q] + first + u, 63)
                        tile = last[pl.ds(pl.multiple_of(row * 8, 8), 8), :]
                        hit = subrows[q] == (first + u) * 8
                        acc[q] = jnp.where(hit, lane_take(tile, lanes_of[q]), acc[q])
                return tuple(acc)

            zero = jnp.zeros((8, LANES), jnp.float32)
            acc = add_rows(0, PEEL, (zero,) * 8)
            more = (jnp.maximum(most - PEEL, 0) + STEP - 1) // STEP
            acc = lax.fori_loop(0, more, lambda n, a: add_rows(PEEL + n * STEP, STEP, a), acc)
            tail = add_last(0, 4, (zero,) * 4)
            tail = lax.fori_loop(4, jnp.maximum(many, 4), lambda n, a: add_last(n, 1, a), tail)
            base = it * (4 * COLS)
            for q in range(4):
                for t in range(2):
                    out[pl.ds(base + q + 32 * t, 8, stride=4), :] = acc[q * 2 + t] * weights[q]
                line = jnp.sum(tail[q], axis=0, keepdims=True)
                out[pl.ds(base + q + 64, 1), :] = line * weights[q][0:1]
            return 0

        lax.fori_loop(0, 8, group, 0)


def slots_call(scale, off, pos, ends, tab, last, keys):
    part = jax.ShapeDtypeStruct((8 * 4 * COLS, LANES), jnp.float32)
    return pl.pallas_call(
        lambda *refs: slots_kernel(scale, off, *refs),
        out_shape=(part,) * 2,
        in_specs=[SMEM, SMEM, VMEM, VMEM, VMEM],
        out_specs=(VMEM,) * 2,
        compiler_params=pltpu.CompilerParams(vmem_limit_bytes=12 * 2**20),
        cost_estimate=pl.CostEstimate(flops=20_000_000, bytes_accessed=22_000_000, transcendentals=0),
        name=f"take_slots_{off}",
    )(pos, ends, tab, last, keys)


def order_kernel(pos_ref, rank_ref, *refs):
    parts, outs, table = refs[:4], refs[4:8], refs[8]
    y, z = pos_ref[2], pos_ref[4]
    table[...] = (parts[0][...] + parts[1][...]) + (parts[2][...] + parts[3][...])
    rows = 8 * COLS
    at = lax.broadcasted_iota(jnp.int32, (rows, LANES), 0)
    code = (at // (4 * COLS)) * 4 + (at & 3)
    ck = lax.broadcasted_iota(jnp.int32, (24, rows), 0)
    cr = lax.broadcasted_iota(jnp.int32, (24, rows), 1)
    collect = jnp.where((cr % (4 * COLS)) // 4 == ck, 1.0, 0.0).astype(jnp.bfloat16)

    def step(i, _):
        for rel, out in enumerate(outs):
            line = z * 32 + ((y + rel) & 3) * 8 + i
            slot = jnp.broadcast_to(rank_ref[pl.ds(line, 1), :], (8, LANES))
            index = slot & 127
            pair = slot >> 10
            acc = [jnp.zeros((8, LANES), jnp.float32)] * COLS
            for n in range(4):
                hit = pair == n
                for t in range(COLS):
                    tile = table[n * rows + 8 * t : n * rows + 8 * t + 8, :]
                    acc[t] = jnp.where(hit, lane_take(tile, index), acc[t])
            chosen = jnp.where(code == ((slot >> 7) & 7)[0:1], jnp.concatenate(acc, axis=0), 0.0)
            hi, lo = split(chosen)
            values = dot(collect, hi) + dot(collect, lo)
            for t in range(2):
                out[pl.ds(i + 64 * t, 8, stride=8), :] = values[8 * t : 8 * t + 8]
            out[pl.ds(i + 128, 1), :] = values[16:17]
        return 0

    lax.fori_loop(0, 8, step, 0)


def order_call(pos, rank, parts):
    rows = 8 * COLS
    return pl.pallas_call(
        order_kernel,
        out_shape=(jax.ShapeDtypeStruct((rows, LANES), jnp.float32),) * 4,
        in_specs=[SMEM] + [VMEM] * 5,
        out_specs=(VMEM,) * 4,
        scratch_shapes=[pltpu.VMEM((4 * rows, LANES), jnp.float32)],
        compiler_params=pltpu.CompilerParams(vmem_limit_bytes=8 * 2**20),
        cost_estimate=pl.CostEstimate(flops=20_000_000, bytes_accessed=18_000_000, transcendentals=0),
        name="given_order",
    )(pos, rank, *parts)


def finish_kernel(factor, pos_ref, owners_ref, p0, p1, p2, p3, sketch, gram, table):
    core, y, x, z = pos_ref[1], pos_ref[2], pos_ref[3], pos_ref[4]
    table[0 : 8 * COLS, :] = (p0[...] + p1[...]) + (p2[...] + p3[...])
    table[8 * COLS :, :] = jnp.zeros((24 * 8 - 8 * COLS, LANES), jnp.float32)
    for h in range(2):
        sketch[:, h * LANES : (h + 1) * LANES] = table[pl.ds(2 * x + h, 24, stride=8), :][:COLS]
    pieces, lefts = [], []
    for tx in range(4):
        for h in range(2):
            v = table[pl.ds(2 * tx + h, 24, stride=8), :]
            owner = owners_ref[y * 4 + tx, core, pl.ds(2 * z + h, 1), :]
            lefts.append(jnp.concatenate([jnp.where(owner == g, v[:16], 0.0) for g in range(GROUPS)], axis=0))
            pieces.append(v)
    value = jnp.concatenate(pieces, axis=1)
    left = jnp.concatenate(lefts, axis=1)
    total = lax.dot_general(
        value, left, (((1,), (1,)), ((), ())),
        precision=lax.Precision.HIGHEST, preferred_element_type=jnp.float32,
    )
    gram[...] = factor * total[:COLS]


def finish_call(factor, pos, owners, parts):
    return pl.pallas_call(
        lambda *refs: finish_kernel(factor, *refs),
        out_shape=(
            jax.ShapeDtypeStruct((COLS, SIDE), jnp.float32),
            jax.ShapeDtypeStruct((COLS, LANES), jnp.float32),
        ),
        in_specs=[SMEM] + [VMEM] * 5,
        out_specs=(VMEM,) * 2,
        scratch_shapes=[pltpu.VMEM((24 * 8, LANES), jnp.float32)],
        compiler_params=pltpu.CompilerParams(vmem_limit_bytes=8 * 2**20),
        name="rows_and_gram",
    )(pos, owners, *parts)


def send(v, axis, off):
    return lax.ppermute(v, AXES, shift(axis, off))


def shards(basis, target, sign_bits, samples, owners):
    rows = basis.shape[1]
    total_samples = samples.shape[0]
    scale = 1.0 / math.sqrt(rows * 128)
    wide = lax.axis_index("wide")
    z = lax.axis_index("quad")
    core, x, y = wide & 1, (wide >> 1) & 3, wide >> 3
    pos = jnp.stack([wide * 4 + z, core, y, x, z, z, z, z]).astype(jnp.int32)

    lined = samples.reshape(16, 2, 4, 8, 32).transpose(0, 1, 3, 2, 4).reshape(16, 2, 8, LANES)
    keys, ends, rank = sort_call(pos, lined)
    tiles = basis.reshape(2, 8, 512, LANES).transpose(0, 2, 1, 3).reshape(8192, LANES)
    tab, last = mix_call(tiles, target.reshape(512, LANES), sign_bits.reshape(512, LANES))
    parts, held = [], []
    for n, off in enumerate((2, 1, 3, 0)):
        if n >= 2:
            keys, held[n - 2] = lax.optimization_barrier((keys, held[n - 2]))
        keep, give = slots_call(scale, off, pos, ends, tab, last, keys)
        held.append(keep + send(give, "c", 1))
        if n >= 2:
            parts.append(send(held[n - 2], "z", (2, 1)[n - 2]))
    parts += [send(held[2], "z", 3), held[3]]
    lines = order_call(pos, rank, parts)
    line = (lines[0] + send(lines[2], "y", 2)) + (send(lines[1], "y", 1) + send(lines[3], "y", 3))
    around = [line] + [send(line, "x", off) for off in (2, 1, 3)]
    sketch, gram = finish_call(GROUPS / total_samples, pos, owners.reshape(16, 2, 8, LANES), around)
    for axis in ("z", "y"):
        gram = (gram + send(gram, axis, 2)) + (send(gram, axis, 1) + send(gram, axis, 3))
    gram = gram + send(gram, "c", 1)
    own = lax.dynamic_slice_in_dim(gram, z * 32, 32, 1)
    return sketch.T, own.T.reshape(2, 16, COLS)


def solution(mesh):
    placed = (P(None, AXES), P(AXES), P(AXES), P(), P())
    return jax.shard_map(
        shards,
        mesh=mesh,
        in_specs=placed,
        out_specs=(P(AXES, None), P("quad", None, None)),
        check_vma=False,
    )
```

time: 1100 us -> 117 us (0.11)
  waiting for transfers between devices: 662 us -> 19.9 us
  local copies, waits for them, and re-layouts: 329 us -> 6.35 us
  blocking collectives: 70.5 us -> 0 us
  Pallas kernels: 0 us -> 57 us
  starting transfers between devices: 0.04 us -> 32.2 us
  other arithmetic: 14 us -> 0.22 us
  matrix products: 13.6 us -> 0 us
  between operations: 14.1 us -> 0.76 us
    reduce_scatter x1 -> x0, waiting for transfers between devices: 662 us -> none  [shards(): lax.psum_scatter(term, ('wide', 'quad'), scatter_dimension=1, tiled=True)]
    gather x2 -> x0, local copies, waits for them, and re-layouts: 300 us -> none  [the longest x1 181 us: shards(): number = samples[slots]]
    psum x1 -> x0, blocking collectives: 70.5 us -> none  [shards(): summed = lax.psum(partial_gram, ('wide', 'quad'))]
    pallas_call x0 -> x8, Pallas kernels: none -> 57 us  [the longest x4 41.4 us: slots_call(): pl.pallas_call(lambda *refs: slots_kernel(scale, off, *refs), out_shape=(...]
    ppermute x0 -> x20, starting transfers between devices: none -> 32.2 us  [send(): return lax.ppermute(v, AXES, shift(axis, off))]
    ppermute x0 -> x20, waiting for transfers between devices: none -> 19.9 us  [send(): return lax.ppermute(v, AXES, shift(axis, off))]
    reshape x1 -> x2, local copies, waits for them, and re-layouts: 18.3 us -> 1.32 us  [shards(): samples.reshape(16, 2, 4, 8, 32).transpose(0, 1, 3, 2, 4)]
    dot_general x3 -> x0, matrix products: 13.6 us -> none  [the longest x1 6.72 us: shards(): jnp.einsum('kab,ac->kcb', cube, table, precision=lax.Precision.HIGHEST)]
  transfers between devices with their start and end apart: 1 -> 20, of which waited for: 1 -> 7; matrix products, arithmetic and copies ran while one was open for 0% -> 0% of each run, Pallas kernels for 0% -> 27%
where the time goes in v2:
time: 117 us; the launch traced here: 116 us
  Pallas kernels  57 us (49%)
  starting transfers between devices  32.2 us (28%)
  waiting for transfers between devices  19.9 us (17%)
  local copies, waits for them, and re-layouts  6.35 us (5%)
    pallas_call x4, Pallas kernels, slots_call(): pl.pallas_call(lambda *refs: slots_kernel(scale, off, *refs), out_shape=(...  41.4 us
    ppermute x20, starting transfers between devices, send(): return lax.ppermute(v, AXES, shift(axis, off))  32.2 us
    ppermute x20, waiting for transfers between devices, send(): return lax.ppermute(v, AXES, shift(axis, off))  19.9 us
    pallas_call x1, Pallas kernels, order_call(): pl.pallas_call(order_kernel, out_shape=(jax.ShapeDtypeStruct((rows, LANES...  5.32 us
    unnamed x9, local copies, waits for them, and re-layouts  4.78 us
    pallas_call x1, Pallas kernels, mix_call(): pl.pallas_call(mix_kernel, out_shape=(jax.ShapeDtypeStruct((512 * 16, LAN...  4.39 us
    pallas_call x1, Pallas kernels, sort_call(): pl.pallas_call(sort_kernel, out_shape=(jax.ShapeDtypeStruct((256, LANES),...  4.22 us
  transfers between devices with their start and end apart: 20, of which 7 were waited for; matrix products, arithmetic and copies ran while one was open for 0% of the time, Pallas kernels for 27%

profile of v2, /device:TPU:1, one launch (start us, length us, event | category | flops | bytes accessed | tf_op | source)
XLA Modules:
  0.0 116.4 jit_solution(2769845363867708245)
XLA Ops:
  0.6 1.1 reshape.29
  1.7 0.2 copy.8
  1.9 0.3 reshape.30.samples_ref
  2.1 0.1 stack.26.pos_ref.refs_0_
  2.2 4.2 %sort_slots.1 = (s32[256,128]{1,0:T(8,128)S(1)}, s32[4,128]{1,0:T(4,128)S(1)}, s32[128,128]{1,0:T(8,128)S(1)}) custom-call(s32[8]{0:T(128)S(1)} %stack.26.pos_ref.refs_0_, s32[16,2,8,128]{3,2,1,0:T(8,128)S(1)} %reshape.30.samples_ref), custom_call_target="tpu_custom_call" | custom-call | flops 20000000 | bytes 20000000 | tf_op jit(solution)/shard_map/sort_slots/pallas_call | solution.py:127
  6.4 0.0 copy-start.1
  6.5 2.2 %copy-done.1 = f32[16,65536]{1,0:T(8,128)S(1)} copy-done((f32[16,65536]{1,0:T(8,128)S(1)}, f32[16,65536]{1,0:T(8,128)}, u32[]{:S(2)}) %copy-start.1) | copy-done | bytes 4194328
  8.6 0.9 copy-done.2
  9.6 0.9 copy-done.3
  10.5 4.4 %local_walsh.1 = (f32[8192,128]{1,0:T(8,128)S(1)}, f32[512,128]{1,0:T(8,128)S(1)}) custom-call(f32[8192,128]{1,0:T(8,128)S(1)} %bitcast.19, f32[512,128]{1,0:T(8,128)S(1)} %bitcast.20, s32[512,128]{1,0:T(8,128)S(1)} %bitcast.21), custom_call_target="tpu_custom_call" | custom-call | flops 4294967296 | bytes 20000000 | tf_op jit(solution)/shard_map/local_walsh/pallas_call | solution.py:179
  14.9 10.3 %take_slots_2.1 = (f32[544,128]{1,0:T(8,128)S(1)}, f32[544,128]{1,0:T(8,128)S(1)}) custom-call(s32[8]{0:T(128)S(1)} %stack.26.pos_ref.refs_0_, s32[4,128]{1,0:T(4,128)S(1)} %get-tuple-element.27.refs_1_, f32[8192,128]{1,0:T(8,128)S(1)} %get-tuple-element.28.refs_2_, f32[512,128]{1,0:T(8,128)S(1)} %get-tuple-element.29.refs_3_, ...), custom_call_target="tpu_custom_call" | custom-call | flops 20000000 | bytes 22000000 | tf_op jit(solution)/shard_map/take_slots_2/pallas_call | solution.py:256
  25.2 1.5 %collective-permute-start = (f32[544,128]{1,0:T(8,128)S(1)}, f32[544,128]{1,0:T(8,128)S(1)}, u32[]{:S(2)}, u32[]{:S(2)}) collective-permute-start(f32[544,128]{1,0:T(8,128)S(1)} %get-tuple-element.31), channel_id=1, source_target_pairs={{0,4},{1,5},{2,6},{3,7},{4,0},{5,1},{6,2},{7,3},{8,12},{9,13},{10,... | collective-permute-start | bytes 835592 | tf_op jit(solution)/shard_map/ppermute | solution.py:353
  26.7 10.4 %take_slots_1.1 = (f32[544,128]{1,0:T(8,128)S(1)}, f32[544,128]{1,0:T(8,128)S(1)}) custom-call(s32[8]{0:T(128)S(1)} %stack.26.pos_ref.refs_0_, s32[4,128]{1,0:T(4,128)S(1)} %get-tuple-element.27.refs_1_, f32[8192,128]{1,0:T(8,128)S(1)} %get-tuple-element.28.refs_2_, f32[512,128]{1,0:T(8,128)S(1)} %get-tuple-element.29.refs_3_, ...), custom_call_target="tpu_custom_call" | custom-call | flops 20000000 | bytes 22000000 | tf_op jit(solution)/shard_map/take_slots_1/pallas_call | solution.py:256
  37.1 0.1 collective-permute-start.2
  37.2 0.0 collective-permute-done
  37.2 10.5 %take_slots_3.1 = (f32[544,128]{1,0:T(8,128)S(1)}, f32[544,128]{1,0:T(8,128)S(1)}) custom-call(s32[8]{0:T(128)S(1)} %stack.26.pos_ref.refs_0_, s32[4,128]{1,0:T(4,128)S(1)} %get-tuple-element.27.refs_1_, f32[8192,128]{1,0:T(8,128)S(1)} %get-tuple-element.28.refs_2_, f32[512,128]{1,0:T(8,128)S(1)} %get-tuple-element.29.refs_3_, ...), custom_call_target="tpu_custom_call" | custom-call | flops 20000000 | bytes 22000000 | tf_op jit(solution)/shard_map/take_slots_3/pallas_call | solution.py:256
  47.8 0.6 collective-permute-start.4
  48.3 3.7 %collective-permute-start.1 = (f32[544,128]{1,0:T(8,128)S(1)}, f32[544,128]{1,0:T(8,128)S(1)}, u32[]{:S(2)}, u32[]{:S(2)}) collective-permute-start(f32[544,128]{1,0:T(8,128)S(1)} %add.49), channel_id=1, source_target_pairs={{0,2},{1,3},{2,0},{3,1},{4,6},{5,7},{6,4},{7,5},{8,10},{9,11},{10,... | collective-permute-start | bytes 835592 | tf_op jit(solution)/shard_map/ppermute | solution.py:353
  52.1 10.3 %take_slots_0.1 = (f32[544,128]{1,0:T(8,128)S(1)}, f32[544,128]{1,0:T(8,128)S(1)}) custom-call(s32[8]{0:T(128)S(1)} %stack.26.pos_ref.refs_0_, s32[4,128]{1,0:T(4,128)S(1)} %get-tuple-element.27.refs_1_, f32[8192,128]{1,0:T(8,128)S(1)} %get-tuple-element.28.refs_2_, f32[512,128]{1,0:T(8,128)S(1)} %get-tuple-element.29.refs_3_, ...), custom_call_target="tpu_custom_call" | custom-call | flops 20000000 | bytes 22000000 | tf_op jit(solution)/shard_map/take_slots_0/pallas_call | solution.py:256
  62.3 0.6 collective-permute-start.6
  63.0 0.6 collective-permute-start.3
  63.6 0.0 collective-permute-done.4
  63.6 2.2 %collective-permute-start.5 = (f32[544,128]{1,0:T(8,128)S(1)}, f32[544,128]{1,0:T(8,128)S(1)}, u32[]{:S(2)}, u32[]{:S(2)}) collective-permute-start(f32[544,128]{1,0:T(8,128)S(1)} %add.51), channel_id=1, source_target_pairs={{0,3},{1,0},{2,1},{3,2},{4,7},{5,4},{6,5},{7,6},{8,11},{9,8},{10,9... | collective-permute-start | bytes 835592 | tf_op jit(solution)/shard_map/ppermute | solution.py:353
  65.8 6.6 %collective-permute-done.3.refs_1_ = f32[544,128]{1,0:T(8,128)S(1)} collective-permute-done((f32[544,128]{1,0:T(8,128)S(1)}, f32[544,128]{1,0:T(8,128)S(1)}, u32[]{:S(2)}, u32[]{:S(2)}) %collective-permute-start.3) | collective-permute-done | bytes 278560 | tf_op jit(solution)/shard_map/ppermute | solution.py:353
  72.4 0.0 collective-permute-done.5.refs_2_
  72.4 5.3 %given_order.1 = (f32[136,128]{1,0:T(8,128)S(1)}, f32[136,128]{1,0:T(8,128)S(1)}, f32[136,128]{1,0:T(8,128)S(1)}, f32[136,128]{1,0:T(8,128)S(1)}) custom-call(s32[8]{0:T(128)S(1)} %stack.26.pos_ref.refs_0_, s32[128,128]{1,0:T(8,128)S(1)} %get-tuple-element.25.rank_ref, f32[544,128]{1,0:T(8,128)S(1)} %collective-permute-done.1.refs_0_, ...), custom_call_target="tpu_custom_call" | custom-call | flops 20000000 | bytes 18000000 | tf_op jit(solution)/shard_map/given_order/pallas_call | solution.py:303
  77.7 1.3 %collective-permute-start.8 = (f32[136,128]{1,0:T(8,128)S(1)}, f32[136,128]{1,0:T(8,128)S(1)}, u32[]{:S(2)}, u32[]{:S(2)}) collective-permute-start(f32[136,128]{1,0:T(8,128)S(1)} %get-tuple-element.44), channel_id=1, source_target_pairs={{0,32},{1,33},{2,34},{3,35},{4,36},{5,37},{6,38},{7,39},{8,40},{9,... | collective-permute-start | bytes 208904 | tf_op jit(solution)/shard_map/ppermute | solution.py:353
  79.1 1.5 %collective-permute-start.9 = (f32[136,128]{1,0:T(8,128)S(1)}, f32[136,128]{1,0:T(8,128)S(1)}, u32[]{:S(2)}, u32[]{:S(2)}) collective-permute-start(f32[136,128]{1,0:T(8,128)S(1)} %get-tuple-element.45), channel_id=1, source_target_pairs={{0,96},{1,97},{2,98},{3,99},{4,100},{5,101},{6,102},{7,103},{8,104... | collective-permute-start | bytes 208904 | tf_op jit(solution)/shard_map/ppermute | solution.py:353
  80.6 1.6 %collective-permute-start.7 = (f32[136,128]{1,0:T(8,128)S(1)}, f32[136,128]{1,0:T(8,128)S(1)}, u32[]{:S(2)}, u32[]{:S(2)}) collective-permute-start(f32[136,128]{1,0:T(8,128)S(1)} %get-tuple-element.43), channel_id=1, source_target_pairs={{0,64},{1,65},{2,66},{3,67},{4,68},{5,69},{6,70},{7,71},{8,72},{9,... | collective-permute-start | bytes 208904 | tf_op jit(solution)/shard_map/ppermute | solution.py:353
  82.1 0.1 collective-permute-done.8
  82.2 0.0 collective-permute-done.9
  82.2 3.2 %collective-permute-done.7 = f32[136,128]{1,0:T(8,128)S(1)} collective-permute-done((f32[136,128]{1,0:T(8,128)S(1)}, f32[136,128]{1,0:T(8,128)S(1)}, u32[]{:S(2)}, u32[]{:S(2)}) %collective-permute-start.7) | collective-permute-done | bytes 69664 | tf_op jit(solution)/shard_map/ppermute | solution.py:353
  85.5 2.8 %collective-permute-start.10 = (f32[136,128]{1,0:T(8,128)S(1)}, f32[136,128]{1,0:T(8,128)S(1)}, u32[]{:S(2)}, u32[]{:S(2)}) collective-permute-start(f32[136,128]{1,0:T(8,128)S(1)} %add_add_fusion.refs_2_), channel_id=1, source_target_pairs={{0,16},{1,17},{2,18},{3,19},{4,20},{5,21},{6,22},{7,23},{8,24},{9,... | collective-permute-start | bytes 208904 | tf_op jit(solution)/shard_map/ppermute | solution.py:353
  88.3 0.3 collective-permute-start.11
  88.6 2.4 %collective-permute-start.12 = (f32[136,128]{1,0:T(8,128)S(1)}, f32[136,128]{1,0:T(8,128)S(1)}, u32[]{:S(2)}, u32[]{:S(2)}) collective-permute-start(f32[136,128]{1,0:T(8,128)S(1)} %add_add_fusion.refs_2_), channel_id=1, source_target_pairs={{0,24},{1,25},{2,26},{3,27},{4,28},{5,29},{6,30},{7,31},{8,0},{9,1... | collective-permute-start | bytes 208904 | tf_op jit(solution)/shard_map/ppermute | solution.py:353
  91.0 2.4 %collective-permute-done.11.refs_4_ = f32[136,128]{1,0:T(8,128)S(1)} collective-permute-done((f32[136,128]{1,0:T(8,128)S(1)}, f32[136,128]{1,0:T(8,128)S(1)}, u32[]{:S(2)}, u32[]{:S(2)}) %collective-permute-start.11) | collective-permute-done | bytes 69664 | tf_op jit(solution)/shard_map/ppermute | solution.py:353
  93.4 1.6 %rows_and_gram.1 = (f32[17,256]{1,0:T(8,128)}, f32[17,128]{1,0:T(8,128)S(1)}) custom-call(s32[8]{0:T(128)S(1)} %stack.26.pos_ref.refs_0_, s32[16,2,8,128]{3,2,1,0:T(8,128)S(1)} %bitcast.18, f32[136,128]{1,0:T(8,128)S(1)} %add_add_fusion.refs_2_, f32[136,128]{1,0:T(8,128)S(1)} %collective-permute-done.10.refs_3_, ...), custom_call_target="tpu_custom_call" | custom-call | tf_op jit(solution)/shard_map/rows_and_gram/pallas_call | solution.py:338
  95.0 2.8 %collective-permute-start.15 = (f32[17,128]{1,0:T(8,128)S(1)}, f32[17,128]{1,0:T(8,128)S(1)}, u32[]{:S(2)}, u32[]{:S(2)}) collective-permute-start(f32[17,128]{1,0:T(8,128)S(1)} %get-tuple-element.47), channel_id=1, source_target_pairs={{0,3},{1,0},{2,1},{3,2},{4,7},{5,4},{6,5},{7,6},{8,11},{9,8},{10,9... | collective-permute-start | bytes 26120 | tf_op jit(solution)/shard_map/ppermute | solution.py:353
  97.8 1.2 %collective-permute-start.13 = (f32[17,128]{1,0:T(8,128)S(1)}, f32[17,128]{1,0:T(8,128)S(1)}, u32[]{:S(2)}, u32[]{:S(2)}) collective-permute-start(f32[17,128]{1,0:T(8,128)S(1)} %get-tuple-element.47), channel_id=1, source_target_pairs={{0,2},{1,3},{2,0},{3,1},{4,6},{5,7},{6,4},{7,5},{8,10},{9,11},{10,... | collective-permute-start | bytes 26120 | tf_op jit(solution)/shard_map/ppermute | solution.py:353
  99.0 2.9 %collective-permute-done.13 = f32[17,128]{1,0:T(8,128)S(1)} collective-permute-done((f32[17,128]{1,0:T(8,128)S(1)}, f32[17,128]{1,0:T(8,128)S(1)}, u32[]{:S(2)}, u32[]{:S(2)}) %collective-permute-start.13) | collective-permute-done | bytes 8736 | tf_op jit(solution)/shard_map/ppermute | solution.py:353
  101.8 2.7 %collective-permute-start.18 = (f32[17,128]{1,0:T(8,128)S(1)}, f32[17,128]{1,0:T(8,128)S(1)}, u32[]{:S(2)}, u32[]{:S(2)}) collective-permute-start(f32[17,128]{1,0:T(8,128)S(1)} %add_add_fusion.2), channel_id=1, source_target_pairs={{0,96},{1,97},{2,98},{3,99},{4,100},{5,101},{6,102},{7,103},{8,104... | collective-permute-start | bytes 26120 | tf_op jit(solution)/shard_map/ppermute | solution.py:353
  104.5 0.2 collective-permute-start.16
  104.7 1.2 %collective-permute-done.17 = f32[17,128]{1,0:T(8,128)S(1)} collective-permute-done((f32[17,128]{1,0:T(8,128)S(1)}, f32[17,128]{1,0:T(8,128)S(1)}, u32[]{:S(2)}, u32[]{:S(2)}) %collective-permute-start.17) | collective-permute-done | bytes 8736 | tf_op jit(solution)/shard_map/ppermute | solution.py:353
  105.9 2.7 %collective-permute-done.16 = f32[17,128]{1,0:T(8,128)S(1)} collective-permute-done((f32[17,128]{1,0:T(8,128)S(1)}, f32[17,128]{1,0:T(8,128)S(1)}, u32[]{:S(2)}, u32[]{:S(2)}) %collective-permute-start.16) | collective-permute-done | bytes 8736 | tf_op jit(solution)/shard_map/ppermute | solution.py:353
  108.6 6.2 %collective-permute-start.19 = (f32[17,128]{1,0:T(8,128)S(1)}, f32[17,128]{1,0:T(8,128)S(1)}, u32[]{:S(2)}, u32[]{:S(2)}) collective-permute-start(f32[17,128]{1,0:T(8,128)S(1)} %add_add_fusion.1), channel_id=1, source_target_pairs={{0,4},{1,5},{2,6},{3,7},{4,0},{5,1},{6,2},{7,3},{8,12},{9,13},{10,... | collective-permute-start | bytes 26120 | tf_op jit(solution)/shard_map/ppermute | solution.py:353
  114.8 0.8 collective-permute-done.19
  115.6 0.1 fusion
  115.7 0.7 copy.10
  (21 shorter events, 0.2 us)
Async XLA Ops:
  6.4 2.2 %copy-start.1 = (f32[16,65536]{1,0:T(8,128)S(1)}, f32[16,65536]{1,0:T(8,128)}, u32[]{:S(2)}) copy-start(f32[16,65536]{1,0:T(8,128)} %param.5) | copy-start | bytes 12582916
  8.6 0.9 copy-start.2
  9.6 0.9 copy-start.3
  25.2 12.0 %collective-permute-start = (f32[544,128]{1,0:T(8,128)S(1)}, f32[544,128]{1,0:T(8,128)S(1)}, u32[]{:S(2)}, u32[]{:S(2)}) collective-permute-start(f32[544,128]{1,0:T(8,128)S(1)} %get-tuple-element.31), channel_id=1, source_target_pairs={{0,4},{1,5},{2,6},{3,7},{4,0},{5,1},{6,2},{7,3},{8,12},{9,13},{10,... | collective-permute-start | bytes 835592 | tf_op jit(solution)/shard_map/ppermute | solution.py:353
  37.1 14.9 %collective-permute-start.2 = (f32[544,128]{1,0:T(8,128)S(1)}, f32[544,128]{1,0:T(8,128)S(1)}, u32[]{:S(2)}, u32[]{:S(2)}) collective-permute-start(f32[544,128]{1,0:T(8,128)S(1)} %get-tuple-element.35), channel_id=1, source_target_pairs={{0,4},{1,5},{2,6},{3,7},{4,0},{5,1},{6,2},{7,3},{8,12},{9,13},{10,... | collective-permute-start | bytes 835592 | tf_op jit(solution)/shard_map/ppermute | solution.py:353
  47.8 15.8 %collective-permute-start.4 = (f32[544,128]{1,0:T(8,128)S(1)}, f32[544,128]{1,0:T(8,128)S(1)}, u32[]{:S(2)}, u32[]{:S(2)}) collective-permute-start(f32[544,128]{1,0:T(8,128)S(1)} %get-tuple-element.38), channel_id=1, source_target_pairs={{0,4},{1,5},{2,6},{3,7},{4,0},{5,1},{6,2},{7,3},{8,12},{9,13},{10,... | collective-permute-start | bytes 835592 | tf_op jit(solution)/shard_map/ppermute | solution.py:353
  48.3 17.5 %collective-permute-start.1 = (f32[544,128]{1,0:T(8,128)S(1)}, f32[544,128]{1,0:T(8,128)S(1)}, u32[]{:S(2)}, u32[]{:S(2)}) collective-permute-start(f32[544,128]{1,0:T(8,128)S(1)} %add.49), channel_id=1, source_target_pairs={{0,2},{1,3},{2,0},{3,1},{4,6},{5,7},{6,4},{7,5},{8,10},{9,11},{10,... | collective-permute-start | bytes 835592 | tf_op jit(solution)/shard_map/ppermute | solution.py:353
  52.0 41.4 %copy-start = (s32[32768]{0:T(1024)S(1)}, s32[32768]{0:T(1024)}, u32[]{:S(2)}) copy-start(s32[32768]{0:T(1024)} %param.9) | copy-start | bytes 393220
  62.3 3.4 %collective-permute-start.6 = (f32[544,128]{1,0:T(8,128)S(1)}, f32[544,128]{1,0:T(8,128)S(1)}, u32[]{:S(2)}, u32[]{:S(2)}) collective-permute-start(f32[544,128]{1,0:T(8,128)S(1)} %get-tuple-element.41), channel_id=1, source_target_pairs={{0,4},{1,5},{2,6},{3,7},{4,0},{5,1},{6,2},{7,3},{8,12},{9,13},{10,... | collective-permute-start | bytes 835592 | tf_op jit(solution)/shard_map/ppermute | solution.py:353
  63.0 9.4 %collective-permute-start.3 = (f32[544,128]{1,0:T(8,128)S(1)}, f32[544,128]{1,0:T(8,128)S(1)}, u32[]{:S(2)}, u32[]{:S(2)}) collective-permute-start(f32[544,128]{1,0:T(8,128)S(1)} %add.50), channel_id=1, source_target_pairs={{0,1},{1,2},{2,3},{3,0},{4,5},{5,6},{6,7},{7,4},{8,9},{9,10},{10,1... | collective-permute-start | bytes 835592 | tf_op jit(solution)/shard_map/ppermute | solution.py:353
  63.6 8.8 %collective-permute-start.5 = (f32[544,128]{1,0:T(8,128)S(1)}, f32[544,128]{1,0:T(8,128)S(1)}, u32[]{:S(2)}, u32[]{:S(2)}) collective-permute-start(f32[544,128]{1,0:T(8,128)S(1)} %add.51), channel_id=1, source_target_pairs={{0,3},{1,0},{2,1},{3,2},{4,7},{5,4},{6,5},{7,6},{8,11},{9,8},{10,9... | collective-permute-start | bytes 835592 | tf_op jit(solution)/shard_map/ppermute | solution.py:353
  77.7 4.5 %collective-permute-start.8 = (f32[136,128]{1,0:T(8,128)S(1)}, f32[136,128]{1,0:T(8,128)S(1)}, u32[]{:S(2)}, u32[]{:S(2)}) collective-permute-start(f32[136,128]{1,0:T(8,128)S(1)} %get-tuple-element.44), channel_id=1, source_target_pairs={{0,32},{1,33},{2,34},{3,35},{4,36},{5,37},{6,38},{7,39},{8,40},{9,... | collective-permute-start | bytes 208904 | tf_op jit(solution)/shard_map/ppermute | solution.py:353
  79.1 3.2 %collective-permute-start.9 = (f32[136,128]{1,0:T(8,128)S(1)}, f32[136,128]{1,0:T(8,128)S(1)}, u32[]{:S(2)}, u32[]{:S(2)}) collective-permute-start(f32[136,128]{1,0:T(8,128)S(1)} %get-tuple-element.45), channel_id=1, source_target_pairs={{0,96},{1,97},{2,98},{3,99},{4,100},{5,101},{6,102},{7,103},{8,104... | collective-permute-start | bytes 208904 | tf_op jit(solution)/shard_map/ppermute | solution.py:353
  80.6 4.9 %collective-permute-start.7 = (f32[136,128]{1,0:T(8,128)S(1)}, f32[136,128]{1,0:T(8,128)S(1)}, u32[]{:S(2)}, u32[]{:S(2)}) collective-permute-start(f32[136,128]{1,0:T(8,128)S(1)} %get-tuple-element.43), channel_id=1, source_target_pairs={{0,64},{1,65},{2,66},{3,67},{4,68},{5,69},{6,70},{7,71},{8,72},{9,... | collective-permute-start | bytes 208904 | tf_op jit(solution)/shard_map/ppermute | solution.py:353
  85.5 5.5 %collective-permute-start.10 = (f32[136,128]{1,0:T(8,128)S(1)}, f32[136,128]{1,0:T(8,128)S(1)}, u32[]{:S(2)}, u32[]{:S(2)}) collective-permute-start(f32[136,128]{1,0:T(8,128)S(1)} %add_add_fusion.refs_2_), channel_id=1, source_target_pairs={{0,16},{1,17},{2,18},{3,19},{4,20},{5,21},{6,22},{7,23},{8,24},{9,... | collective-permute-start | bytes 208904 | tf_op jit(solution)/shard_map/ppermute | solution.py:353
  88.3 5.1 %collective-permute-start.11 = (f32[136,128]{1,0:T(8,128)S(1)}, f32[136,128]{1,0:T(8,128)S(1)}, u32[]{:S(2)}, u32[]{:S(2)}) collective-permute-start(f32[136,128]{1,0:T(8,128)S(1)} %add_add_fusion.refs_2_), channel_id=1, source_target_pairs={{0,8},{1,9},{2,10},{3,11},{4,12},{5,13},{6,14},{7,15},{8,16},{9,17... | collective-permute-start | bytes 208904 | tf_op jit(solution)/shard_map/ppermute | solution.py:353
  88.6 4.8 %collective-permute-start.12 = (f32[136,128]{1,0:T(8,128)S(1)}, f32[136,128]{1,0:T(8,128)S(1)}, u32[]{:S(2)}, u32[]{:S(2)}) collective-permute-start(f32[136,128]{1,0:T(8,128)S(1)} %add_add_fusion.refs_2_), channel_id=1, source_target_pairs={{0,24},{1,25},{2,26},{3,27},{4,28},{5,29},{6,30},{7,31},{8,0},{9,1... | collective-permute-start | bytes 208904 | tf_op jit(solution)/shard_map/ppermute | solution.py:353
  95.0 4.0 %collective-permute-start.14 = (f32[17,128]{1,0:T(8,128)S(1)}, f32[17,128]{1,0:T(8,128)S(1)}, u32[]{:S(2)}, u32[]{:S(2)}) collective-permute-start(f32[17,128]{1,0:T(8,128)S(1)} %get-tuple-element.47), channel_id=1, source_target_pairs={{0,1},{1,2},{2,3},{3,0},{4,5},{5,6},{6,7},{7,4},{8,9},{9,10},{10,1... | collective-permute-start | bytes 26120 | tf_op jit(solution)/shard_map/ppermute | solution.py:353
  95.0 4.0 %collective-permute-start.15 = (f32[17,128]{1,0:T(8,128)S(1)}, f32[17,128]{1,0:T(8,128)S(1)}, u32[]{:S(2)}, u32[]{:S(2)}) collective-permute-start(f32[17,128]{1,0:T(8,128)S(1)} %get-tuple-element.47), channel_id=1, source_target_pairs={{0,3},{1,0},{2,1},{3,2},{4,7},{5,4},{6,5},{7,6},{8,11},{9,8},{10,9... | collective-permute-start | bytes 26120 | tf_op jit(solution)/shard_map/ppermute | solution.py:353
  97.8 4.0 %collective-permute-start.13 = (f32[17,128]{1,0:T(8,128)S(1)}, f32[17,128]{1,0:T(8,128)S(1)}, u32[]{:S(2)}, u32[]{:S(2)}) collective-permute-start(f32[17,128]{1,0:T(8,128)S(1)} %get-tuple-element.47), channel_id=1, source_target_pairs={{0,2},{1,3},{2,0},{3,1},{4,6},{5,7},{6,4},{7,5},{8,10},{9,11},{10,... | collective-permute-start | bytes 26120 | tf_op jit(solution)/shard_map/ppermute | solution.py:353
  101.8 4.1 %collective-permute-start.17 = (f32[17,128]{1,0:T(8,128)S(1)}, f32[17,128]{1,0:T(8,128)S(1)}, u32[]{:S(2)}, u32[]{:S(2)}) collective-permute-start(f32[17,128]{1,0:T(8,128)S(1)} %add_add_fusion.2), channel_id=1, source_target_pairs={{0,32},{1,33},{2,34},{3,35},{4,36},{5,37},{6,38},{7,39},{8,40},{9,... | collective-permute-start | bytes 26120 | tf_op jit(solution)/shard_map/ppermute | solution.py:353
  101.8 4.0 %collective-permute-start.18 = (f32[17,128]{1,0:T(8,128)S(1)}, f32[17,128]{1,0:T(8,128)S(1)}, u32[]{:S(2)}, u32[]{:S(2)}) collective-permute-start(f32[17,128]{1,0:T(8,128)S(1)} %add_add_fusion.2), channel_id=1, source_target_pairs={{0,96},{1,97},{2,98},{3,99},{4,100},{5,101},{6,102},{7,103},{8,104... | collective-permute-start | bytes 26120 | tf_op jit(solution)/shard_map/ppermute | solution.py:353
  104.5 4.0 %collective-permute-start.16 = (f32[17,128]{1,0:T(8,128)S(1)}, f32[17,128]{1,0:T(8,128)S(1)}, u32[]{:S(2)}, u32[]{:S(2)}) collective-permute-start(f32[17,128]{1,0:T(8,128)S(1)} %add_add_fusion.2), channel_id=1, source_target_pairs={{0,64},{1,65},{2,66},{3,67},{4,68},{5,69},{6,70},{7,71},{8,72},{9,... | collective-permute-start | bytes 26120 | tf_op jit(solution)/shard_map/ppermute | solution.py:353
  108.6 7.1 %collective-permute-start.19 = (f32[17,128]{1,0:T(8,128)S(1)}, f32[17,128]{1,0:T(8,128)S(1)}, u32[]{:S(2)}, u32[]{:S(2)}) collective-permute-start(f32[17,128]{1,0:T(8,128)S(1)} %add_add_fusion.1), channel_id=1, source_target_pairs={{0,4},{1,5},{2,6},{3,7},{4,0},{5,1},{6,2},{7,3},{8,12},{9,13},{10,... | collective-permute-start | bytes 26120 | tf_op jit(solution)/shard_map/ppermute | solution.py:353

commit v3 on v2

--- a/solution.py
+++ b/solution.py
@@ -14,6 +14,9 @@
 SIDE = 256
 PEEL = 20
 STEP = 4
+EIGHTHS = 4
+ROWS = 512
+ROWS_PAD = 536
 
 
 def number(y, x, c, z):
@@ -87,70 +90,59 @@
     return v
 
 
-def sort_kernel(pos_ref, samples_ref, keys_ref, ends_ref, rank_ref, scratch):
+def swap_bits(t, sub, lane, p, q):
+    sb, lb = (sub >> p) & 1, (lane >> q) & 1
+    o = lane_take(t, lane ^ (1 << q))
+    o = jnp.where(sb == 1, pltpu.roll(o, 1 << p, 0), pltpu.roll(o, 8 - (1 << p), 0))
+    return jnp.where(sb == lb, t, o)
+
+
+def split(x):
+    hi = x.astype(jnp.bfloat16)
+    lo = (x - hi.astype(jnp.float32)).astype(jnp.bfloat16)
+    return hi, lo
+
+
+def dot(a, b):
+    return lax.dot_general(a, b, (((1,), (0,)), ((), ())), preferred_element_type=jnp.float32)
+
+
+def prepare_kernel(
+    pos_ref, samples_ref, basis_hbm, target_hbm, bits_hbm, keys_ref, ends_ref, own_ref, tab, last,
+    basis_ref, target_ref, bits_ref, scratch, sems,
+):
+    copies = [
+        pltpu.make_async_copy(src, dst, sems.at[n])
+        for n, (src, dst) in enumerate(
+            ((bits_hbm, bits_ref), (target_hbm, target_ref), (basis_hbm, basis_ref))
+        )
+    ]
+    for copy in copies:
+        copy.start()
+
     me, core = pos_ref[0], pos_ref[1]
     sub = lax.broadcasted_iota(jnp.int32, (8, LANES), 0)
     lane = lax.broadcasted_iota(jnp.int32, (8, LANES), 1)
-    both = []
     for c in range(2):
         v = []
         for i in range(16):
             s = samples_ref[i, c]
+            s = swap_bits(swap_bits(s, sub, lane, 1, 5), sub, lane, 2, 6)
             p = s & 65535
             place = (((p >> 7) & 1) << 15) | ((p >> 8) << 7) | (p & 127)
             odd = fold((s >> 16) & me)
-            r = i * 256 + sub * 32 + (lane & 31)
+            r = i * 256 + (sub & 1) * 128 + (sub >> 1) * 32 + (lane & 31)
             v.append((place << 13) | (r << 1) | odd)
         v = bitonic(v, sub, lane)
-        both.append(v)
         for i in range(16):
-            scratch[pl.ds(i, 8, stride=16), :] = v[i]
-        ends_ref[2 * c : 2 * c + 1, :] = scratch[0:1, :] >> 20
-        ends_ref[2 * c + 1 : 2 * c + 2, :] = scratch[127:128, :] >> 20
-        keys_ref[c * LANES : (c + 1) * LANES, :] = scratch[...].T
-    v = []
-    for i in range(16):
-        key = jnp.where(core == 0, both[0][i], both[1][i])
-        slot = (lane & 31) * LANES + sub * 16 + i
-        v.append((((key >> 1) & 4095) << 12) | slot)
-    v = bitonic(v, sub, lane)
-    for i in range(16):
-        scratch[pl.ds(i, 8, stride=16), :] = v[i] & 4095
-    rank_ref[...] = scratch[...].T
-
-
-VMEM = pl.BlockSpec(memory_space=pltpu.VMEM)
-SMEM = pl.BlockSpec(memory_space=pltpu.SMEM)
-
-
-def sort_call(pos, samples):
-    return pl.pallas_call(
-        sort_kernel,
-        out_shape=(
-            jax.ShapeDtypeStruct((256, LANES), jnp.int32),
-            jax.ShapeDtypeStruct((4, LANES), jnp.int32),
-            jax.ShapeDtypeStruct((LANES, LANES), jnp.int32),
-        ),
-        in_specs=[SMEM, VMEM],
-        out_specs=(VMEM,) * 3,
-        scratch_shapes=[pltpu.VMEM((LANES, LANES), jnp.int32)],
-        compiler_params=pltpu.CompilerParams(vmem_limit_bytes=8 * 2**20),
-        cost_estimate=pl.CostEstimate(flops=20_000_000, bytes_accessed=20_000_000, transcendentals=0),
-        name="sort_slots",
-    )(pos, samples)
-
-
-def split(x):
-    hi = x.astype(jnp.bfloat16)
-    lo = (x - hi.astype(jnp.float32)).astype(jnp.bfloat16)
-    return hi, lo
-
-
-def dot(a, b):
-    return lax.dot_general(a, b, (((1,), (0,)), ((), ())), preferred_element_type=jnp.float32)
-
-
-def mix_kernel(basis_ref, target_ref, bits_ref, tab, last):
+            scratch[c, pl.ds(i, 8, stride=16), :] = v[i]
+        ends_ref[2 * c : 2 * c + 1, :] = scratch[c, 0:1, :] >> 20
+        ends_ref[2 * c + 1 : 2 * c + 2, :] = scratch[c, 127:128, :] >> 20
+        keys_ref[c * LANES : (c + 1) * LANES, :] = scratch[c].T
+    own_ref[...] = scratch[core]
+
+    for copy in copies:
+        copy.wait()
     a = lax.broadcasted_iota(jnp.int32, (SIDE, SIDE), 0)
     b = lax.broadcasted_iota(jnp.int32, (SIDE, SIDE), 1)
     walsh = (1 - 2 * fold(a & b)).astype(jnp.float32).astype(jnp.bfloat16)
@@ -173,21 +165,66 @@
                 tab[pl.ds(bh * SIDE * 16 + k, SIDE, stride=16), :] = half
             else:
                 last[bh * SIDE : (bh + 1) * SIDE, :] = half
-
-
-def mix_call(basis, target, bits):
-    return pl.pallas_call(
-        mix_kernel,
+    tab[ROWS * 16 :, :] = jnp.zeros(((ROWS_PAD - ROWS) * 16, LANES), jnp.float32)
+    last[ROWS:, :] = jnp.zeros((ROWS_PAD - ROWS, LANES), jnp.float32)
+
+
+VMEM = pl.BlockSpec(memory_space=pltpu.VMEM)
+SMEM = pl.BlockSpec(memory_space=pltpu.SMEM)
+FAR = pl.BlockSpec(memory_space=pltpu.HBM)
+COST = pl.CostEstimate(flops=1_000_000, bytes_accessed=1_000_000, transcendentals=0)
+
+
+def prepare_call(pos, samples, basis, target, bits):
+    return pl.pallas_call(
+        prepare_kernel,
         out_shape=(
-            jax.ShapeDtypeStruct((512 * 16, LANES), jnp.float32),
-            jax.ShapeDtypeStruct((512, LANES), jnp.float32),
+            jax.ShapeDtypeStruct((256, LANES), jnp.int32),
+            jax.ShapeDtypeStruct((4, LANES), jnp.int32),
+            jax.ShapeDtypeStruct((LANES, LANES), jnp.int32),
+            jax.ShapeDtypeStruct((ROWS_PAD * 16, LANES), jnp.float32),
+            jax.ShapeDtypeStruct((ROWS_PAD, LANES), jnp.float32),
         ),
-        in_specs=[VMEM] * 3,
-        out_specs=(VMEM,) * 2,
-        compiler_params=pltpu.CompilerParams(vmem_limit_bytes=16 * 2**20),
-        cost_estimate=pl.CostEstimate(flops=2 * 2**31, bytes_accessed=20_000_000, transcendentals=0),
-        name="local_walsh",
-    )(basis, target, bits)
+        in_specs=[SMEM, VMEM, FAR, FAR, FAR],
+        out_specs=(VMEM,) * 5,
+        scratch_shapes=[
+            pltpu.VMEM((8192, LANES), jnp.float32),
+            pltpu.VMEM((512, LANES), jnp.float32),
+            pltpu.VMEM((512, LANES), jnp.int32),
+            pltpu.VMEM((2, LANES, LANES), jnp.int32),
+            pltpu.SemaphoreType.DMA((3,)),
+        ],
+        compiler_params=pltpu.CompilerParams(vmem_limit_bytes=24 * 2**20),
+        cost_estimate=COST,
+        name="sort_and_walsh",
+    )(pos, samples, basis, target, bits)
+
+
+def rank_kernel(own_ref, rank_ref, scratch):
+    sub = lax.broadcasted_iota(jnp.int32, (8, LANES), 0)
+    lane = lax.broadcasted_iota(jnp.int32, (8, LANES), 1)
+    v = []
+    for i in range(16):
+        key = own_ref[pl.ds(i, 8, stride=16), :]
+        slot = (lane & 31) * LANES + sub * 16 + i
+        v.append((((key >> 1) & 4095) << 12) | slot)
+    v = bitonic(v, sub, lane)
+    for i in range(16):
+        scratch[pl.ds(i, 8, stride=16), :] = v[i] & 4095
+    rank_ref[...] = scratch[...].T
+
+
+def rank_call(own):
+    return pl.pallas_call(
+        rank_kernel,
+        out_shape=jax.ShapeDtypeStruct((LANES, LANES), jnp.int32),
+        in_specs=[VMEM],
+        out_specs=VMEM,
+        scratch_shapes=[pltpu.VMEM((LANES, LANES), jnp.int32)],
+        compiler_params=pltpu.CompilerParams(vmem_limit_bytes=4 * 2**20),
+        cost_estimate=COST,
+        name="row_rank",
+    )(own)
 
 
 def slots_kernel(scale, off, pos_ref, ends_ref, tab, last, keys_ref, keep, give):
@@ -213,38 +250,37 @@
                 subrows.append((key >> 20) - (low >> 3) * 8 - sub)
                 weights.append(jnp.where((key & 1) != 0, -scale, scale))
 
-            def add_rows(first, count, acc):
+            def add_rows(first, count, eighth, eighths, acc, end=None):
                 acc = list(acc)
-                for u in range(count):
-                    for q in range(4):
-                        row = jnp.minimum(lows[q] + first + u, 511)
+                for q in range(4):
+                    for u in range(count):
+                        row = lows[q] + first + u
+                        row = row if end is None else jnp.minimum(row, end)
                         hit = rows_of[q] == first + u
                         for t in range(2):
                             tile = tab[pl.ds(pl.multiple_of(row * 16 + 8 * t, 8), 8), :]
-                            acc[q * 2 + t] = jnp.where(hit, lane_take(tile, lanes_of[q]), acc[q * 2 + t])
+                            acc[q * 3 + t] = jnp.where(hit, lane_take(tile, lanes_of[q]), acc[q * 3 + t])
+                    for u in range(eighths):
+                        row = tiles[q] + eighth + u
+                        row = row if end is None else jnp.minimum(row, end // 8)
+                        tile = last[pl.ds(pl.multiple_of(row * 8, 8), 8), :]
+                        hit = subrows[q] == (eighth + u) * 8
+                        acc[q * 3 + 2] = jnp.where(hit, lane_take(tile, lanes_of[q]), acc[q * 3 + 2])
                 return tuple(acc)
 
-            def add_last(first, count, acc):
-                acc = list(acc)
-                for u in range(count):
-                    for q in range(4):
-                        row = jnp.minimum(tiles[q] + first + u, 63)
-                        tile = last[pl.ds(pl.multiple_of(row * 8, 8), 8), :]
-                        hit = subrows[q] == (first + u) * 8
-                        acc[q] = jnp.where(hit, lane_take(tile, lanes_of[q]), acc[q])
-                return tuple(acc)
-
-            zero = jnp.zeros((8, LANES), jnp.float32)
-            acc = add_rows(0, PEEL, (zero,) * 8)
+            acc = add_rows(0, PEEL, 0, EIGHTHS, (jnp.zeros((8, LANES), jnp.float32),) * 12)
             more = (jnp.maximum(most - PEEL, 0) + STEP - 1) // STEP
-            acc = lax.fori_loop(0, more, lambda n, a: add_rows(PEEL + n * STEP, STEP, a), acc)
-            tail = add_last(0, 4, (zero,) * 4)
-            tail = lax.fori_loop(4, jnp.maximum(many, 4), lambda n, a: add_last(n, 1, a), tail)
+            more = jnp.maximum(more, many - EIGHTHS)
+
+            def further(n, acc):
+                return add_rows(PEEL + n * STEP, STEP, EIGHTHS + n, 1, acc, ROWS - 1)
+
+            acc = lax.fori_loop(0, more, further, acc)
             base = it * (4 * COLS)
             for q in range(4):
                 for t in range(2):
-                    out[pl.ds(base + q + 32 * t, 8, stride=4), :] = acc[q * 2 + t] * weights[q]
-                line = jnp.sum(tail[q], axis=0, keepdims=True)
+                    out[pl.ds(base + q + 32 * t, 8, stride=4), :] = acc[q * 3 + t] * weights[q]
+                line = jnp.sum(acc[q * 3 + 2], axis=0, keepdims=True)
                 out[pl.ds(base + q + 64, 1), :] = line * weights[q][0:1]
             return 0
 
@@ -259,13 +295,13 @@
         in_specs=[SMEM, SMEM, VMEM, VMEM, VMEM],
         out_specs=(VMEM,) * 2,
         compiler_params=pltpu.CompilerParams(vmem_limit_bytes=12 * 2**20),
-        cost_estimate=pl.CostEstimate(flops=20_000_000, bytes_accessed=22_000_000, transcendentals=0),
+        cost_estimate=COST,
         name=f"take_slots_{off}",
     )(pos, ends, tab, last, keys)
 
 
-def order_kernel(pos_ref, rank_ref, *refs):
-    parts, outs, table = refs[:4], refs[4:8], refs[8]
+def order_kernel(rels, pos_ref, rank_ref, *refs):
+    parts, outs, table = refs[:4], refs[4:-1], refs[-1]
     y, z = pos_ref[2], pos_ref[4]
     table[...] = (parts[0][...] + parts[1][...]) + (parts[2][...] + parts[3][...])
     rows = 8 * COLS
@@ -276,7 +312,7 @@
     collect = jnp.where((cr % (4 * COLS)) // 4 == ck, 1.0, 0.0).astype(jnp.bfloat16)
 
     def step(i, _):
-        for rel, out in enumerate(outs):
+        for rel, out in zip(rels, outs):
             line = z * 32 + ((y + rel) & 3) * 8 + i
             slot = jnp.broadcast_to(rank_ref[pl.ds(line, 1), :], (8, LANES))
             index = slot & 127
@@ -298,17 +334,17 @@
     lax.fori_loop(0, 8, step, 0)
 
 
-def order_call(pos, rank, parts):
+def order_call(rels, pos, rank, parts):
     rows = 8 * COLS
     return pl.pallas_call(
-        order_kernel,
-        out_shape=(jax.ShapeDtypeStruct((rows, LANES), jnp.float32),) * 4,
+        lambda *refs: order_kernel(rels, *refs),
+        out_shape=(jax.ShapeDtypeStruct((rows, LANES), jnp.float32),) * len(rels),
         in_specs=[SMEM] + [VMEM] * 5,
-        out_specs=(VMEM,) * 4,
+        out_specs=(VMEM,) * len(rels),
         scratch_shapes=[pltpu.VMEM((4 * rows, LANES), jnp.float32)],
         compiler_params=pltpu.CompilerParams(vmem_limit_bytes=8 * 2**20),
-        cost_estimate=pl.CostEstimate(flops=20_000_000, bytes_accessed=18_000_000, transcendentals=0),
-        name="given_order",
+        cost_estimate=COST,
+        name=f"given_order_{len(rels)}",
     )(pos, rank, *parts)
 
 
@@ -331,7 +367,12 @@
         value, left, (((1,), (1,)), ((), ())),
         precision=lax.Precision.HIGHEST, preferred_element_type=jnp.float32,
     )
-    gram[...] = factor * total[:COLS]
+    total = factor * total
+    for to in range(4):
+        own = [total[8 * n : 8 * n + 8, 32 * to : 32 * to + 32] for n in range(3)]
+        message = jnp.concatenate(own + [jnp.zeros((8, 32), jnp.float32)], axis=1)
+        for row in range(4):
+            gram[row * 4 + to] = message
 
 
 def finish_call(factor, pos, owners, parts):
@@ -339,7 +380,7 @@
         lambda *refs: finish_kernel(factor, *refs),
         out_shape=(
             jax.ShapeDtypeStruct((COLS, SIDE), jnp.float32),
-            jax.ShapeDtypeStruct((COLS, LANES), jnp.float32),
+            jax.ShapeDtypeStruct((16, 8, LANES), jnp.float32),
         ),
         in_specs=[SMEM] + [VMEM] * 5,
         out_specs=(VMEM,) * 2,
@@ -349,8 +390,30 @@
     )(pos, owners, *parts)
 
 
+def gram_kernel(a, b, out):
+    total = a[...] + b[...]
+    total = jnp.concatenate([total[:, 32 * n : 32 * n + 32] for n in range(3)], axis=0).T
+    for g in range(2):
+        out[g] = total[16 * g : 16 * g + 16, :COLS]
+
+
+def gram_call(a, b):
+    return pl.pallas_call(
+        gram_kernel,
+        out_shape=jax.ShapeDtypeStruct((2, 16, COLS), jnp.float32),
+        in_specs=[VMEM] * 2,
+        out_specs=VMEM,
+        compiler_params=pltpu.CompilerParams(vmem_limit_bytes=4 * 2**20),
+        name="own_gram",
+    )(a, b)
+
+
 def send(v, axis, off):
     return lax.ppermute(v, AXES, shift(axis, off))
+
+
+def planes():
+    return [[number(y, x, c, z) for y in range(4) for z in range(4)] for x in range(4) for c in range(2)]
 
 
 def shards(basis, target, sign_bits, samples, owners):
@@ -362,10 +425,10 @@
     core, x, y = wide & 1, (wide >> 1) & 3, wide >> 3
     pos = jnp.stack([wide * 4 + z, core, y, x, z, z, z, z]).astype(jnp.int32)
 
-    lined = samples.reshape(16, 2, 4, 8, 32).transpose(0, 1, 3, 2, 4).reshape(16, 2, 8, LANES)
-    keys, ends, rank = sort_call(pos, lined)
     tiles = basis.reshape(2, 8, 512, LANES).transpose(0, 2, 1, 3).reshape(8192, LANES)
-    tab, last = mix_call(tiles, target.reshape(512, LANES), sign_bits.reshape(512, LANES))
+    far = [tiles, target.reshape(512, LANES), sign_bits.reshape(512, LANES)]
+    far = [pltpu.with_memory_space_constraint(v, pltpu.HBM) for v in far]
+    keys, ends, own, tab, last = prepare_call(pos, samples.reshape(16, 2, 8, LANES), *far)
     parts, held = [], []
     for n, off in enumerate((2, 1, 3, 0)):
         if n >= 2:
@@ -374,16 +437,17 @@
         held.append(keep + send(give, "c", 1))
         if n >= 2:
             parts.append(send(held[n - 2], "z", (2, 1)[n - 2]))
+    own, keep = lax.optimization_barrier((own, keep))
+    rank = rank_call(own)
     parts += [send(held[2], "z", 3), held[3]]
-    lines = order_call(pos, rank, parts)
-    line = (lines[0] + send(lines[2], "y", 2)) + (send(lines[1], "y", 1) + send(lines[3], "y", 3))
+    lines = order_call((2, 1, 3), pos, rank, parts)
+    line = order_call((0,), pos, rank, parts)[0]
+    line = (line + send(lines[0], "y", 2)) + (send(lines[1], "y", 1) + send(lines[2], "y", 3))
     around = [line] + [send(line, "x", off) for off in (2, 1, 3)]
     sketch, gram = finish_call(GROUPS / total_samples, pos, owners.reshape(16, 2, 8, LANES), around)
-    for axis in ("z", "y"):
-        gram = (gram + send(gram, axis, 2)) + (send(gram, axis, 1) + send(gram, axis, 3))
-    gram = gram + send(gram, "c", 1)
-    own = lax.dynamic_slice_in_dim(gram, z * 32, 32, 1)
-    return sketch.T, own.T.reshape(2, 16, COLS)
+    gram = lax.all_to_all(gram, AXES, 0, 0, tiled=True, axis_index_groups=planes())
+    gram = jnp.sum(gram, axis=0)
+    return sketch.T, gram_call(gram, send(gram, "c", 1))
 
 
 def solution(mesh):

time: 117 us -> 88.4 us (0.76)
  Pallas kernels: 57 us -> 41.2 us
  blocking collectives: 0 us -> 10.8 us
  waiting for transfers between devices: 19.9 us -> 10.2 us
  starting transfers between devices: 32.2 us -> 24 us
  local copies, waits for them, and re-layouts: 6.35 us -> 1 us
    pallas_call x4, Pallas kernels: 41.4 us -> 20.3 us  [slots_call(): pl.pallas_call(lambda *refs: slots_kernel(scale, off, *refs), out_shape=(...]
    all_to_all x0 -> x1, blocking collectives: none -> 10.8 us  [shards(): lax.all_to_all(gram, AXES, 0, 0, tiled=True, axis_index_groups=planes())]
    ppermute x20 -> x14, waiting for transfers between devices: 19.9 us -> 10.2 us  [send(): return lax.ppermute(v, AXES, shift(axis, off))]
    ppermute x20 -> x14, starting transfers between devices: 32.2 us -> 24 us  [send(): return lax.ppermute(v, AXES, shift(axis, off))]
    pallas_call x3 -> x5, Pallas kernels: 13.9 us -> 19.3 us  [the longest x1 9.46 us: prepare_call(): pl.pallas_call(prepare_kernel, out_shape=(jax.ShapeDtypeStruct((256, LANE...]
    unnamed x9 -> x4, local copies, waits for them, and re-layouts: 4.78 us -> 0.91 us
    reshape x2 -> x0, local copies, waits for them, and re-layouts: 1.32 us -> none  [shards(): samples.reshape(16, 2, 4, 8, 32).transpose(0, 1, 3, 2, 4)]
  transfers between devices with their start and end apart: 20 -> 14, of which waited for: 7 -> 4; matrix products, arithmetic and copies ran while one was open for 0% -> 0% of each run, Pallas kernels for 27% -> 22%
where the time goes in v3:
time: 88.4 us; the launch traced here: 88.1 us
  Pallas kernels  41.2 us (47%)
  starting transfers between devices  24 us (27%)
  blocking collectives  10.8 us (12%)
  waiting for transfers between devices  10.2 us (12%)
  local copies, waits for them, and re-layouts  1 us (1%)
    ppermute x14, starting transfers between devices, send(): return lax.ppermute(v, AXES, shift(axis, off))  24 us
    pallas_call x4, Pallas kernels, slots_call(): pl.pallas_call(lambda *refs: slots_kernel(scale, off, *refs), out_shape=(...  20.3 us
    all_to_all x1, blocking collectives, shards(): lax.all_to_all(gram, AXES, 0, 0, tiled=True, axis_index_groups=planes())  10.8 us
    ppermute x14, waiting for transfers between devices, send(): return lax.ppermute(v, AXES, shift(axis, off))  10.2 us
    pallas_call x1, Pallas kernels, prepare_call(): pl.pallas_call(prepare_kernel, out_shape=(jax.ShapeDtypeStruct((256, LANE...  9.46 us
    pallas_call x2, Pallas kernels, order_call(): pl.pallas_call(lambda *refs: order_kernel(rels, *refs), out_shape=(jax.Sh...  7.46 us
  transfers between devices with their start and end apart: 14, of which 4 were waited for; matrix products, arithmetic and copies ran while one was open for 0% of the time, Pallas kernels for 22%

profile of v3, /device:TPU:1, one launch (start us, length us, event | category | flops | bytes accessed | tf_op | source)
XLA Modules:
  0.0 88.1 jit_solution(18011887768900806929)
XLA Ops:
  0.6 0.1 stack.26.pos_ref.refs_0_
  0.7 0.0 copy-start
  0.7 0.9 %copy-done = s32[32768]{0:T(1024)S(1)} copy-done((s32[32768]{0:T(1024)S(1)}, s32[32768]{0:T(1024)}, u32[]{:S(2)}) %copy-start) | copy-done | bytes 131096
  1.6 9.5 %sort_and_walsh.1 = (s32[256,128]{1,0:T(8,128)S(1)}, s32[4,128]{1,0:T(4,128)S(1)}, s32[128,128]{1,0:T(8,128)S(1)}, f32[8576,128]{1,0:T(8,128)S(1)}, f32[536,128]{1,0:T(8,128)S(1)}) custom-call(s32[8]{0:T(128)S(1)} %stack.26.pos_ref.refs_0_, s32[16,2,8,128]{3,2,1,0:T(8,128)S(1)} %bitcast.15, f32[8192,128]{1,0:T(8,128)} %bitcast.17, f32[512,128]{1,0:T(8,128)} %bitcast.18, ...), custom_call_target="tpu_custom_call" | custom-call | flops 1000000 | bytes 1000000 | tf_op jit(solution)/shard_map/sort_and_walsh/pallas_call | solution.py:179
  11.1 5.1 %take_slots_2.1 = (f32[544,128]{1,0:T(8,128)S(1)}, f32[544,128]{1,0:T(8,128)S(1)}) custom-call(s32[8]{0:T(128)S(1)} %stack.26.pos_ref.refs_0_, s32[4,128]{1,0:T(4,128)S(1)} %get-tuple-element.26.refs_1_, f32[8576,128]{1,0:T(8,128)S(1)} %get-tuple-element.27.refs_2_, f32[536,128]{1,0:T(8,128)S(1)} %get-tuple-element.28.refs_3_, ...), custom_call_target="tpu_custom_call" | custom-call | flops 1000000 | bytes 1000000 | tf_op jit(solution)/shard_map/take_slots_2/pallas_call | solution.py:292
  16.2 1.5 %collective-permute-start = (f32[544,128]{1,0:T(8,128)S(1)}, f32[544,128]{1,0:T(8,128)S(1)}, u32[]{:S(2)}, u32[]{:S(2)}) collective-permute-start(f32[544,128]{1,0:T(8,128)S(1)} %get-tuple-element.31), channel_id=1, source_target_pairs={{0,4},{1,5},{2,6},{3,7},{4,0},{5,1},{6,2},{7,3},{8,12},{9,13},{10,... | collective-permute-start | bytes 835592 | tf_op jit(solution)/shard_map/ppermute | solution.py:412
  17.7 5.1 %take_slots_1.1 = (f32[544,128]{1,0:T(8,128)S(1)}, f32[544,128]{1,0:T(8,128)S(1)}) custom-call(s32[8]{0:T(128)S(1)} %stack.26.pos_ref.refs_0_, s32[4,128]{1,0:T(4,128)S(1)} %get-tuple-element.26.refs_1_, f32[8576,128]{1,0:T(8,128)S(1)} %get-tuple-element.27.refs_2_, f32[536,128]{1,0:T(8,128)S(1)} %get-tuple-element.28.refs_3_, ...), custom_call_target="tpu_custom_call" | custom-call | flops 1000000 | bytes 1000000 | tf_op jit(solution)/shard_map/take_slots_1/pallas_call | solution.py:292
  22.9 0.1 collective-permute-start.1
  23.0 0.0 collective-permute-done
  23.0 5.0 %take_slots_3.1 = (f32[544,128]{1,0:T(8,128)S(1)}, f32[544,128]{1,0:T(8,128)S(1)}) custom-call(s32[8]{0:T(128)S(1)} %stack.26.pos_ref.refs_0_, s32[4,128]{1,0:T(4,128)S(1)} %get-tuple-element.26.refs_1_, f32[8576,128]{1,0:T(8,128)S(1)} %get-tuple-element.27.refs_2_, f32[536,128]{1,0:T(8,128)S(1)} %get-tuple-element.28.refs_3_, ...), custom_call_target="tpu_custom_call" | custom-call | flops 1000000 | bytes 1000000 | tf_op jit(solution)/shard_map/take_slots_3/pallas_call | solution.py:292
  28.0 0.6 collective-permute-start.4
  28.6 0.0 collective-permute-done.1
  28.6 0.0 copy-start.1
  28.6 1.7 %collective-permute-start.3 = (f32[544,128]{1,0:T(8,128)S(1)}, f32[544,128]{1,0:T(8,128)S(1)}, u32[]{:S(2)}, u32[]{:S(2)}) collective-permute-start(f32[544,128]{1,0:T(8,128)S(1)} %add.26), channel_id=1, source_target_pairs={{0,1},{1,2},{2,3},{3,0},{4,5},{5,6},{6,7},{7,4},{8,9},{9,10},{10,1... | collective-permute-start | bytes 835592 | tf_op jit(solution)/shard_map/ppermute | solution.py:412
  30.3 3.4 %collective-permute-start.2 = (f32[544,128]{1,0:T(8,128)S(1)}, f32[544,128]{1,0:T(8,128)S(1)}, u32[]{:S(2)}, u32[]{:S(2)}) collective-permute-start(f32[544,128]{1,0:T(8,128)S(1)} %add.25), channel_id=1, source_target_pairs={{0,2},{1,3},{2,0},{3,1},{4,6},{5,7},{6,4},{7,5},{8,10},{9,11},{10,... | collective-permute-start | bytes 835592 | tf_op jit(solution)/shard_map/ppermute | solution.py:412
  33.7 5.0 %take_slots_0.1 = (f32[544,128]{1,0:T(8,128)S(1)}, f32[544,128]{1,0:T(8,128)S(1)}) custom-call(s32[8]{0:T(128)S(1)} %stack.26.pos_ref.refs_0_, s32[4,128]{1,0:T(4,128)S(1)} %get-tuple-element.26.refs_1_, f32[8576,128]{1,0:T(8,128)S(1)} %get-tuple-element.27.refs_2_, f32[536,128]{1,0:T(8,128)S(1)} %get-tuple-element.28.refs_3_, ...), custom_call_target="tpu_custom_call" | custom-call | flops 1000000 | bytes 1000000 | tf_op jit(solution)/shard_map/take_slots_0/pallas_call | solution.py:292
  38.8 0.7 collective-permute-start.6
  39.4 0.0 collective-permute-done.4
  39.5 0.7 collective-permute-start.5
  40.1 1.7 %row_rank.1.refs_1_ = s32[128,128]{1,0:T(8,128)S(1)} custom-call(s32[128,128]{1,0:T(8,128)S(1)} %get-tuple-element.37.own_ref), custom_call_target="tpu_custom_call" | custom-call | flops 1000000 | bytes 1000000 | tf_op jit(solution)/shard_map/row_rank/pallas_call | solution.py:218
  41.8 0.0 collective-permute-done.6
  41.8 0.0 collective-permute-done.3.refs_3_
  41.9 4.7 %collective-permute-done.2.refs_2_ = f32[544,128]{1,0:T(8,128)S(1)} collective-permute-done((f32[544,128]{1,0:T(8,128)S(1)}, f32[544,128]{1,0:T(8,128)S(1)}, u32[]{:S(2)}, u32[]{:S(2)}) %collective-permute-start.2) | collective-permute-done | bytes 278560 | tf_op jit(solution)/shard_map/ppermute | solution.py:412
  46.5 1.3 %collective-permute-done.5.refs_4_ = f32[544,128]{1,0:T(8,128)S(1)} collective-permute-done((f32[544,128]{1,0:T(8,128)S(1)}, f32[544,128]{1,0:T(8,128)S(1)}, u32[]{:S(2)}, u32[]{:S(2)}) %collective-permute-start.5) | collective-permute-done | bytes 278560 | tf_op jit(solution)/shard_map/ppermute | solution.py:412
  47.8 4.7 %given_order_3.1 = (f32[136,128]{1,0:T(8,128)S(1)}, f32[136,128]{1,0:T(8,128)S(1)}, f32[136,128]{1,0:T(8,128)S(1)}) custom-call(s32[8]{0:T(128)S(1)} %stack.26.pos_ref.refs_0_, s32[128,128]{1,0:T(8,128)S(1)} %row_rank.1.refs_1_, f32[544,128]{1,0:T(8,128)S(1)} %collective-permute-done.2.refs_2_, f32[544,128]{1,0:T(8,128)S(1)} %collective-permute-done.3.refs_3_, ...), custom_call_target="tpu_custom_call" | custom-call | flops 1000000 | bytes 1000000 | tf_op jit(solution)/shard_map/given_order_3/pallas_call | solution.py:339
  52.5 3.0 %collective-permute-start.7 = (f32[136,128]{1,0:T(8,128)S(1)}, f32[136,128]{1,0:T(8,128)S(1)}, u32[]{:S(2)}, u32[]{:S(2)}) collective-permute-start(f32[136,128]{1,0:T(8,128)S(1)} %get-tuple-element.43), channel_id=1, source_target_pairs={{0,64},{1,65},{2,66},{3,67},{4,68},{5,69},{6,70},{7,71},{8,72},{9,... | collective-permute-start | bytes 208904 | tf_op jit(solution)/shard_map/ppermute | solution.py:412
  55.4 0.4 collective-permute-start.8
  55.9 2.3 %collective-permute-start.9 = (f32[136,128]{1,0:T(8,128)S(1)}, f32[136,128]{1,0:T(8,128)S(1)}, u32[]{:S(2)}, u32[]{:S(2)}) collective-permute-start(f32[136,128]{1,0:T(8,128)S(1)} %get-tuple-element.45), channel_id=1, source_target_pairs={{0,96},{1,97},{2,98},{3,99},{4,100},{5,101},{6,102},{7,103},{8,104... | collective-permute-start | bytes 208904 | tf_op jit(solution)/shard_map/ppermute | solution.py:412
  58.1 2.8 %given_order_1.1 = f32[136,128]{1,0:T(8,128)S(1)} custom-call(s32[8]{0:T(128)S(1)} %stack.26.pos_ref.refs_0_, s32[128,128]{1,0:T(8,128)S(1)} %row_rank.1.refs_1_, f32[544,128]{1,0:T(8,128)S(1)} %collective-permute-done.2.refs_2_, f32[544,128]{1,0:T(8,128)S(1)} %collective-permute-done.3.refs_3_, f32[544,128]{1,0:T(8,128)S(1)} %collective-permute-done.5.refs_4_, ...), custom_call_target="tpu_custom_call" | custom-call | flops 1000000 | bytes 1000000 | tf_op jit(solution)/shard_map/given_order_1/pallas_call | solution.py:339
  60.9 0.0 collective-permute-done.7
  60.9 0.0 collective-permute-done.8
  60.9 0.0 collective-permute-done.9
  61.0 2.5 %collective-permute-start.12 = (f32[136,128]{1,0:T(8,128)S(1)}, f32[136,128]{1,0:T(8,128)S(1)}, u32[]{:S(2)}, u32[]{:S(2)}) collective-permute-start(f32[136,128]{1,0:T(8,128)S(1)} %add_add_fusion.refs_2_), channel_id=1, source_target_pairs={{0,24},{1,25},{2,26},{3,27},{4,28},{5,29},{6,30},{7,31},{8,0},{9,1... | collective-permute-start | bytes 208904 | tf_op jit(solution)/shard_map/ppermute | solution.py:412
  63.5 0.0 collective-permute-start.11
  63.5 1.7 %collective-permute-start.10 = (f32[136,128]{1,0:T(8,128)S(1)}, f32[136,128]{1,0:T(8,128)S(1)}, u32[]{:S(2)}, u32[]{:S(2)}) collective-permute-start(f32[136,128]{1,0:T(8,128)S(1)} %add_add_fusion.refs_2_), channel_id=1, source_target_pairs={{0,16},{1,17},{2,18},{3,19},{4,20},{5,21},{6,22},{7,23},{8,24},{9,... | collective-permute-start | bytes 208904 | tf_op jit(solution)/shard_map/ppermute | solution.py:412
  65.2 0.0 collective-permute-done.12.refs_5_
  65.2 3.4 %collective-permute-done.11.refs_4_ = f32[136,128]{1,0:T(8,128)S(1)} collective-permute-done((f32[136,128]{1,0:T(8,128)S(1)}, f32[136,128]{1,0:T(8,128)S(1)}, u32[]{:S(2)}, u32[]{:S(2)}) %collective-permute-start.11) | collective-permute-done | bytes 69664 | tf_op jit(solution)/shard_map/ppermute | solution.py:412
  68.6 0.0 collective-permute-done.10.refs_3_
  68.6 0.0 copy-done.1
  68.6 1.6 %rows_and_gram.1 = (f32[17,256]{1,0:T(8,128)}, f32[16,8,128]{2,1,0:T(8,128)S(1)}) custom-call(s32[8]{0:T(128)S(1)} %stack.26.pos_ref.refs_0_, s32[16,2,8,128]{3,2,1,0:T(8,128)S(1)} %bitcast.16, f32[136,128]{1,0:T(8,128)S(1)} %add_add_fusion.refs_2_, f32[136,128]{1,0:T(8,128)S(1)} %collective-permute-done.10.refs_3_, ...), custom_call_target="tpu_custom_call" | custom-call | tf_op jit(solution)/shard_map/rows_and_gram/pallas_call | solution.py:379
  70.2 10.8 %all_to_all.5 = f32[16,8,128]{2,1,0:T(8,128)S(1)} all-to-all(f32[16,8,128]{2,1,0:T(8,128)S(1)} %get-tuple-element.47), channel_id=1, replica_groups={{0,1,2,3,32,33,34,35,64,65,66,67,96,97,98,99},{4,5,6,7,36,37,38,39,68,6..., dimensions={0} | all-to-all | bytes 131072 | tf_op jit(solution)/shard_map/all_to_all | solution.py:448
  81.0 5.4 %collective-permute-start.13 = (f32[8,128]{1,0:T(8,128)S(1)}, f32[8,128]{1,0:T(8,128)S(1)}, u32[]{:S(2)}, u32[]{:S(2)}) collective-permute-start(f32[8,128]{1,0:T(8,128)S(1)} %reduce_sum.9.a), channel_id=1, source_target_pairs={{0,4},{1,5},{2,6},{3,7},{4,0},{5,1},{6,2},{7,3},{8,12},{9,13},{10,... | collective-permute-start | bytes 12296 | tf_op jit(solution)/shard_map/ppermute | solution.py:412
  86.5 0.8 collective-permute-done.13.b
  87.3 0.7 own_gram.1
  (6 shorter events, 0.2 us)
Async XLA Ops:
  0.7 0.9 %copy-start = (s32[32768]{0:T(1024)S(1)}, s32[32768]{0:T(1024)}, u32[]{:S(2)}) copy-start(s32[32768]{0:T(1024)} %param.8) | copy-start | bytes 393220
  16.2 6.7 %collective-permute-start = (f32[544,128]{1,0:T(8,128)S(1)}, f32[544,128]{1,0:T(8,128)S(1)}, u32[]{:S(2)}, u32[]{:S(2)}) collective-permute-start(f32[544,128]{1,0:T(8,128)S(1)} %get-tuple-element.31), channel_id=1, source_target_pairs={{0,4},{1,5},{2,6},{3,7},{4,0},{5,1},{6,2},{7,3},{8,12},{9,13},{10,... | collective-permute-start | bytes 835592 | tf_op jit(solution)/shard_map/ppermute | solution.py:412
  22.9 5.7 %collective-permute-start.1 = (f32[544,128]{1,0:T(8,128)S(1)}, f32[544,128]{1,0:T(8,128)S(1)}, u32[]{:S(2)}, u32[]{:S(2)}) collective-permute-start(f32[544,128]{1,0:T(8,128)S(1)} %get-tuple-element.34), channel_id=1, source_target_pairs={{0,4},{1,5},{2,6},{3,7},{4,0},{5,1},{6,2},{7,3},{8,12},{9,13},{10,... | collective-permute-start | bytes 835592 | tf_op jit(solution)/shard_map/ppermute | solution.py:412
  28.0 11.4 %collective-permute-start.4 = (f32[544,128]{1,0:T(8,128)S(1)}, f32[544,128]{1,0:T(8,128)S(1)}, u32[]{:S(2)}, u32[]{:S(2)}) collective-permute-start(f32[544,128]{1,0:T(8,128)S(1)} %get-tuple-element.41), channel_id=1, source_target_pairs={{0,4},{1,5},{2,6},{3,7},{4,0},{5,1},{6,2},{7,3},{8,12},{9,13},{10,... | collective-permute-start | bytes 835592 | tf_op jit(solution)/shard_map/ppermute | solution.py:412
  28.6 40.0 %copy-start.1 = (s32[32768]{0:T(1024)S(1)}, s32[32768]{0:T(1024)}, u32[]{:S(2)}) copy-start(s32[32768]{0:T(1024)} %param.9) | copy-start | bytes 393220
  28.6 13.2 %collective-permute-start.3 = (f32[544,128]{1,0:T(8,128)S(1)}, f32[544,128]{1,0:T(8,128)S(1)}, u32[]{:S(2)}, u32[]{:S(2)}) collective-permute-start(f32[544,128]{1,0:T(8,128)S(1)} %add.26), channel_id=1, source_target_pairs={{0,1},{1,2},{2,3},{3,0},{4,5},{5,6},{6,7},{7,4},{8,9},{9,10},{10,1... | collective-permute-start | bytes 835592 | tf_op jit(solution)/shard_map/ppermute | solution.py:412
  30.3 16.2 %collective-permute-start.2 = (f32[544,128]{1,0:T(8,128)S(1)}, f32[544,128]{1,0:T(8,128)S(1)}, u32[]{:S(2)}, u32[]{:S(2)}) collective-permute-start(f32[544,128]{1,0:T(8,128)S(1)} %add.25), channel_id=1, source_target_pairs={{0,2},{1,3},{2,0},{3,1},{4,6},{5,7},{6,4},{7,5},{8,10},{9,11},{10,... | collective-permute-start | bytes 835592 | tf_op jit(solution)/shard_map/ppermute | solution.py:412
  38.8 3.0 %collective-permute-start.6 = (f32[544,128]{1,0:T(8,128)S(1)}, f32[544,128]{1,0:T(8,128)S(1)}, u32[]{:S(2)}, u32[]{:S(2)}) collective-permute-start(f32[544,128]{1,0:T(8,128)S(1)} %get-tuple-element.42), channel_id=1, source_target_pairs={{0,4},{1,5},{2,6},{3,7},{4,0},{5,1},{6,2},{7,3},{8,12},{9,13},{10,... | collective-permute-start | bytes 835592 | tf_op jit(solution)/shard_map/ppermute | solution.py:412
  39.5 8.3 %collective-permute-start.5 = (f32[544,128]{1,0:T(8,128)S(1)}, f32[544,128]{1,0:T(8,128)S(1)}, u32[]{:S(2)}, u32[]{:S(2)}) collective-permute-start(f32[544,128]{1,0:T(8,128)S(1)} %add.27), channel_id=1, source_target_pairs={{0,3},{1,0},{2,1},{3,2},{4,7},{5,4},{6,5},{7,6},{8,11},{9,8},{10,9... | collective-permute-start | bytes 835592 | tf_op jit(solution)/shard_map/ppermute | solution.py:412
  52.5 8.4 %collective-permute-start.7 = (f32[136,128]{1,0:T(8,128)S(1)}, f32[136,128]{1,0:T(8,128)S(1)}, u32[]{:S(2)}, u32[]{:S(2)}) collective-permute-start(f32[136,128]{1,0:T(8,128)S(1)} %get-tuple-element.43), channel_id=1, source_target_pairs={{0,64},{1,65},{2,66},{3,67},{4,68},{5,69},{6,70},{7,71},{8,72},{9,... | collective-permute-start | bytes 208904 | tf_op jit(solution)/shard_map/ppermute | solution.py:412
  55.4 5.5 %collective-permute-start.8 = (f32[136,128]{1,0:T(8,128)S(1)}, f32[136,128]{1,0:T(8,128)S(1)}, u32[]{:S(2)}, u32[]{:S(2)}) collective-permute-start(f32[136,128]{1,0:T(8,128)S(1)} %get-tuple-element.44), channel_id=1, source_target_pairs={{0,32},{1,33},{2,34},{3,35},{4,36},{5,37},{6,38},{7,39},{8,40},{9,... | collective-permute-start | bytes 208904 | tf_op jit(solution)/shard_map/ppermute | solution.py:412
  55.9 5.1 %collective-permute-start.9 = (f32[136,128]{1,0:T(8,128)S(1)}, f32[136,128]{1,0:T(8,128)S(1)}, u32[]{:S(2)}, u32[]{:S(2)}) collective-permute-start(f32[136,128]{1,0:T(8,128)S(1)} %get-tuple-element.45), channel_id=1, source_target_pairs={{0,96},{1,97},{2,98},{3,99},{4,100},{5,101},{6,102},{7,103},{8,104... | collective-permute-start | bytes 208904 | tf_op jit(solution)/shard_map/ppermute | solution.py:412
  61.0 4.3 %collective-permute-start.12 = (f32[136,128]{1,0:T(8,128)S(1)}, f32[136,128]{1,0:T(8,128)S(1)}, u32[]{:S(2)}, u32[]{:S(2)}) collective-permute-start(f32[136,128]{1,0:T(8,128)S(1)} %add_add_fusion.refs_2_), channel_id=1, source_target_pairs={{0,24},{1,25},{2,26},{3,27},{4,28},{5,29},{6,30},{7,31},{8,0},{9,1... | collective-permute-start | bytes 208904 | tf_op jit(solution)/shard_map/ppermute | solution.py:412
  63.5 5.1 %collective-permute-start.11 = (f32[136,128]{1,0:T(8,128)S(1)}, f32[136,128]{1,0:T(8,128)S(1)}, u32[]{:S(2)}, u32[]{:S(2)}) collective-permute-start(f32[136,128]{1,0:T(8,128)S(1)} %add_add_fusion.refs_2_), channel_id=1, source_target_pairs={{0,8},{1,9},{2,10},{3,11},{4,12},{5,13},{6,14},{7,15},{8,16},{9,17... | collective-permute-start | bytes 208904 | tf_op jit(solution)/shard_map/ppermute | solution.py:412
  63.5 5.1 %collective-permute-start.10 = (f32[136,128]{1,0:T(8,128)S(1)}, f32[136,128]{1,0:T(8,128)S(1)}, u32[]{:S(2)}, u32[]{:S(2)}) collective-permute-start(f32[136,128]{1,0:T(8,128)S(1)} %add_add_fusion.refs_2_), channel_id=1, source_target_pairs={{0,16},{1,17},{2,18},{3,19},{4,20},{5,21},{6,22},{7,23},{8,24},{9,... | collective-permute-start | bytes 208904 | tf_op jit(solution)/shard_map/ppermute | solution.py:412
  81.0 6.3 %collective-permute-start.13 = (f32[8,128]{1,0:T(8,128)S(1)}, f32[8,128]{1,0:T(8,128)S(1)}, u32[]{:S(2)}, u32[]{:S(2)}) collective-permute-start(f32[8,128]{1,0:T(8,128)S(1)} %reduce_sum.9.a), channel_id=1, source_target_pairs={{0,4},{1,5},{2,6},{3,7},{4,0},{5,1},{6,2},{7,3},{8,12},{9,13},{10,... | collective-permute-start | bytes 12296 | tf_op jit(solution)/shard_map/ppermute | solution.py:412

commit v4 on v3

--- a/solution.py
+++ b/solution.py
@@ -49,17 +49,17 @@
     return jnp.take_along_axis(tile, index, axis=1)
 
 
-def bitonic(v, sub, lane):
+def bitonic_steps(v, sub, lane):
     for k in range(1, 13):
         for b in (k - 1, k):
             if b == 0 or b == 12:
                 continue
             if b < 4:
-                v = [~t if (i >> b) & 1 else t for i, t in enumerate(v)]
+                v[:] = [~t if (i >> b) & 1 else t for i, t in enumerate(v)]
             else:
                 bit = (sub >> (b - 4)) if b < 7 else (lane >> (b - 7))
                 m = -(bit & 1)
-                v = [t ^ m for t in v]
+                v[:] = [t ^ m for t in v]
         for j in range(k - 1, -1, -1):
             if j < 4:
                 new = list(v)
@@ -68,7 +68,7 @@
                         a, b = v[i], v[i | (1 << j)]
                         new[i] = jnp.minimum(a, b)
                         new[i | (1 << j)] = jnp.maximum(a, b)
-                v = new
+                v[:] = new
             elif j < 7:
                 d = 1 << (j - 4)
                 up = (sub & d) != 0
@@ -77,7 +77,7 @@
                     prev = pltpu.roll(t, d, 0)
                     nxt = prev if d == 4 else pltpu.roll(t, 8 - d, 0)
                     new.append(jnp.where(up, jnp.maximum(t, prev), jnp.minimum(t, nxt)))
-                v = new
+                v[:] = new
             else:
                 d = 1 << (j - 7)
                 up = (lane & d) != 0
@@ -86,7 +86,13 @@
                 for t in v:
                     o = lane_take(t, other)
                     new.append(jnp.where(up, jnp.maximum(t, o), jnp.minimum(t, o)))
-                v = new
+                v[:] = new
+            yield
+
+
+def bitonic(v, sub, lane):
+    for _ in bitonic_steps(v, sub, lane):
+        pass
     return v
 
 
@@ -109,7 +115,7 @@
 
 def prepare_kernel(
     pos_ref, samples_ref, basis_hbm, target_hbm, bits_hbm, keys_ref, ends_ref, own_ref, tab, last,
-    basis_ref, target_ref, bits_ref, scratch, sems,
+    basis_ref, target_ref, bits_ref, scratch, walsh_ref, flip_ref, sems,
 ):
     copies = [
         pltpu.make_async_copy(src, dst, sems.at[n])
@@ -123,7 +129,7 @@
     me, core = pos_ref[0], pos_ref[1]
     sub = lax.broadcasted_iota(jnp.int32, (8, LANES), 0)
     lane = lax.broadcasted_iota(jnp.int32, (8, LANES), 1)
-    for c in range(2):
+    def load(c):
         v = []
         for i in range(16):
             s = samples_ref[i, c]
@@ -133,29 +139,27 @@
             odd = fold((s >> 16) & me)
             r = i * 256 + (sub & 1) * 128 + (sub >> 1) * 32 + (lane & 31)
             v.append((place << 13) | (r << 1) | odd)
-        v = bitonic(v, sub, lane)
+        return v
+
+    def store(c, v):
         for i in range(16):
             scratch[c, pl.ds(i, 8, stride=16), :] = v[i]
         ends_ref[2 * c : 2 * c + 1, :] = scratch[c, 0:1, :] >> 20
         ends_ref[2 * c + 1 : 2 * c + 2, :] = scratch[c, 127:128, :] >> 20
         keys_ref[c * LANES : (c + 1) * LANES, :] = scratch[c].T
-    own_ref[...] = scratch[core]
-
-    for copy in copies:
-        copy.wait()
-    a = lax.broadcasted_iota(jnp.int32, (SIDE, SIDE), 0)
-    b = lax.broadcasted_iota(jnp.int32, (SIDE, SIDE), 1)
-    walsh = (1 - 2 * fold(a & b)).astype(jnp.float32).astype(jnp.bfloat16)
-    flips = [(1 - 2 * bits_ref[pl.ds(bh, SIDE, stride=2), :]).astype(jnp.float32) for bh in range(2)]
-    flip = jnp.concatenate(flips, axis=1)
-    for k in range(COLS):
+
+    def flips_of(bh):
+        return (1 - 2 * bits_ref[pl.ds(bh, SIDE, stride=2), :]).astype(jnp.float32)
+
+    def mix(k):
         if k < 16:
             base = (k // 8) * 4096 + k % 8
             halves = [basis_ref[pl.ds(base + 8 * bh, SIDE, stride=16), :] for bh in range(2)]
         else:
             halves = [target_ref[pl.ds(bh, SIDE, stride=2), :] for bh in range(2)]
-        x = jnp.concatenate(halves, axis=1) * flip
+        x = jnp.concatenate(halves, axis=1) * flip_ref[...]
         hi, lo = split(x)
+        walsh = walsh_ref[...]
         y = dot(hi, walsh) + dot(lo, walsh)
         hi, lo = split(y)
         z = dot(walsh, hi) + dot(walsh, lo)
@@ -165,6 +169,23 @@
                 tab[pl.ds(bh * SIDE * 16 + k, SIDE, stride=16), :] = half
             else:
                 last[bh * SIDE : (bh + 1) * SIDE, :] = half
+
+    a = lax.broadcasted_iota(jnp.int32, (SIDE, SIDE), 0)
+    b = lax.broadcasted_iota(jnp.int32, (SIDE, SIDE), 1)
+    walsh_ref[...] = (1 - 2 * fold(a & b)).astype(jnp.float32).astype(jnp.bfloat16)
+    store(0, bitonic(load(0), sub, lane))
+    for copy in copies:
+        copy.wait()
+    flip_ref[...] = jnp.concatenate([flips_of(0), flips_of(1)], axis=1)
+    v = load(1)
+    todo = list(range(COLS))
+    for n, _ in enumerate(bitonic_steps(v, sub, lane)):
+        if n % 5 == 0 and todo:
+            mix(todo.pop(0))
+    while todo:
+        mix(todo.pop(0))
+    store(1, v)
+    own_ref[...] = scratch[core]
     tab[ROWS * 16 :, :] = jnp.zeros(((ROWS_PAD - ROWS) * 16, LANES), jnp.float32)
     last[ROWS:, :] = jnp.zeros((ROWS_PAD - ROWS, LANES), jnp.float32)
 
@@ -192,6 +213,8 @@
             pltpu.VMEM((512, LANES), jnp.float32),
             pltpu.VMEM((512, LANES), jnp.int32),
             pltpu.VMEM((2, LANES, LANES), jnp.int32),
+            pltpu.VMEM((SIDE, SIDE), jnp.bfloat16),
+            pltpu.VMEM((SIDE, SIDE), jnp.float32),
             pltpu.SemaphoreType.DMA((3,)),
         ],
         compiler_params=pltpu.CompilerParams(vmem_limit_bytes=24 * 2**20),
@@ -227,11 +250,11 @@
     )(own)
 
 
-def slots_kernel(scale, off, pos_ref, ends_ref, tab, last, keys_ref, keep, give):
+def slots_kernel(scale, off, cores, pos_ref, ends_ref, tab, last, keys_ref, *outs):
     core = pos_ref[1]
     z = (pos_ref[4] + off) & 3
     sub = lax.broadcasted_iota(jnp.int32, (8, LANES), 0)
-    for rel_core, out in enumerate((keep, give)):
+    for rel_core, out in zip(cores, outs):
         c = core ^ rel_core
 
         def group(it, _, c=c, out=out):
@@ -287,65 +310,65 @@
         lax.fori_loop(0, 8, group, 0)
 
 
-def slots_call(scale, off, pos, ends, tab, last, keys):
+def slots_call(scale, off, cores, pos, ends, tab, last, keys):
     part = jax.ShapeDtypeStruct((8 * 4 * COLS, LANES), jnp.float32)
     return pl.pallas_call(
-        lambda *refs: slots_kernel(scale, off, *refs),
-        out_shape=(part,) * 2,
+        lambda *refs: slots_kernel(scale, off, cores, *refs),
+        out_shape=(part,) * len(cores),
         in_specs=[SMEM, SMEM, VMEM, VMEM, VMEM],
-        out_specs=(VMEM,) * 2,
+        out_specs=(VMEM,) * len(cores),
         compiler_params=pltpu.CompilerParams(vmem_limit_bytes=12 * 2**20),
         cost_estimate=COST,
-        name=f"take_slots_{off}",
+        name=f"take_slots_{off}" + "".join(map(str, cores)),
     )(pos, ends, tab, last, keys)
 
 
-def order_kernel(rels, pos_ref, rank_ref, *refs):
-    parts, outs, table = refs[:4], refs[4:-1], refs[-1]
+def order_lines(rel, pos_ref, rank_ref, table, out, boxes):
     y, z = pos_ref[2], pos_ref[4]
-    table[...] = (parts[0][...] + parts[1][...]) + (parts[2][...] + parts[3][...])
     rows = 8 * COLS
     at = lax.broadcasted_iota(jnp.int32, (rows, LANES), 0)
-    code = (at // (4 * COLS)) * 4 + (at & 3)
-    ck = lax.broadcasted_iota(jnp.int32, (24, rows), 0)
-    cr = lax.broadcasted_iota(jnp.int32, (24, rows), 1)
-    collect = jnp.where((cr % (4 * COLS)) // 4 == ck, 1.0, 0.0).astype(jnp.bfloat16)
-
-    def step(i, _):
-        for rel, out in zip(rels, outs):
-            line = z * 32 + ((y + rel) & 3) * 8 + i
-            slot = jnp.broadcast_to(rank_ref[pl.ds(line, 1), :], (8, LANES))
-            index = slot & 127
-            pair = slot >> 10
-            acc = [jnp.zeros((8, LANES), jnp.float32)] * COLS
-            for n in range(4):
-                hit = pair == n
-                for t in range(COLS):
-                    tile = table[n * rows + 8 * t : n * rows + 8 * t + 8, :]
-                    acc[t] = jnp.where(hit, lane_take(tile, index), acc[t])
-            chosen = jnp.where(code == ((slot >> 7) & 7)[0:1], jnp.concatenate(acc, axis=0), 0.0)
-            hi, lo = split(chosen)
-            values = dot(collect, hi) + dot(collect, lo)
-            for t in range(2):
-                out[pl.ds(i + 64 * t, 8, stride=8), :] = values[8 * t : 8 * t + 8]
-            out[pl.ds(i + 128, 1), :] = values[16:17]
-        return 0
-
-    lax.fori_loop(0, 8, step, 0)
-
-
-def order_call(rels, pos, rank, parts):
+    code = jnp.where(at >= rows // 2, 4, 0) + (at & 3)
+    for i in range(8):
+        line = z * 32 + ((y + rel) & 3) * 8 + i
+        slot = jnp.broadcast_to(rank_ref[pl.ds(line, 1), :], (8, LANES))
+        index = slot & 127
+        pair = slot >> 10
+        acc = [jnp.zeros((8, LANES), jnp.float32)] * COLS
+        for n in range(4):
+            hit = pair == n
+            for t in range(COLS):
+                tile = table[n * rows + 8 * t : n * rows + 8 * t + 8, :]
+                acc[t] = jnp.where(hit, lane_take(tile, index), acc[t])
+        boxes[i] = jnp.where(code == ((slot >> 7) & 7)[0:1], jnp.concatenate(acc, axis=0), 0.0)
+        starts = [half * (rows // 2) + q for half in range(2) for q in range(4)]
+        values = sum(boxes[i, pl.ds(first, 16, stride=4), :] for first in starts)
+        for t in range(2):
+            out[pl.ds(i + 64 * t, 8, stride=8), :] = values[8 * t : 8 * t + 8]
+        out[128 + i : 129 + i, :] = sum(boxes[i, first + 64 : first + 65, :] for first in starts)
+
+
+def order_first_kernel(rels, pos_ref, rank_ref, p0, p1, p2, p3, table, *refs):
+    table[...] = (p0[...] + p1[...]) + (p2[...] + p3[...])
+    for rel, out in zip(rels, refs):
+        order_lines(rel, pos_ref, rank_ref, table, out, refs[-1])
+
+
+def order_call(rel, pos, rank, *given):
     rows = 8 * COLS
+    out = jax.ShapeDtypeStruct((rows, LANES), jnp.float32)
+    table = jax.ShapeDtypeStruct((4 * rows, LANES), jnp.float32)
+    first = len(given) > 1
+    kernel = order_first_kernel if first else order_lines
     return pl.pallas_call(
-        lambda *refs: order_kernel(rels, *refs),
-        out_shape=(jax.ShapeDtypeStruct((rows, LANES), jnp.float32),) * len(rels),
-        in_specs=[SMEM] + [VMEM] * 5,
-        out_specs=(VMEM,) * len(rels),
-        scratch_shapes=[pltpu.VMEM((4 * rows, LANES), jnp.float32)],
+        lambda *refs: kernel(rel, *refs),
+        out_shape=(table,) + (out,) * len(rel) if first else out,
+        in_specs=[SMEM] + [VMEM] * (1 + len(given)),
+        out_specs=(VMEM,) * (1 + len(rel)) if first else VMEM,
+        scratch_shapes=[pltpu.VMEM((8, rows, LANES), jnp.float32)],
         compiler_params=pltpu.CompilerParams(vmem_limit_bytes=8 * 2**20),
         cost_estimate=COST,
-        name=f"given_order_{len(rels)}",
-    )(pos, rank, *parts)
+        name="given_order_far" if first else "given_order_own",
+    )(pos, rank, *given)
 
 
 def finish_kernel(factor, pos_ref, owners_ref, p0, p1, p2, p3, sketch, gram, table):
@@ -429,20 +452,37 @@
     far = [tiles, target.reshape(512, LANES), sign_bits.reshape(512, LANES)]
     far = [pltpu.with_memory_space_constraint(v, pltpu.HBM) for v in far]
     keys, ends, own, tab, last = prepare_call(pos, samples.reshape(16, 2, 8, LANES), *far)
-    parts, held = [], []
-    for n, off in enumerate((2, 1, 3, 0)):
-        if n >= 2:
-            keys, held[n - 2] = lax.optimization_barrier((keys, held[n - 2]))
-        keep, give = slots_call(scale, off, pos, ends, tab, last, keys)
-        held.append(keep + send(give, "c", 1))
-        if n >= 2:
-            parts.append(send(held[n - 2], "z", (2, 1)[n - 2]))
-    own, keep = lax.optimization_barrier((own, keep))
-    rank = rank_call(own)
-    parts += [send(held[2], "z", 3), held[3]]
-    lines = order_call((2, 1, 3), pos, rank, parts)
-    line = order_call((0,), pos, rank, parts)[0]
-    line = (line + send(lines[0], "y", 2)) + (send(lines[1], "y", 1) + send(lines[2], "y", 3))
+    def after(v, *others):
+        return lax.optimization_barrier((v,) + others)[0]
+
+    def take(off, *cores):
+        return slots_call(scale, off, cores, pos, ends, tab, last, keys)
+
+    keep2, give2 = take(2, 0, 1)
+    got2 = send(give2, "c", 1)
+    give1, = take(1, 1)
+    got1 = send(give1, "c", 1)
+    both2 = keep2 + got2
+    keys = after(keys, give1, both2)
+    keep1, = take(1, 0)
+    both1 = keep1 + got1
+    keys = after(keys, both1)
+    give3, = take(3, 1)
+    got3 = send(give3, "c", 1)
+    part2 = send(both2, "z", 2)
+    keys = after(keys, give3, part2)
+    keep3, = take(3, 0)
+    both3 = keep3 + got3
+    part1 = send(both1, "z", 1)
+    part3 = send(both3, "z", 3)
+    keys = after(keys, both3)
+    keep, give = take(0, 0, 1)
+    rank = rank_call(after(own, keep, part1, part3))
+    parts = [part2, part1, part3, keep + send(give, "c", 1)]
+    rels = (2, 1, 3)
+    table, *lines = order_call(rels, pos, rank, *parts)
+    got = [send(line, "y", rel) for line, rel in zip(lines, rels)]
+    line = (order_call(0, pos, rank, table) + got[0]) + (got[1] + got[2])
     around = [line] + [send(line, "x", off) for off in (2, 1, 3)]
     sketch, gram = finish_call(GROUPS / total_samples, pos, owners.reshape(16, 2, 8, LANES), around)
     gram = lax.all_to_all(gram, AXES, 0, 0, tiled=True, axis_index_groups=planes())

time: 88.4 us -> 83 us (0.939)
  waiting for transfers between devices: 10.2 us -> 4.65 us
  Pallas kernels: 41.2 us -> 37.6 us
  starting transfers between devices: 24 us -> 26.6 us
  blocking collectives: 10.8 us -> 12.2 us
    ppermute x14, waiting for transfers between devices: 10.2 us -> 4.65 us  [send(): return lax.ppermute(v, AXES, shift(axis, off))]
    ppermute x14, starting transfers between devices: 24 us -> 26.6 us  [send(): return lax.ppermute(v, AXES, shift(axis, off))]
    pallas_call x6 -> x8, Pallas kernels: 27.7 us -> 25.8 us  [the longest x6 21.9 us: slots_call(): pl.pallas_call(lambda *refs: slots_kernel(scale, off, cores, *refs), out_...]
    pallas_call x1, Pallas kernels: 9.46 us -> 7.74 us  [prepare_call(): pl.pallas_call(prepare_kernel, out_shape=(jax.ShapeDtypeStruct((256, LANE...]
    all_to_all x1, blocking collectives: 10.8 us -> 12.2 us  [shards(): lax.all_to_all(gram, AXES, 0, 0, tiled=True, axis_index_groups=planes())]
  transfers between devices with their start and end apart: 14 -> 14, of which waited for: 4 -> 3; matrix products, arithmetic and copies ran while one was open for 0% -> 0% of each run, Pallas kernels for 22% -> 24%
where the time goes in v4:
time: 83 us; the launch traced here: 83.1 us
  Pallas kernels  37.6 us (45%)
  starting transfers between devices  26.6 us (32%)
  blocking collectives  12.2 us (15%)
  waiting for transfers between devices  4.65 us (6%)
  local copies, waits for them, and re-layouts  1 us (1%)
    ppermute x14, starting transfers between devices, send(): return lax.ppermute(v, AXES, shift(axis, off))  26.6 us
    pallas_call x6, Pallas kernels, slots_call(): pl.pallas_call(lambda *refs: slots_kernel(scale, off, cores, *refs), out_...  21.9 us
    all_to_all x1, blocking collectives, shards(): lax.all_to_all(gram, AXES, 0, 0, tiled=True, axis_index_groups=planes())  12.2 us
    pallas_call x1, Pallas kernels, prepare_call(): pl.pallas_call(prepare_kernel, out_shape=(jax.ShapeDtypeStruct((256, LANE...  7.74 us
    ppermute x14, waiting for transfers between devices, send(): return lax.ppermute(v, AXES, shift(axis, off))  4.65 us
    pallas_call x2, Pallas kernels, order_call(): pl.pallas_call(lambda *refs: kernel(rel, *refs), out_shape=(table,) + (ou...  3.89 us
    pallas_call x1, Pallas kernels, rank_call(): pl.pallas_call(rank_kernel, out_shape=jax.ShapeDtypeStruct((LANES, LANES)...  1.66 us
  transfers between devices with their start and end apart: 14, of which 3 were waited for; matrix products, arithmetic and copies ran while one was open for 0% of the time, Pallas kernels for 24%

profile of v4, /device:TPU:1, one launch (start us, length us, event | category | flops | bytes accessed | tf_op | source)
XLA Modules:
  0.0 83.1 jit_solution(16560077351973480222)
XLA Ops:
  0.6 0.1 stack.26.pos_ref.refs_0_
  0.7 0.0 copy-start
  0.7 0.9 %copy-done = s32[32768]{0:T(1024)S(1)} copy-done((s32[32768]{0:T(1024)S(1)}, s32[32768]{0:T(1024)}, u32[]{:S(2)}) %copy-start) | copy-done | bytes 131096
  1.6 7.7 %sort_and_walsh.1 = (s32[256,128]{1,0:T(8,128)S(1)}, s32[4,128]{1,0:T(4,128)S(1)}, s32[128,128]{1,0:T(8,128)S(1)}, f32[8576,128]{1,0:T(8,128)S(1)}, f32[536,128]{1,0:T(8,128)S(1)}) custom-call(s32[8]{0:T(128)S(1)} %stack.26.pos_ref.refs_0_, s32[16,2,8,128]{3,2,1,0:T(8,128)S(1)} %bitcast.15, f32[8192,128]{1,0:T(8,128)} %bitcast.17, f32[512,128]{1,0:T(8,128)} %bitcast.18, ...), custom_call_target="tpu_custom_call" | custom-call | flops 1000000 | bytes 1000000 | tf_op jit(solution)/shard_map/sort_and_walsh/pallas_call | solution.py:200
  9.4 5.3 %take_slots_201.1 = (f32[544,128]{1,0:T(8,128)S(1)}, f32[544,128]{1,0:T(8,128)S(1)}) custom-call(s32[8]{0:T(128)S(1)} %stack.26.pos_ref.refs_0_, s32[4,128]{1,0:T(4,128)S(1)} %get-tuple-element.23.refs_1_, f32[8576,128]{1,0:T(8,128)S(1)} %get-tuple-element.24.refs_2_, f32[536,128]{1,0:T(8,128)S(1)} %get-tuple-element.25.refs_3_, ...), custom_call_target="tpu_custom_call" | custom-call | flops 1000000 | bytes 1000000 | tf_op jit(solution)/shard_map/take_slots_201/pallas_call | solution.py:315
  14.7 1.5 %collective-permute-start = (f32[544,128]{1,0:T(8,128)S(1)}, f32[544,128]{1,0:T(8,128)S(1)}, u32[]{:S(2)}, u32[]{:S(2)}) collective-permute-start(f32[544,128]{1,0:T(8,128)S(1)} %get-tuple-element.28), channel_id=1, source_target_pairs={{0,4},{1,5},{2,6},{3,7},{4,0},{5,1},{6,2},{7,3},{8,12},{9,13},{10,... | collective-permute-start | bytes 835592 | tf_op jit(solution)/shard_map/ppermute | solution.py:435
  16.2 2.8 %take_slots_11.1 = f32[544,128]{1,0:T(8,128)S(1)} custom-call(s32[8]{0:T(128)S(1)} %stack.26.pos_ref.refs_0_, s32[4,128]{1,0:T(4,128)S(1)} %get-tuple-element.23.refs_1_, f32[8576,128]{1,0:T(8,128)S(1)} %get-tuple-element.24.refs_2_, f32[536,128]{1,0:T(8,128)S(1)} %get-tuple-element.25.refs_3_, s32[256,128]{1,0:T(8,128)S(1)} %get-tuple-element.32.refs_4_), custom_call_target="tpu_custom_call" | custom-call | flops 1000000 | bytes 1000000 | tf_op jit(solution)/shard_map/take_slots_11/pallas_call | solution.py:315
  19.0 0.2 collective-permute-start.1
  19.2 0.0 collective-permute-done
  19.2 3.8 %collective-permute-start.2 = (f32[544,128]{1,0:T(8,128)S(1)}, f32[544,128]{1,0:T(8,128)S(1)}, u32[]{:S(2)}, u32[]{:S(2)}) collective-permute-start(f32[544,128]{1,0:T(8,128)S(1)} %add.25), channel_id=1, source_target_pairs={{0,2},{1,3},{2,0},{3,1},{4,6},{5,7},{6,4},{7,5},{8,10},{9,11},{10,... | collective-permute-start | bytes 835592 | tf_op jit(solution)/shard_map/ppermute | solution.py:435
  23.0 2.9 %take_slots_10.1 = f32[544,128]{1,0:T(8,128)S(1)} custom-call(s32[8]{0:T(128)S(1)} %stack.26.pos_ref.refs_0_, s32[4,128]{1,0:T(4,128)S(1)} %get-tuple-element.23.refs_1_, f32[8576,128]{1,0:T(8,128)S(1)} %get-tuple-element.24.refs_2_, f32[536,128]{1,0:T(8,128)S(1)} %get-tuple-element.25.refs_3_, s32[256,128]{1,0:T(8,128)S(1)} %get-tuple-element.32.refs_4_), custom_call_target="tpu_custom_call" | custom-call | flops 1000000 | bytes 1000000 | tf_op jit(solution)/shard_map/take_slots_10/pallas_call | solution.py:315
  25.9 0.0 collective-permute-done.1
  26.0 3.1 %take_slots_31.1 = f32[544,128]{1,0:T(8,128)S(1)} custom-call(s32[8]{0:T(128)S(1)} %stack.26.pos_ref.refs_0_, s32[4,128]{1,0:T(4,128)S(1)} %get-tuple-element.23.refs_1_, f32[8576,128]{1,0:T(8,128)S(1)} %get-tuple-element.24.refs_2_, f32[536,128]{1,0:T(8,128)S(1)} %get-tuple-element.25.refs_3_, s32[256,128]{1,0:T(8,128)S(1)} %get-tuple-element.32.refs_4_), custom_call_target="tpu_custom_call" | custom-call | flops 1000000 | bytes 1000000 | tf_op jit(solution)/shard_map/take_slots_31/pallas_call | solution.py:315
  29.0 0.5 collective-permute-start.3
  29.5 0.6 collective-permute-start.4
  30.1 0.0 collective-permute-done.2.refs_2_
  30.1 2.8 %take_slots_30.1 = f32[544,128]{1,0:T(8,128)S(1)} custom-call(s32[8]{0:T(128)S(1)} %stack.26.pos_ref.refs_0_, s32[4,128]{1,0:T(4,128)S(1)} %get-tuple-element.23.refs_1_, f32[8576,128]{1,0:T(8,128)S(1)} %get-tuple-element.24.refs_2_, f32[536,128]{1,0:T(8,128)S(1)} %get-tuple-element.25.refs_3_, s32[256,128]{1,0:T(8,128)S(1)} %get-tuple-element.32.refs_4_), custom_call_target="tpu_custom_call" | custom-call | flops 1000000 | bytes 1000000 | tf_op jit(solution)/shard_map/take_slots_30/pallas_call | solution.py:315
  32.9 0.0 copy-start.1
  32.9 0.0 collective-permute-done.3
  32.9 2.5 %collective-permute-start.5 = (f32[544,128]{1,0:T(8,128)S(1)}, f32[544,128]{1,0:T(8,128)S(1)}, u32[]{:S(2)}, u32[]{:S(2)}) collective-permute-start(f32[544,128]{1,0:T(8,128)S(1)} %add.27), channel_id=1, source_target_pairs={{0,3},{1,0},{2,1},{3,2},{4,7},{5,4},{6,5},{7,6},{8,11},{9,8},{10,9... | collective-permute-start | bytes 835592 | tf_op jit(solution)/shard_map/ppermute | solution.py:435
  35.4 5.1 %take_slots_001.1 = (f32[544,128]{1,0:T(8,128)S(1)}, f32[544,128]{1,0:T(8,128)S(1)}) custom-call(s32[8]{0:T(128)S(1)} %stack.26.pos_ref.refs_0_, s32[4,128]{1,0:T(4,128)S(1)} %get-tuple-element.23.refs_1_, f32[8576,128]{1,0:T(8,128)S(1)} %get-tuple-element.24.refs_2_, f32[536,128]{1,0:T(8,128)S(1)} %get-tuple-element.25.refs_3_, ...), custom_call_target="tpu_custom_call" | custom-call | flops 1000000 | bytes 1000000 | tf_op jit(solution)/shard_map/take_slots_001/pallas_call | solution.py:315
  40.6 1.6 %collective-permute-start.6 = (f32[544,128]{1,0:T(8,128)S(1)}, f32[544,128]{1,0:T(8,128)S(1)}, u32[]{:S(2)}, u32[]{:S(2)}) collective-permute-start(f32[544,128]{1,0:T(8,128)S(1)} %get-tuple-element.35), channel_id=1, source_target_pairs={{0,4},{1,5},{2,6},{3,7},{4,0},{5,1},{6,2},{7,3},{8,12},{9,13},{10,... | collective-permute-start | bytes 835592 | tf_op jit(solution)/shard_map/ppermute | solution.py:435
  42.2 0.0 collective-permute-done.4.refs_3_
  42.2 0.0 collective-permute-done.5.refs_4_
  42.2 1.7 %row_rank.1.refs_1_ = s32[128,128]{1,0:T(8,128)S(1)} custom-call(s32[128,128]{1,0:T(8,128)S(1)} %get-tuple-element.34.own_ref), custom_call_target="tpu_custom_call" | custom-call | flops 1000000 | bytes 1000000 | tf_op jit(solution)/shard_map/row_rank/pallas_call | solution.py:241
  43.9 0.0 collective-permute-done.6
  43.9 2.6 %given_order_far.1 = (f32[544,128]{1,0:T(8,128)S(1)}, f32[136,128]{1,0:T(8,128)S(1)}, f32[136,128]{1,0:T(8,128)S(1)}, f32[136,128]{1,0:T(8,128)S(1)}) custom-call(s32[8]{0:T(128)S(1)} %stack.26.pos_ref.refs_0_, s32[128,128]{1,0:T(8,128)S(1)} %row_rank.1.refs_1_, f32[544,128]{1,0:T(8,128)S(1)} %collective-permute-done.2.refs_2_, ...), custom_call_target="tpu_custom_call" | custom-call | flops 1000000 | bytes 1000000 | tf_op jit(solution)/shard_map/given_order_far/pallas_call | solution.py:362
  46.6 3.0 %collective-permute-start.7 = (f32[136,128]{1,0:T(8,128)S(1)}, f32[136,128]{1,0:T(8,128)S(1)}, u32[]{:S(2)}, u32[]{:S(2)}) collective-permute-start(f32[136,128]{1,0:T(8,128)S(1)} %get-tuple-element.37), channel_id=1, source_target_pairs={{0,64},{1,65},{2,66},{3,67},{4,68},{5,69},{6,70},{7,71},{8,72},{9,... | collective-permute-start | bytes 208904 | tf_op jit(solution)/shard_map/ppermute | solution.py:435
  49.6 0.4 collective-permute-start.8
  50.0 2.3 %collective-permute-start.9 = (f32[136,128]{1,0:T(8,128)S(1)}, f32[136,128]{1,0:T(8,128)S(1)}, u32[]{:S(2)}, u32[]{:S(2)}) collective-permute-start(f32[136,128]{1,0:T(8,128)S(1)} %get-tuple-element.39), channel_id=1, source_target_pairs={{0,96},{1,97},{2,98},{3,99},{4,100},{5,101},{6,102},{7,103},{8,104... | collective-permute-start | bytes 208904 | tf_op jit(solution)/shard_map/ppermute | solution.py:435
  52.2 1.3 %given_order_own.1 = f32[136,128]{1,0:T(8,128)S(1)} custom-call(s32[8]{0:T(128)S(1)} %stack.26.pos_ref.refs_0_, s32[128,128]{1,0:T(8,128)S(1)} %row_rank.1.refs_1_, f32[544,128]{1,0:T(8,128)S(1)} %get-tuple-element.36.refs_2_), custom_call_target="tpu_custom_call" | custom-call | flops 1000000 | bytes 1000000 | tf_op jit(solution)/shard_map/given_order_own/pallas_call | solution.py:362
  53.5 0.0 collective-permute-done.7
  53.5 0.4 collective-permute-done.8
  53.9 0.0 collective-permute-done.9
  54.0 2.5 %collective-permute-start.12 = (f32[136,128]{1,0:T(8,128)S(1)}, f32[136,128]{1,0:T(8,128)S(1)}, u32[]{:S(2)}, u32[]{:S(2)}) collective-permute-start(f32[136,128]{1,0:T(8,128)S(1)} %add_add_fusion.refs_2_), channel_id=1, source_target_pairs={{0,24},{1,25},{2,26},{3,27},{4,28},{5,29},{6,30},{7,31},{8,0},{9,1... | collective-permute-start | bytes 208904 | tf_op jit(solution)/shard_map/ppermute | solution.py:435
  56.5 0.0 collective-permute-start.11
  56.5 1.7 %collective-permute-start.10 = (f32[136,128]{1,0:T(8,128)S(1)}, f32[136,128]{1,0:T(8,128)S(1)}, u32[]{:S(2)}, u32[]{:S(2)}) collective-permute-start(f32[136,128]{1,0:T(8,128)S(1)} %add_add_fusion.refs_2_), channel_id=1, source_target_pairs={{0,16},{1,17},{2,18},{3,19},{4,20},{5,21},{6,22},{7,23},{8,24},{9,... | collective-permute-start | bytes 208904 | tf_op jit(solution)/shard_map/ppermute | solution.py:435
  58.2 0.0 collective-permute-done.12.refs_5_
  58.2 3.4 %collective-permute-done.11.refs_4_ = f32[136,128]{1,0:T(8,128)S(1)} collective-permute-done((f32[136,128]{1,0:T(8,128)S(1)}, f32[136,128]{1,0:T(8,128)S(1)}, u32[]{:S(2)}, u32[]{:S(2)}) %collective-permute-start.11) | collective-permute-done | bytes 69664 | tf_op jit(solution)/shard_map/ppermute | solution.py:435
  61.6 0.0 collective-permute-done.10.refs_3_
  61.6 0.0 copy-done.1
  61.6 1.6 %rows_and_gram.1 = (f32[17,256]{1,0:T(8,128)}, f32[16,8,128]{2,1,0:T(8,128)S(1)}) custom-call(s32[8]{0:T(128)S(1)} %stack.26.pos_ref.refs_0_, s32[16,2,8,128]{3,2,1,0:T(8,128)S(1)} %bitcast.16, f32[136,128]{1,0:T(8,128)S(1)} %add_add_fusion.refs_2_, f32[136,128]{1,0:T(8,128)S(1)} %collective-permute-done.10.refs_3_, ...), custom_call_target="tpu_custom_call" | custom-call | tf_op jit(solution)/shard_map/rows_and_gram/pallas_call | solution.py:402
  63.3 12.2 %all_to_all.5 = f32[16,8,128]{2,1,0:T(8,128)S(1)} all-to-all(f32[16,8,128]{2,1,0:T(8,128)S(1)} %get-tuple-element.41), channel_id=1, replica_groups={{0,1,2,3,32,33,34,35,64,65,66,67,96,97,98,99},{4,5,6,7,36,37,38,39,68,6..., dimensions={0} | all-to-all | bytes 131072 | tf_op jit(solution)/shard_map/all_to_all | solution.py:488
  75.5 6.0 %collective-permute-start.13 = (f32[8,128]{1,0:T(8,128)S(1)}, f32[8,128]{1,0:T(8,128)S(1)}, u32[]{:S(2)}, u32[]{:S(2)}) collective-permute-start(f32[8,128]{1,0:T(8,128)S(1)} %reduce_sum.9.a), channel_id=1, source_target_pairs={{0,4},{1,5},{2,6},{3,7},{4,0},{5,1},{6,2},{7,3},{8,12},{9,13},{10,... | collective-permute-start | bytes 12296 | tf_op jit(solution)/shard_map/ppermute | solution.py:435
  81.5 0.8 collective-permute-done.13.b
  82.3 0.7 own_gram.1
  (6 shorter events, 0.2 us)
Async XLA Ops:
  0.7 0.9 %copy-start = (s32[32768]{0:T(1024)S(1)}, s32[32768]{0:T(1024)}, u32[]{:S(2)}) copy-start(s32[32768]{0:T(1024)} %param.8) | copy-start | bytes 393220
  14.7 4.5 %collective-permute-start = (f32[544,128]{1,0:T(8,128)S(1)}, f32[544,128]{1,0:T(8,128)S(1)}, u32[]{:S(2)}, u32[]{:S(2)}) collective-permute-start(f32[544,128]{1,0:T(8,128)S(1)} %get-tuple-element.28), channel_id=1, source_target_pairs={{0,4},{1,5},{2,6},{3,7},{4,0},{5,1},{6,2},{7,3},{8,12},{9,13},{10,... | collective-permute-start | bytes 835592 | tf_op jit(solution)/shard_map/ppermute | solution.py:435
  19.0 7.0 %collective-permute-start.1 = (f32[544,128]{1,0:T(8,128)S(1)}, f32[544,128]{1,0:T(8,128)S(1)}, u32[]{:S(2)}, u32[]{:S(2)}) collective-permute-start(f32[544,128]{1,0:T(8,128)S(1)} %take_slots_11.1), channel_id=1, source_target_pairs={{0,4},{1,5},{2,6},{3,7},{4,0},{5,1},{6,2},{7,3},{8,12},{9,13},{10,... | collective-permute-start | bytes 835592 | tf_op jit(solution)/shard_map/ppermute | solution.py:435
  19.2 10.9 %collective-permute-start.2 = (f32[544,128]{1,0:T(8,128)S(1)}, f32[544,128]{1,0:T(8,128)S(1)}, u32[]{:S(2)}, u32[]{:S(2)}) collective-permute-start(f32[544,128]{1,0:T(8,128)S(1)} %add.25), channel_id=1, source_target_pairs={{0,2},{1,3},{2,0},{3,1},{4,6},{5,7},{6,4},{7,5},{8,10},{9,11},{10,... | collective-permute-start | bytes 835592 | tf_op jit(solution)/shard_map/ppermute | solution.py:435
  29.0 3.9 %collective-permute-start.3 = (f32[544,128]{1,0:T(8,128)S(1)}, f32[544,128]{1,0:T(8,128)S(1)}, u32[]{:S(2)}, u32[]{:S(2)}) collective-permute-start(f32[544,128]{1,0:T(8,128)S(1)} %take_slots_31.1), channel_id=1, source_target_pairs={{0,4},{1,5},{2,6},{3,7},{4,0},{5,1},{6,2},{7,3},{8,12},{9,13},{10,... | collective-permute-start | bytes 835592 | tf_op jit(solution)/shard_map/ppermute | solution.py:435
  29.5 12.7 %collective-permute-start.4 = (f32[544,128]{1,0:T(8,128)S(1)}, f32[544,128]{1,0:T(8,128)S(1)}, u32[]{:S(2)}, u32[]{:S(2)}) collective-permute-start(f32[544,128]{1,0:T(8,128)S(1)} %add.26), channel_id=1, source_target_pairs={{0,1},{1,2},{2,3},{3,0},{4,5},{5,6},{6,7},{7,4},{8,9},{9,10},{10,1... | collective-permute-start | bytes 835592 | tf_op jit(solution)/shard_map/ppermute | solution.py:435
  32.9 28.8 %copy-start.1 = (s32[32768]{0:T(1024)S(1)}, s32[32768]{0:T(1024)}, u32[]{:S(2)}) copy-start(s32[32768]{0:T(1024)} %param.9) | copy-start | bytes 393220
  32.9 9.3 %collective-permute-start.5 = (f32[544,128]{1,0:T(8,128)S(1)}, f32[544,128]{1,0:T(8,128)S(1)}, u32[]{:S(2)}, u32[]{:S(2)}) collective-permute-start(f32[544,128]{1,0:T(8,128)S(1)} %add.27), channel_id=1, source_target_pairs={{0,3},{1,0},{2,1},{3,2},{4,7},{5,4},{6,5},{7,6},{8,11},{9,8},{10,9... | collective-permute-start | bytes 835592 | tf_op jit(solution)/shard_map/ppermute | solution.py:435
  40.6 3.3 %collective-permute-start.6 = (f32[544,128]{1,0:T(8,128)S(1)}, f32[544,128]{1,0:T(8,128)S(1)}, u32[]{:S(2)}, u32[]{:S(2)}) collective-permute-start(f32[544,128]{1,0:T(8,128)S(1)} %get-tuple-element.35), channel_id=1, source_target_pairs={{0,4},{1,5},{2,6},{3,7},{4,0},{5,1},{6,2},{7,3},{8,12},{9,13},{10,... | collective-permute-start | bytes 835592 | tf_op jit(solution)/shard_map/ppermute | solution.py:435
  46.6 7.0 %collective-permute-start.7 = (f32[136,128]{1,0:T(8,128)S(1)}, f32[136,128]{1,0:T(8,128)S(1)}, u32[]{:S(2)}, u32[]{:S(2)}) collective-permute-start(f32[136,128]{1,0:T(8,128)S(1)} %get-tuple-element.37), channel_id=1, source_target_pairs={{0,64},{1,65},{2,66},{3,67},{4,68},{5,69},{6,70},{7,71},{8,72},{9,... | collective-permute-start | bytes 208904 | tf_op jit(solution)/shard_map/ppermute | solution.py:435
  49.6 4.4 %collective-permute-start.8 = (f32[136,128]{1,0:T(8,128)S(1)}, f32[136,128]{1,0:T(8,128)S(1)}, u32[]{:S(2)}, u32[]{:S(2)}) collective-permute-start(f32[136,128]{1,0:T(8,128)S(1)} %get-tuple-element.38), channel_id=1, source_target_pairs={{0,32},{1,33},{2,34},{3,35},{4,36},{5,37},{6,38},{7,39},{8,40},{9,... | collective-permute-start | bytes 208904 | tf_op jit(solution)/shard_map/ppermute | solution.py:435
  50.0 4.0 %collective-permute-start.9 = (f32[136,128]{1,0:T(8,128)S(1)}, f32[136,128]{1,0:T(8,128)S(1)}, u32[]{:S(2)}, u32[]{:S(2)}) collective-permute-start(f32[136,128]{1,0:T(8,128)S(1)} %get-tuple-element.39), channel_id=1, source_target_pairs={{0,96},{1,97},{2,98},{3,99},{4,100},{5,101},{6,102},{7,103},{8,104... | collective-permute-start | bytes 208904 | tf_op jit(solution)/shard_map/ppermute | solution.py:435
  54.0 4.3 %collective-permute-start.12 = (f32[136,128]{1,0:T(8,128)S(1)}, f32[136,128]{1,0:T(8,128)S(1)}, u32[]{:S(2)}, u32[]{:S(2)}) collective-permute-start(f32[136,128]{1,0:T(8,128)S(1)} %add_add_fusion.refs_2_), channel_id=1, source_target_pairs={{0,24},{1,25},{2,26},{3,27},{4,28},{5,29},{6,30},{7,31},{8,0},{9,1... | collective-permute-start | bytes 208904 | tf_op jit(solution)/shard_map/ppermute | solution.py:435
  56.5 5.1 %collective-permute-start.11 = (f32[136,128]{1,0:T(8,128)S(1)}, f32[136,128]{1,0:T(8,128)S(1)}, u32[]{:S(2)}, u32[]{:S(2)}) collective-permute-start(f32[136,128]{1,0:T(8,128)S(1)} %add_add_fusion.refs_2_), channel_id=1, source_target_pairs={{0,8},{1,9},{2,10},{3,11},{4,12},{5,13},{6,14},{7,15},{8,16},{9,17... | collective-permute-start | bytes 208904 | tf_op jit(solution)/shard_map/ppermute | solution.py:435
  56.5 5.1 %collective-permute-start.10 = (f32[136,128]{1,0:T(8,128)S(1)}, f32[136,128]{1,0:T(8,128)S(1)}, u32[]{:S(2)}, u32[]{:S(2)}) collective-permute-start(f32[136,128]{1,0:T(8,128)S(1)} %add_add_fusion.refs_2_), channel_id=1, source_target_pairs={{0,16},{1,17},{2,18},{3,19},{4,20},{5,21},{6,22},{7,23},{8,24},{9,... | collective-permute-start | bytes 208904 | tf_op jit(solution)/shard_map/ppermute | solution.py:435
  75.5 6.8 %collective-permute-start.13 = (f32[8,128]{1,0:T(8,128)S(1)}, f32[8,128]{1,0:T(8,128)S(1)}, u32[]{:S(2)}, u32[]{:S(2)}) collective-permute-start(f32[8,128]{1,0:T(8,128)S(1)} %reduce_sum.9.a), channel_id=1, source_target_pairs={{0,4},{1,5},{2,6},{3,7},{4,0},{5,1},{6,2},{7,3},{8,12},{9,13},{10,... | collective-permute-start | bytes 12296 | tf_op jit(solution)/shard_map/ppermute | solution.py:435

commit v5 on v4

--- a/solution.py
+++ b/solution.py
@@ -114,13 +114,13 @@
 
 
 def prepare_kernel(
-    pos_ref, samples_ref, basis_hbm, target_hbm, bits_hbm, keys_ref, ends_ref, own_ref, tab, last,
-    basis_ref, target_ref, bits_ref, scratch, walsh_ref, flip_ref, sems,
+    pos_ref, samples_hbm, basis_hbm, target_hbm, bits_hbm, keys_ref, ends_ref, rank_ref, tab, last,
+    samples_ref, basis_ref, target_ref, bits_ref, scratch, walsh_ref, flip_ref, sems,
 ):
     copies = [
         pltpu.make_async_copy(src, dst, sems.at[n])
         for n, (src, dst) in enumerate(
-            ((bits_hbm, bits_ref), (target_hbm, target_ref), (basis_hbm, basis_ref))
+            ((samples_hbm, samples_ref), (bits_hbm, bits_ref), (target_hbm, target_ref), (basis_hbm, basis_ref))
         )
     ]
     for copy in copies:
@@ -173,19 +173,28 @@
     a = lax.broadcasted_iota(jnp.int32, (SIDE, SIDE), 0)
     b = lax.broadcasted_iota(jnp.int32, (SIDE, SIDE), 1)
     walsh_ref[...] = (1 - 2 * fold(a & b)).astype(jnp.float32).astype(jnp.bfloat16)
+    copies[0].wait()
     store(0, bitonic(load(0), sub, lane))
-    for copy in copies:
+    for copy in copies[1:]:
         copy.wait()
     flip_ref[...] = jnp.concatenate([flips_of(0), flips_of(1)], axis=1)
     v = load(1)
     todo = list(range(COLS))
     for n, _ in enumerate(bitonic_steps(v, sub, lane)):
-        if n % 5 == 0 and todo:
+        if n % 9 == 0:
             mix(todo.pop(0))
-    while todo:
-        mix(todo.pop(0))
     store(1, v)
-    own_ref[...] = scratch[core]
+    v = []
+    for i in range(16):
+        key = scratch[core, pl.ds(i, 8, stride=16), :]
+        slot = (lane & 31) * LANES + sub * 16 + i
+        v.append((((key >> 1) & 4095) << 12) | slot)
+    for n, _ in enumerate(bitonic_steps(v, sub, lane)):
+        if n % 9 == 0 and todo:
+            mix(todo.pop(0))
+    for i in range(16):
+        scratch[2, pl.ds(i, 8, stride=16), :] = v[i] & 4095
+    rank_ref[...] = scratch[2].T
     tab[ROWS * 16 :, :] = jnp.zeros(((ROWS_PAD - ROWS) * 16, LANES), jnp.float32)
     last[ROWS:, :] = jnp.zeros((ROWS_PAD - ROWS, LANES), jnp.float32)
 
@@ -206,48 +215,22 @@
             jax.ShapeDtypeStruct((ROWS_PAD * 16, LANES), jnp.float32),
             jax.ShapeDtypeStruct((ROWS_PAD, LANES), jnp.float32),
         ),
-        in_specs=[SMEM, VMEM, FAR, FAR, FAR],
+        in_specs=[SMEM, FAR, FAR, FAR, FAR],
         out_specs=(VMEM,) * 5,
         scratch_shapes=[
+            pltpu.VMEM((16, 2, 8, LANES), jnp.int32),
             pltpu.VMEM((8192, LANES), jnp.float32),
             pltpu.VMEM((512, LANES), jnp.float32),
             pltpu.VMEM((512, LANES), jnp.int32),
-            pltpu.VMEM((2, LANES, LANES), jnp.int32),
+            pltpu.VMEM((3, LANES, LANES), jnp.int32),
             pltpu.VMEM((SIDE, SIDE), jnp.bfloat16),
             pltpu.VMEM((SIDE, SIDE), jnp.float32),
-            pltpu.SemaphoreType.DMA((3,)),
+            pltpu.SemaphoreType.DMA((4,)),
         ],
         compiler_params=pltpu.CompilerParams(vmem_limit_bytes=24 * 2**20),
         cost_estimate=COST,
         name="sort_and_walsh",
     )(pos, samples, basis, target, bits)
-
-
-def rank_kernel(own_ref, rank_ref, scratch):
-    sub = lax.broadcasted_iota(jnp.int32, (8, LANES), 0)
-    lane = lax.broadcasted_iota(jnp.int32, (8, LANES), 1)
-    v = []
-    for i in range(16):
-        key = own_ref[pl.ds(i, 8, stride=16), :]
-        slot = (lane & 31) * LANES + sub * 16 + i
-        v.append((((key >> 1) & 4095) << 12) | slot)
-    v = bitonic(v, sub, lane)
-    for i in range(16):
-        scratch[pl.ds(i, 8, stride=16), :] = v[i] & 4095
-    rank_ref[...] = scratch[...].T
-
-
-def rank_call(own):
-    return pl.pallas_call(
-        rank_kernel,
-        out_shape=jax.ShapeDtypeStruct((LANES, LANES), jnp.int32),
-        in_specs=[VMEM],
-        out_specs=VMEM,
-        scratch_shapes=[pltpu.VMEM((LANES, LANES), jnp.int32)],
-        compiler_params=pltpu.CompilerParams(vmem_limit_bytes=4 * 2**20),
-        cost_estimate=COST,
-        name="row_rank",
-    )(own)
 
 
 def slots_kernel(scale, off, cores, pos_ref, ends_ref, tab, last, keys_ref, *outs):
@@ -377,25 +360,27 @@
     table[8 * COLS :, :] = jnp.zeros((24 * 8 - 8 * COLS, LANES), jnp.float32)
     for h in range(2):
         sketch[:, h * LANES : (h + 1) * LANES] = table[pl.ds(2 * x + h, 24, stride=8), :][:COLS]
-    pieces, lefts = [], []
+    pieces, lefts = ([], []), ([], [])
     for tx in range(4):
         for h in range(2):
             v = table[pl.ds(2 * tx + h, 24, stride=8), :]
             owner = owners_ref[y * 4 + tx, core, pl.ds(2 * z + h, 1), :]
-            lefts.append(jnp.concatenate([jnp.where(owner == g, v[:16], 0.0) for g in range(GROUPS)], axis=0))
-            pieces.append(v)
-    value = jnp.concatenate(pieces, axis=1)
-    left = jnp.concatenate(lefts, axis=1)
-    total = lax.dot_general(
-        value, left, (((1,), (1,)), ((), ())),
-        precision=lax.Precision.HIGHEST, preferred_element_type=jnp.float32,
+            for n, term in enumerate(split(v)):
+                wide = term.astype(jnp.float32)
+                left = [jnp.where(owner == g, wide[:16], 0.0) for g in range(GROUPS)]
+                lefts[n].append(jnp.concatenate(left, axis=0).astype(jnp.bfloat16))
+                pieces[n].append(term)
+    value = [jnp.concatenate(p, axis=1) for p in pieces]
+    left = [jnp.concatenate(p, axis=1) for p in lefts]
+    total = sum(
+        lax.dot_general(value[p], left[q], (((1,), (1,)), ((), ())), preferred_element_type=jnp.float32)
+        for p, q in ((0, 0), (0, 1), (1, 0))
     )
     total = factor * total
     for to in range(4):
         own = [total[8 * n : 8 * n + 8, 32 * to : 32 * to + 32] for n in range(3)]
         message = jnp.concatenate(own + [jnp.zeros((8, 32), jnp.float32)], axis=1)
-        for row in range(4):
-            gram[row * 4 + to] = message
+        gram[to] = message
 
 
 def finish_call(factor, pos, owners, parts):
@@ -403,7 +388,7 @@
         lambda *refs: finish_kernel(factor, *refs),
         out_shape=(
             jax.ShapeDtypeStruct((COLS, SIDE), jnp.float32),
-            jax.ShapeDtypeStruct((16, 8, LANES), jnp.float32),
+            jax.ShapeDtypeStruct((4, 8, LANES), jnp.float32),
         ),
         in_specs=[SMEM] + [VMEM] * 5,
         out_specs=(VMEM,) * 2,
@@ -413,22 +398,22 @@
     )(pos, owners, *parts)
 
 
-def gram_kernel(a, b, out):
-    total = a[...] + b[...]
+def gram_kernel(messages, out):
+    total = jnp.sum(messages[...], axis=0)
     total = jnp.concatenate([total[:, 32 * n : 32 * n + 32] for n in range(3)], axis=0).T
     for g in range(2):
         out[g] = total[16 * g : 16 * g + 16, :COLS]
 
 
-def gram_call(a, b):
+def gram_call(messages):
     return pl.pallas_call(
         gram_kernel,
         out_shape=jax.ShapeDtypeStruct((2, 16, COLS), jnp.float32),
-        in_specs=[VMEM] * 2,
+        in_specs=[VMEM],
         out_specs=VMEM,
         compiler_params=pltpu.CompilerParams(vmem_limit_bytes=4 * 2**20),
         name="own_gram",
-    )(a, b)
+    )(messages)
 
 
 def send(v, axis, off):
@@ -449,9 +434,9 @@
     pos = jnp.stack([wide * 4 + z, core, y, x, z, z, z, z]).astype(jnp.int32)
 
     tiles = basis.reshape(2, 8, 512, LANES).transpose(0, 2, 1, 3).reshape(8192, LANES)
-    far = [tiles, target.reshape(512, LANES), sign_bits.reshape(512, LANES)]
+    far = [samples.reshape(16, 2, 8, LANES), tiles, target.reshape(512, LANES), sign_bits.reshape(512, LANES)]
     far = [pltpu.with_memory_space_constraint(v, pltpu.HBM) for v in far]
-    keys, ends, own, tab, last = prepare_call(pos, samples.reshape(16, 2, 8, LANES), *far)
+    keys, ends, rank, tab, last = prepare_call(pos, *far)
     def after(v, *others):
         return lax.optimization_barrier((v,) + others)[0]
 
@@ -477,17 +462,18 @@
     part3 = send(both3, "z", 3)
     keys = after(keys, both3)
     keep, give = take(0, 0, 1)
-    rank = rank_call(after(own, keep, part1, part3))
-    parts = [part2, part1, part3, keep + send(give, "c", 1)]
+    both0 = keep + send(give, "c", 1)
+    rank = after(rank, keep, part1, part3)
+    parts = [part2, part1, part3, both0]
     rels = (2, 1, 3)
     table, *lines = order_call(rels, pos, rank, *parts)
     got = [send(line, "y", rel) for line, rel in zip(lines, rels)]
     line = (order_call(0, pos, rank, table) + got[0]) + (got[1] + got[2])
     around = [line] + [send(line, "x", off) for off in (2, 1, 3)]
     sketch, gram = finish_call(GROUPS / total_samples, pos, owners.reshape(16, 2, 8, LANES), around)
+    gram = jnp.concatenate([gram + send(gram, "c", 1)] * 4, axis=0)
     gram = lax.all_to_all(gram, AXES, 0, 0, tiled=True, axis_index_groups=planes())
-    gram = jnp.sum(gram, axis=0)
-    return sketch.T, gram_call(gram, send(gram, "c", 1))
+    return sketch.T, gram_call(gram)
 
 
 def solution(mesh):

time: 83 us -> 80.2 us (0.966)
  starting transfers between devices: 26.6 us -> 24.4 us
  waiting for transfers between devices: 4.65 us -> 5.84 us
  Pallas kernels: 37.6 us -> 36.5 us
  local copies, waits for them, and re-layouts: 1 us -> 0.09 us
    ppermute x14, starting transfers between devices: 26.6 us -> 24.4 us  [send(): return lax.ppermute(v, AXES, shift(axis, off))]
    pallas_call x1 -> x0, Pallas kernels: 1.66 us -> none  [rank_call(): pl.pallas_call(rank_kernel, out_shape=jax.ShapeDtypeStruct((LANES, LANES)...]
    ppermute x14, waiting for transfers between devices: 4.65 us -> 5.84 us  [send(): return lax.ppermute(v, AXES, shift(axis, off))]
    pallas_call x1, Pallas kernels: 7.74 us -> 8.77 us  [prepare_call(): pl.pallas_call(prepare_kernel, out_shape=(jax.ShapeDtypeStruct((256, LANE...]
    unnamed x4 -> x2, local copies, waits for them, and re-layouts: 0.91 us -> 0.01 us
  transfers between devices with their start and end apart: 14 -> 14, of which waited for: 3 -> 4; matrix products, arithmetic and copies ran while one was open for 0% -> 0% of each run, Pallas kernels for 24% -> 22%
where the time goes in v5:
time: 80.2 us; the launch traced here: 79.7 us
  Pallas kernels  36.5 us (46%)
  starting transfers between devices  24.4 us (30%)
  blocking collectives  12 us (15%)
  waiting for transfers between devices  5.84 us (7%)
    ppermute x14, starting transfers between devices, send(): return lax.ppermute(v, AXES, shift(axis, off))  24.4 us
    pallas_call x6, Pallas kernels, slots_call(): pl.pallas_call(lambda *refs: slots_kernel(scale, off, cores, *refs), out_...  21.7 us
    all_to_all x1, blocking collectives, shards(): lax.all_to_all(gram, AXES, 0, 0, tiled=True, axis_index_groups=planes())  12 us
    pallas_call x1, Pallas kernels, prepare_call(): pl.pallas_call(prepare_kernel, out_shape=(jax.ShapeDtypeStruct((256, LANE...  8.77 us
    ppermute x14, waiting for transfers between devices, send(): return lax.ppermute(v, AXES, shift(axis, off))  5.84 us
    pallas_call x2, Pallas kernels, order_call(): pl.pallas_call(lambda *refs: kernel(rel, *refs), out_shape=(table,) + (ou...  3.89 us
  transfers between devices with their start and end apart: 14, of which 4 were waited for; matrix products, arithmetic and copies ran while one was open for 0% of the time, Pallas kernels for 22%

profile of v5, /device:TPU:1, one launch (start us, length us, event | category | flops | bytes accessed | tf_op | source)
XLA Modules:
  0.0 79.7 jit_solution(13774414879410772525)
XLA Ops:
  0.6 0.1 stack.26.pos_ref.refs_0_
  0.7 8.8 %sort_and_walsh.1 = (s32[256,128]{1,0:T(8,128)S(1)}, s32[4,128]{1,0:T(4,128)S(1)}, s32[128,128]{1,0:T(8,128)S(1)}, f32[8576,128]{1,0:T(8,128)S(1)}, f32[536,128]{1,0:T(8,128)S(1)}) custom-call(s32[8]{0:T(128)S(1)} %stack.26.pos_ref.refs_0_, s32[16,2,8,128]{3,2,1,0:T(8,128)} %bitcast.19, f32[8192,128]{1,0:T(8,128)} %bitcast.16, f32[512,128]{1,0:T(8,128)} %bitcast.17, ...), custom_call_target="tpu_custom_call" | custom-call | flops 1000000 | bytes 1000000 | tf_op jit(solution)/shard_map/sort_and_walsh/pallas_call | solution.py:209
  9.5 5.1 %take_slots_201.1 = (f32[544,128]{1,0:T(8,128)S(1)}, f32[544,128]{1,0:T(8,128)S(1)}) custom-call(s32[8]{0:T(128)S(1)} %stack.26.pos_ref.refs_0_, s32[4,128]{1,0:T(4,128)S(1)} %get-tuple-element.23.refs_1_, f32[8576,128]{1,0:T(8,128)S(1)} %get-tuple-element.24.refs_2_, f32[536,128]{1,0:T(8,128)S(1)} %get-tuple-element.25.refs_3_, ...), custom_call_target="tpu_custom_call" | custom-call | flops 1000000 | bytes 1000000 | tf_op jit(solution)/shard_map/take_slots_201/pallas_call | solution.py:298
  14.6 1.5 %collective-permute-start = (f32[544,128]{1,0:T(8,128)S(1)}, f32[544,128]{1,0:T(8,128)S(1)}, u32[]{:S(2)}, u32[]{:S(2)}) collective-permute-start(f32[544,128]{1,0:T(8,128)S(1)} %get-tuple-element.28), channel_id=1, source_target_pairs={{0,4},{1,5},{2,6},{3,7},{4,0},{5,1},{6,2},{7,3},{8,12},{9,13},{10,... | collective-permute-start | bytes 835592 | tf_op jit(solution)/shard_map/ppermute | solution.py:420
  16.1 2.9 %take_slots_11.1 = f32[544,128]{1,0:T(8,128)S(1)} custom-call(s32[8]{0:T(128)S(1)} %stack.26.pos_ref.refs_0_, s32[4,128]{1,0:T(4,128)S(1)} %get-tuple-element.23.refs_1_, f32[8576,128]{1,0:T(8,128)S(1)} %get-tuple-element.24.refs_2_, f32[536,128]{1,0:T(8,128)S(1)} %get-tuple-element.25.refs_3_, s32[256,128]{1,0:T(8,128)S(1)} %get-tuple-element.32.refs_4_), custom_call_target="tpu_custom_call" | custom-call | flops 1000000 | bytes 1000000 | tf_op jit(solution)/shard_map/take_slots_11/pallas_call | solution.py:298
  19.1 0.1 collective-permute-start.1
  19.2 0.0 collective-permute-done
  19.2 3.6 %collective-permute-start.2 = (f32[544,128]{1,0:T(8,128)S(1)}, f32[544,128]{1,0:T(8,128)S(1)}, u32[]{:S(2)}, u32[]{:S(2)}) collective-permute-start(f32[544,128]{1,0:T(8,128)S(1)} %add.28), channel_id=1, source_target_pairs={{0,2},{1,3},{2,0},{3,1},{4,6},{5,7},{6,4},{7,5},{8,10},{9,11},{10,... | collective-permute-start | bytes 835592 | tf_op jit(solution)/shard_map/ppermute | solution.py:420
  22.9 2.9 %take_slots_10.1 = f32[544,128]{1,0:T(8,128)S(1)} custom-call(s32[8]{0:T(128)S(1)} %stack.26.pos_ref.refs_0_, s32[4,128]{1,0:T(4,128)S(1)} %get-tuple-element.23.refs_1_, f32[8576,128]{1,0:T(8,128)S(1)} %get-tuple-element.24.refs_2_, f32[536,128]{1,0:T(8,128)S(1)} %get-tuple-element.25.refs_3_, s32[256,128]{1,0:T(8,128)S(1)} %get-tuple-element.32.refs_4_), custom_call_target="tpu_custom_call" | custom-call | flops 1000000 | bytes 1000000 | tf_op jit(solution)/shard_map/take_slots_10/pallas_call | solution.py:298
  25.8 0.0 collective-permute-done.1
  25.8 2.8 %take_slots_31.1 = f32[544,128]{1,0:T(8,128)S(1)} custom-call(s32[8]{0:T(128)S(1)} %stack.26.pos_ref.refs_0_, s32[4,128]{1,0:T(4,128)S(1)} %get-tuple-element.23.refs_1_, f32[8576,128]{1,0:T(8,128)S(1)} %get-tuple-element.24.refs_2_, f32[536,128]{1,0:T(8,128)S(1)} %get-tuple-element.25.refs_3_, s32[256,128]{1,0:T(8,128)S(1)} %get-tuple-element.32.refs_4_), custom_call_target="tpu_custom_call" | custom-call | flops 1000000 | bytes 1000000 | tf_op jit(solution)/shard_map/take_slots_31/pallas_call | solution.py:298
  28.6 0.8 %collective-permute-start.3 = (f32[544,128]{1,0:T(8,128)S(1)}, f32[544,128]{1,0:T(8,128)S(1)}, u32[]{:S(2)}, u32[]{:S(2)}) collective-permute-start(f32[544,128]{1,0:T(8,128)S(1)} %take_slots_31.1), channel_id=1, source_target_pairs={{0,4},{1,5},{2,6},{3,7},{4,0},{5,1},{6,2},{7,3},{8,12},{9,13},{10,... | collective-permute-start | bytes 835592 | tf_op jit(solution)/shard_map/ppermute | solution.py:420
  29.5 1.0 %collective-permute-start.4 = (f32[544,128]{1,0:T(8,128)S(1)}, f32[544,128]{1,0:T(8,128)S(1)}, u32[]{:S(2)}, u32[]{:S(2)}) collective-permute-start(f32[544,128]{1,0:T(8,128)S(1)} %add.29), channel_id=1, source_target_pairs={{0,1},{1,2},{2,3},{3,0},{4,5},{5,6},{6,7},{7,4},{8,9},{9,10},{10,1... | collective-permute-start | bytes 835592 | tf_op jit(solution)/shard_map/ppermute | solution.py:420
  30.5 0.0 collective-permute-done.2.refs_2_
  30.5 2.8 %take_slots_30.1 = f32[544,128]{1,0:T(8,128)S(1)} custom-call(s32[8]{0:T(128)S(1)} %stack.26.pos_ref.refs_0_, s32[4,128]{1,0:T(4,128)S(1)} %get-tuple-element.23.refs_1_, f32[8576,128]{1,0:T(8,128)S(1)} %get-tuple-element.24.refs_2_, f32[536,128]{1,0:T(8,128)S(1)} %get-tuple-element.25.refs_3_, s32[256,128]{1,0:T(8,128)S(1)} %get-tuple-element.32.refs_4_), custom_call_target="tpu_custom_call" | custom-call | flops 1000000 | bytes 1000000 | tf_op jit(solution)/shard_map/take_slots_30/pallas_call | solution.py:298
  33.3 0.0 copy-start
  33.3 0.0 collective-permute-done.3
  33.3 2.1 %collective-permute-start.5 = (f32[544,128]{1,0:T(8,128)S(1)}, f32[544,128]{1,0:T(8,128)S(1)}, u32[]{:S(2)}, u32[]{:S(2)}) collective-permute-start(f32[544,128]{1,0:T(8,128)S(1)} %add.30), channel_id=1, source_target_pairs={{0,3},{1,0},{2,1},{3,2},{4,7},{5,4},{6,5},{7,6},{8,11},{9,8},{10,9... | collective-permute-start | bytes 835592 | tf_op jit(solution)/shard_map/ppermute | solution.py:420
  35.4 5.1 %take_slots_001.1 = (f32[544,128]{1,0:T(8,128)S(1)}, f32[544,128]{1,0:T(8,128)S(1)}) custom-call(s32[8]{0:T(128)S(1)} %stack.26.pos_ref.refs_0_, s32[4,128]{1,0:T(4,128)S(1)} %get-tuple-element.23.refs_1_, f32[8576,128]{1,0:T(8,128)S(1)} %get-tuple-element.24.refs_2_, f32[536,128]{1,0:T(8,128)S(1)} %get-tuple-element.25.refs_3_, ...), custom_call_target="tpu_custom_call" | custom-call | flops 1000000 | bytes 1000000 | tf_op jit(solution)/shard_map/take_slots_001/pallas_call | solution.py:298
  40.6 2.0 %collective-permute-start.6 = (f32[544,128]{1,0:T(8,128)S(1)}, f32[544,128]{1,0:T(8,128)S(1)}, u32[]{:S(2)}, u32[]{:S(2)}) collective-permute-start(f32[544,128]{1,0:T(8,128)S(1)} %get-tuple-element.35), channel_id=1, source_target_pairs={{0,4},{1,5},{2,6},{3,7},{4,0},{5,1},{6,2},{7,3},{8,12},{9,13},{10,... | collective-permute-start | bytes 835592 | tf_op jit(solution)/shard_map/ppermute | solution.py:420
  42.6 0.0 collective-permute-done.4.refs_3_
  42.6 0.0 collective-permute-done.5.refs_4_
  42.6 1.2 %collective-permute-done.6 = f32[544,128]{1,0:T(8,128)S(1)} collective-permute-done((f32[544,128]{1,0:T(8,128)S(1)}, f32[544,128]{1,0:T(8,128)S(1)}, u32[]{:S(2)}, u32[]{:S(2)}) %collective-permute-start.6) | collective-permute-done | bytes 278560 | tf_op jit(solution)/shard_map/ppermute | solution.py:420
  43.8 2.6 %given_order_far.1 = (f32[544,128]{1,0:T(8,128)S(1)}, f32[136,128]{1,0:T(8,128)S(1)}, f32[136,128]{1,0:T(8,128)S(1)}, f32[136,128]{1,0:T(8,128)S(1)}) custom-call(s32[8]{0:T(128)S(1)} %stack.26.pos_ref.refs_0_, s32[128,128]{1,0:T(8,128)S(1)} %get-tuple-element.34.refs_1_, f32[544,128]{1,0:T(8,128)S(1)} %collective-permute-done.2.refs_2_, ...), custom_call_target="tpu_custom_call" | custom-call | flops 1000000 | bytes 1000000 | tf_op jit(solution)/shard_map/given_order_far/pallas_call | solution.py:345
  46.4 3.0 %collective-permute-start.7 = (f32[136,128]{1,0:T(8,128)S(1)}, f32[136,128]{1,0:T(8,128)S(1)}, u32[]{:S(2)}, u32[]{:S(2)}) collective-permute-start(f32[136,128]{1,0:T(8,128)S(1)} %get-tuple-element.37), channel_id=1, source_target_pairs={{0,64},{1,65},{2,66},{3,67},{4,68},{5,69},{6,70},{7,71},{8,72},{9,... | collective-permute-start | bytes 208904 | tf_op jit(solution)/shard_map/ppermute | solution.py:420
  49.4 0.4 collective-permute-start.8
  49.8 2.3 %collective-permute-start.9 = (f32[136,128]{1,0:T(8,128)S(1)}, f32[136,128]{1,0:T(8,128)S(1)}, u32[]{:S(2)}, u32[]{:S(2)}) collective-permute-start(f32[136,128]{1,0:T(8,128)S(1)} %get-tuple-element.39), channel_id=1, source_target_pairs={{0,96},{1,97},{2,98},{3,99},{4,100},{5,101},{6,102},{7,103},{8,104... | collective-permute-start | bytes 208904 | tf_op jit(solution)/shard_map/ppermute | solution.py:420
  52.1 1.3 %given_order_own.1 = f32[136,128]{1,0:T(8,128)S(1)} custom-call(s32[8]{0:T(128)S(1)} %stack.26.pos_ref.refs_0_, s32[128,128]{1,0:T(8,128)S(1)} %get-tuple-element.34.refs_1_, f32[544,128]{1,0:T(8,128)S(1)} %get-tuple-element.36.refs_2_), custom_call_target="tpu_custom_call" | custom-call | flops 1000000 | bytes 1000000 | tf_op jit(solution)/shard_map/given_order_own/pallas_call | solution.py:345
  53.4 0.0 collective-permute-done.7
  53.4 0.4 collective-permute-done.8
  53.8 0.0 collective-permute-done.9
  53.8 2.5 %collective-permute-start.12 = (f32[136,128]{1,0:T(8,128)S(1)}, f32[136,128]{1,0:T(8,128)S(1)}, u32[]{:S(2)}, u32[]{:S(2)}) collective-permute-start(f32[136,128]{1,0:T(8,128)S(1)} %add_add_fusion.refs_2_), channel_id=1, source_target_pairs={{0,24},{1,25},{2,26},{3,27},{4,28},{5,29},{6,30},{7,31},{8,0},{9,1... | collective-permute-start | bytes 208904 | tf_op jit(solution)/shard_map/ppermute | solution.py:420
  56.4 0.0 collective-permute-start.11
  56.4 1.7 %collective-permute-start.10 = (f32[136,128]{1,0:T(8,128)S(1)}, f32[136,128]{1,0:T(8,128)S(1)}, u32[]{:S(2)}, u32[]{:S(2)}) collective-permute-start(f32[136,128]{1,0:T(8,128)S(1)} %add_add_fusion.refs_2_), channel_id=1, source_target_pairs={{0,16},{1,17},{2,18},{3,19},{4,20},{5,21},{6,22},{7,23},{8,24},{9,... | collective-permute-start | bytes 208904 | tf_op jit(solution)/shard_map/ppermute | solution.py:420
  58.1 0.0 collective-permute-done.12.refs_5_
  58.1 3.4 %collective-permute-done.11.refs_4_ = f32[136,128]{1,0:T(8,128)S(1)} collective-permute-done((f32[136,128]{1,0:T(8,128)S(1)}, f32[136,128]{1,0:T(8,128)S(1)}, u32[]{:S(2)}, u32[]{:S(2)}) %collective-permute-start.11) | collective-permute-done | bytes 69664 | tf_op jit(solution)/shard_map/ppermute | solution.py:420
  61.5 0.0 collective-permute-done.10.refs_3_
  61.5 0.0 copy-done
  61.5 1.4 %rows_and_gram.1 = (f32[17,256]{1,0:T(8,128)}, f32[4,8,128]{2,1,0:T(8,128)S(1)}) custom-call(s32[8]{0:T(128)S(1)} %stack.26.pos_ref.refs_0_, s32[16,2,8,128]{3,2,1,0:T(8,128)S(1)} %bitcast.15, f32[136,128]{1,0:T(8,128)S(1)} %add_add_fusion.refs_2_, f32[136,128]{1,0:T(8,128)S(1)} %collective-permute-done.10.refs_3_, ...), custom_call_target="tpu_custom_call" | custom-call | tf_op jit(solution)/shard_map/rows_and_gram/pallas_call | solution.py:387
  62.9 3.2 %collective-permute-start.13 = (f32[4,8,128]{2,1,0:T(8,128)S(1)}, f32[4,8,128]{2,1,0:T(8,128)S(1)}, u32[]{:S(2)}, u32[]{:S(2)}) collective-permute-start(f32[4,8,128]{2,1,0:T(8,128)S(1)} %get-tuple-element.41), channel_id=1, source_target_pairs={{0,4},{1,5},{2,6},{3,7},{4,0},{5,1},{6,2},{7,3},{8,12},{9,13},{10,... | collective-permute-start | bytes 49160 | tf_op jit(solution)/shard_map/ppermute | solution.py:420
  66.1 0.8 %collective-permute-done.13 = f32[4,8,128]{2,1,0:T(8,128)S(1)} collective-permute-done((f32[4,8,128]{2,1,0:T(8,128)S(1)}, f32[4,8,128]{2,1,0:T(8,128)S(1)}, u32[]{:S(2)}, u32[]{:S(2)}) %collective-permute-start.13) | collective-permute-done | bytes 16416 | tf_op jit(solution)/shard_map/ppermute | solution.py:420
  67.0 12.0 %all_to_all.5.messages = f32[16,8,128]{2,1,0:T(8,128)S(1)} all-to-all(f32[16,8,128]{2,1,0:T(8,128)S(1)} %pad_maximum_fusion), channel_id=1, replica_groups={{0,1,2,3,32,33,34,35,64,65,66,67,96,97,98,99},{4,5,6,7,36,37,38,39,68,6..., dimensions={0} | all-to-all | bytes 131072 | tf_op jit(solution)/shard_map/all_to_all | solution.py:475
  78.9 0.8 own_gram.1
  (7 shorter events, 0.2 us)
Async XLA Ops:
  14.6 4.5 %collective-permute-start = (f32[544,128]{1,0:T(8,128)S(1)}, f32[544,128]{1,0:T(8,128)S(1)}, u32[]{:S(2)}, u32[]{:S(2)}) collective-permute-start(f32[544,128]{1,0:T(8,128)S(1)} %get-tuple-element.28), channel_id=1, source_target_pairs={{0,4},{1,5},{2,6},{3,7},{4,0},{5,1},{6,2},{7,3},{8,12},{9,13},{10,... | collective-permute-start | bytes 835592 | tf_op jit(solution)/shard_map/ppermute | solution.py:420
  19.1 6.7 %collective-permute-start.1 = (f32[544,128]{1,0:T(8,128)S(1)}, f32[544,128]{1,0:T(8,128)S(1)}, u32[]{:S(2)}, u32[]{:S(2)}) collective-permute-start(f32[544,128]{1,0:T(8,128)S(1)} %take_slots_11.1), channel_id=1, source_target_pairs={{0,4},{1,5},{2,6},{3,7},{4,0},{5,1},{6,2},{7,3},{8,12},{9,13},{10,... | collective-permute-start | bytes 835592 | tf_op jit(solution)/shard_map/ppermute | solution.py:420
  19.2 11.3 %collective-permute-start.2 = (f32[544,128]{1,0:T(8,128)S(1)}, f32[544,128]{1,0:T(8,128)S(1)}, u32[]{:S(2)}, u32[]{:S(2)}) collective-permute-start(f32[544,128]{1,0:T(8,128)S(1)} %add.28), channel_id=1, source_target_pairs={{0,2},{1,3},{2,0},{3,1},{4,6},{5,7},{6,4},{7,5},{8,10},{9,11},{10,... | collective-permute-start | bytes 835592 | tf_op jit(solution)/shard_map/ppermute | solution.py:420
  28.6 4.7 %collective-permute-start.3 = (f32[544,128]{1,0:T(8,128)S(1)}, f32[544,128]{1,0:T(8,128)S(1)}, u32[]{:S(2)}, u32[]{:S(2)}) collective-permute-start(f32[544,128]{1,0:T(8,128)S(1)} %take_slots_31.1), channel_id=1, source_target_pairs={{0,4},{1,5},{2,6},{3,7},{4,0},{5,1},{6,2},{7,3},{8,12},{9,13},{10,... | collective-permute-start | bytes 835592 | tf_op jit(solution)/shard_map/ppermute | solution.py:420
  29.5 13.1 %collective-permute-start.4 = (f32[544,128]{1,0:T(8,128)S(1)}, f32[544,128]{1,0:T(8,128)S(1)}, u32[]{:S(2)}, u32[]{:S(2)}) collective-permute-start(f32[544,128]{1,0:T(8,128)S(1)} %add.29), channel_id=1, source_target_pairs={{0,1},{1,2},{2,3},{3,0},{4,5},{5,6},{6,7},{7,4},{8,9},{9,10},{10,1... | collective-permute-start | bytes 835592 | tf_op jit(solution)/shard_map/ppermute | solution.py:420
  33.3 28.2 %copy-start = (s32[32768]{0:T(1024)S(1)}, s32[32768]{0:T(1024)}, u32[]{:S(2)}) copy-start(s32[32768]{0:T(1024)} %param.9) | copy-start | bytes 393220
  33.3 9.2 %collective-permute-start.5 = (f32[544,128]{1,0:T(8,128)S(1)}, f32[544,128]{1,0:T(8,128)S(1)}, u32[]{:S(2)}, u32[]{:S(2)}) collective-permute-start(f32[544,128]{1,0:T(8,128)S(1)} %add.30), channel_id=1, source_target_pairs={{0,3},{1,0},{2,1},{3,2},{4,7},{5,4},{6,5},{7,6},{8,11},{9,8},{10,9... | collective-permute-start | bytes 835592 | tf_op jit(solution)/shard_map/ppermute | solution.py:420
  40.6 3.2 %collective-permute-start.6 = (f32[544,128]{1,0:T(8,128)S(1)}, f32[544,128]{1,0:T(8,128)S(1)}, u32[]{:S(2)}, u32[]{:S(2)}) collective-permute-start(f32[544,128]{1,0:T(8,128)S(1)} %get-tuple-element.35), channel_id=1, source_target_pairs={{0,4},{1,5},{2,6},{3,7},{4,0},{5,1},{6,2},{7,3},{8,12},{9,13},{10,... | collective-permute-start | bytes 835592 | tf_op jit(solution)/shard_map/ppermute | solution.py:420
  46.4 6.9 %collective-permute-start.7 = (f32[136,128]{1,0:T(8,128)S(1)}, f32[136,128]{1,0:T(8,128)S(1)}, u32[]{:S(2)}, u32[]{:S(2)}) collective-permute-start(f32[136,128]{1,0:T(8,128)S(1)} %get-tuple-element.37), channel_id=1, source_target_pairs={{0,64},{1,65},{2,66},{3,67},{4,68},{5,69},{6,70},{7,71},{8,72},{9,... | collective-permute-start | bytes 208904 | tf_op jit(solution)/shard_map/ppermute | solution.py:420
  49.4 4.4 %collective-permute-start.8 = (f32[136,128]{1,0:T(8,128)S(1)}, f32[136,128]{1,0:T(8,128)S(1)}, u32[]{:S(2)}, u32[]{:S(2)}) collective-permute-start(f32[136,128]{1,0:T(8,128)S(1)} %get-tuple-element.38), channel_id=1, source_target_pairs={{0,32},{1,33},{2,34},{3,35},{4,36},{5,37},{6,38},{7,39},{8,40},{9,... | collective-permute-start | bytes 208904 | tf_op jit(solution)/shard_map/ppermute | solution.py:420
  49.8 4.0 %collective-permute-start.9 = (f32[136,128]{1,0:T(8,128)S(1)}, f32[136,128]{1,0:T(8,128)S(1)}, u32[]{:S(2)}, u32[]{:S(2)}) collective-permute-start(f32[136,128]{1,0:T(8,128)S(1)} %get-tuple-element.39), channel_id=1, source_target_pairs={{0,96},{1,97},{2,98},{3,99},{4,100},{5,101},{6,102},{7,103},{8,104... | collective-permute-start | bytes 208904 | tf_op jit(solution)/shard_map/ppermute | solution.py:420
  53.8 4.3 %collective-permute-start.12 = (f32[136,128]{1,0:T(8,128)S(1)}, f32[136,128]{1,0:T(8,128)S(1)}, u32[]{:S(2)}, u32[]{:S(2)}) collective-permute-start(f32[136,128]{1,0:T(8,128)S(1)} %add_add_fusion.refs_2_), channel_id=1, source_target_pairs={{0,24},{1,25},{2,26},{3,27},{4,28},{5,29},{6,30},{7,31},{8,0},{9,1... | collective-permute-start | bytes 208904 | tf_op jit(solution)/shard_map/ppermute | solution.py:420
  56.4 5.1 %collective-permute-start.11 = (f32[136,128]{1,0:T(8,128)S(1)}, f32[136,128]{1,0:T(8,128)S(1)}, u32[]{:S(2)}, u32[]{:S(2)}) collective-permute-start(f32[136,128]{1,0:T(8,128)S(1)} %add_add_fusion.refs_2_), channel_id=1, source_target_pairs={{0,8},{1,9},{2,10},{3,11},{4,12},{5,13},{6,14},{7,15},{8,16},{9,17... | collective-permute-start | bytes 208904 | tf_op jit(solution)/shard_map/ppermute | solution.py:420
  56.4 5.1 %collective-permute-start.10 = (f32[136,128]{1,0:T(8,128)S(1)}, f32[136,128]{1,0:T(8,128)S(1)}, u32[]{:S(2)}, u32[]{:S(2)}) collective-permute-start(f32[136,128]{1,0:T(8,128)S(1)} %add_add_fusion.refs_2_), channel_id=1, source_target_pairs={{0,16},{1,17},{2,18},{3,19},{4,20},{5,21},{6,22},{7,23},{8,24},{9,... | collective-permute-start | bytes 208904 | tf_op jit(solution)/shard_map/ppermute | solution.py:420
  62.9 4.1 %collective-permute-start.13 = (f32[4,8,128]{2,1,0:T(8,128)S(1)}, f32[4,8,128]{2,1,0:T(8,128)S(1)}, u32[]{:S(2)}, u32[]{:S(2)}) collective-permute-start(f32[4,8,128]{2,1,0:T(8,128)S(1)} %get-tuple-element.41), channel_id=1, source_target_pairs={{0,4},{1,5},{2,6},{3,7},{4,0},{5,1},{6,2},{7,3},{8,12},{9,13},{10,... | collective-permute-start | bytes 49160 | tf_op jit(solution)/shard_map/ppermute | solution.py:420

commit v6 on v5

--- a/solution.py
+++ b/solution.py
@@ -12,6 +12,7 @@
 LANES = 128
 COLS = 17
 SIDE = 256
+FETCHED = 36
 PEEL = 20
 STEP = 4
 EIGHTHS = 4
@@ -32,9 +33,13 @@
                     at = {"y": y, "x": x, "c": c, "z": z}
                     size = 2 if axis == "c" else 4
                     to = dict(at)
-                    to[axis] = (at[axis] + off) % size
+                    to[axis] = (at[axis] + (-off if c else off)) % size
                     pairs.append((number(**at), number(**to)))
     return pairs
+
+
+def away(core, off):
+    return jnp.where(core == 0, off, -off)
 
 
 def fold(v):
@@ -174,16 +179,17 @@
     b = lax.broadcasted_iota(jnp.int32, (SIDE, SIDE), 1)
     walsh_ref[...] = (1 - 2 * fold(a & b)).astype(jnp.float32).astype(jnp.bfloat16)
     copies[0].wait()
-    store(0, bitonic(load(0), sub, lane))
-    for copy in copies[1:]:
-        copy.wait()
-    flip_ref[...] = jnp.concatenate([flips_of(0), flips_of(1)], axis=1)
-    v = load(1)
+    v, w = load(0), load(1)
     todo = list(range(COLS))
-    for n, _ in enumerate(bitonic_steps(v, sub, lane)):
-        if n % 9 == 0:
+    for n, _ in enumerate(zip(bitonic_steps(v, sub, lane), bitonic_steps(w, sub, lane))):
+        if n == FETCHED:
+            for copy in copies[1:]:
+                copy.wait()
+            flip_ref[...] = jnp.concatenate([flips_of(0), flips_of(1)], axis=1)
+        if n >= FETCHED and (n - FETCHED) % 5 == 0 and len(todo) > 9:
             mix(todo.pop(0))
-    store(1, v)
+    store(0, v)
+    store(1, w)
     v = []
     for i in range(16):
         key = scratch[core, pl.ds(i, 8, stride=16), :]
@@ -192,6 +198,8 @@
     for n, _ in enumerate(bitonic_steps(v, sub, lane)):
         if n % 9 == 0 and todo:
             mix(todo.pop(0))
+    while todo:
+        mix(todo.pop(0))
     for i in range(16):
         scratch[2, pl.ds(i, 8, stride=16), :] = v[i] & 4095
     rank_ref[...] = scratch[2].T
@@ -235,12 +243,12 @@
 
 def slots_kernel(scale, off, cores, pos_ref, ends_ref, tab, last, keys_ref, *outs):
     core = pos_ref[1]
-    z = (pos_ref[4] + off) & 3
     sub = lax.broadcasted_iota(jnp.int32, (8, LANES), 0)
     for rel_core, out in zip(cores, outs):
         c = core ^ rel_core
-
-        def group(it, _, c=c, out=out):
+        z = (pos_ref[4] + away(c, off)) & 3
+
+        def group(it, _, c=c, z=z, out=out):
             lows, tiles, lanes_of, rows_of, subrows, weights = [], [], [], [], [], []
             most, many = jnp.int32(0), jnp.int32(0)
             for q in range(4):
@@ -307,12 +315,12 @@
 
 
 def order_lines(rel, pos_ref, rank_ref, table, out, boxes):
-    y, z = pos_ref[2], pos_ref[4]
+    y, z = pos_ref[2] + away(pos_ref[1], rel), pos_ref[4]
     rows = 8 * COLS
     at = lax.broadcasted_iota(jnp.int32, (rows, LANES), 0)
     code = jnp.where(at >= rows // 2, 4, 0) + (at & 3)
     for i in range(8):
-        line = z * 32 + ((y + rel) & 3) * 8 + i
+        line = z * 32 + (y & 3) * 8 + i
         slot = jnp.broadcast_to(rank_ref[pl.ds(line, 1), :], (8, LANES))
         index = slot & 127
         pair = slot >> 10

time: 80.2 us -> 78.3 us (0.976)
  waiting for transfers between devices: 5.84 us -> 8.94 us
  starting transfers between devices: 24.4 us -> 21.8 us
  blocking collectives: 12 us -> 10.4 us
  Pallas kernels: 36.5 us -> 35.6 us
    ppermute x14, waiting for transfers between devices: 5.84 us -> 8.94 us  [send(): return lax.ppermute(v, AXES, shift(axis, off))]
    ppermute x14, starting transfers between devices: 24.4 us -> 21.8 us  [send(): return lax.ppermute(v, AXES, shift(axis, off))]
    all_to_all x1, blocking collectives: 12 us -> 10.4 us  [shards(): lax.all_to_all(gram, AXES, 0, 0, tiled=True, axis_index_groups=planes())]
  transfers between devices with their start and end apart: 14 -> 14, of which waited for: 4 -> 7; matrix products, arithmetic and copies ran while one was open for 0% -> 0% of each run, Pallas kernels for 22% -> 22%
where the time goes in v6:
time: 78.3 us; the launch traced here: 77.7 us
  Pallas kernels  35.6 us (45%)
  starting transfers between devices  21.8 us (28%)
  blocking collectives  10.4 us (13%)
  waiting for transfers between devices  8.94 us (11%)
    ppermute x14, starting transfers between devices, send(): return lax.ppermute(v, AXES, shift(axis, off))  21.8 us
    pallas_call x6, Pallas kernels, slots_call(): pl.pallas_call(lambda *refs: slots_kernel(scale, off, cores, *refs), out_...  21.2 us
    all_to_all x1, blocking collectives, shards(): lax.all_to_all(gram, AXES, 0, 0, tiled=True, axis_index_groups=planes())  10.4 us
    ppermute x14, waiting for transfers between devices, send(): return lax.ppermute(v, AXES, shift(axis, off))  8.94 us
    pallas_call x1, Pallas kernels, prepare_call(): pl.pallas_call(prepare_kernel, out_shape=(jax.ShapeDtypeStruct((256, LANE...  8.41 us
    pallas_call x2, Pallas kernels, order_call(): pl.pallas_call(lambda *refs: kernel(rel, *refs), out_shape=(table,) + (ou...  3.9 us
  transfers between devices with their start and end apart: 14, of which 7 were waited for; matrix products, arithmetic and copies ran while one was open for 0% of the time, Pallas kernels for 22%

profile of v6, /device:TPU:1, one launch (start us, length us, event | category | flops | bytes accessed | tf_op | source)
XLA Modules:
  0.0 77.7 jit_solution(13336258526066587626)
XLA Ops:
  0.6 0.1 stack.26.pos_ref.refs_0_
  0.7 8.4 %sort_and_walsh.1 = (s32[256,128]{1,0:T(8,128)S(1)}, s32[4,128]{1,0:T(4,128)S(1)}, s32[128,128]{1,0:T(8,128)S(1)}, f32[8576,128]{1,0:T(8,128)S(1)}, f32[536,128]{1,0:T(8,128)S(1)}) custom-call(s32[8]{0:T(128)S(1)} %stack.26.pos_ref.refs_0_, s32[16,2,8,128]{3,2,1,0:T(8,128)} %bitcast.19, f32[8192,128]{1,0:T(8,128)} %bitcast.16, f32[512,128]{1,0:T(8,128)} %bitcast.17, ...), custom_call_target="tpu_custom_call" | custom-call | flops 1000000 | bytes 1000000 | tf_op jit(solution)/shard_map/sort_and_walsh/pallas_call | solution.py:217
  9.1 5.0 %take_slots_201.1 = (f32[544,128]{1,0:T(8,128)S(1)}, f32[544,128]{1,0:T(8,128)S(1)}) custom-call(s32[8]{0:T(128)S(1)} %stack.26.pos_ref.refs_0_, s32[4,128]{1,0:T(4,128)S(1)} %get-tuple-element.23.refs_1_, f32[8576,128]{1,0:T(8,128)S(1)} %get-tuple-element.24.refs_2_, f32[536,128]{1,0:T(8,128)S(1)} %get-tuple-element.25.refs_3_, ...), custom_call_target="tpu_custom_call" | custom-call | flops 1000000 | bytes 1000000 | tf_op jit(solution)/shard_map/take_slots_201/pallas_call | solution.py:306
  14.2 1.5 %collective-permute-start = (f32[544,128]{1,0:T(8,128)S(1)}, f32[544,128]{1,0:T(8,128)S(1)}, u32[]{:S(2)}, u32[]{:S(2)}) collective-permute-start(f32[544,128]{1,0:T(8,128)S(1)} %get-tuple-element.28), channel_id=1, source_target_pairs={{0,4},{1,5},{2,6},{3,7},{4,0},{5,1},{6,2},{7,3},{8,12},{9,13},{10,... | collective-permute-start | bytes 835592 | tf_op jit(solution)/shard_map/ppermute | solution.py:428
  15.7 2.8 %take_slots_11.1 = f32[544,128]{1,0:T(8,128)S(1)} custom-call(s32[8]{0:T(128)S(1)} %stack.26.pos_ref.refs_0_, s32[4,128]{1,0:T(4,128)S(1)} %get-tuple-element.23.refs_1_, f32[8576,128]{1,0:T(8,128)S(1)} %get-tuple-element.24.refs_2_, f32[536,128]{1,0:T(8,128)S(1)} %get-tuple-element.25.refs_3_, s32[256,128]{1,0:T(8,128)S(1)} %get-tuple-element.32.refs_4_), custom_call_target="tpu_custom_call" | custom-call | flops 1000000 | bytes 1000000 | tf_op jit(solution)/shard_map/take_slots_11/pallas_call | solution.py:306
  18.5 0.1 collective-permute-start.1
  18.6 0.0 collective-permute-done
  18.6 3.8 %collective-permute-start.2 = (f32[544,128]{1,0:T(8,128)S(1)}, f32[544,128]{1,0:T(8,128)S(1)}, u32[]{:S(2)}, u32[]{:S(2)}) collective-permute-start(f32[544,128]{1,0:T(8,128)S(1)} %add.28), channel_id=1, source_target_pairs={{0,2},{1,3},{2,0},{3,1},{4,6},{5,7},{6,4},{7,5},{8,10},{9,11},{10,... | collective-permute-start | bytes 835592 | tf_op jit(solution)/shard_map/ppermute | solution.py:428
  22.4 2.8 %take_slots_10.1 = f32[544,128]{1,0:T(8,128)S(1)} custom-call(s32[8]{0:T(128)S(1)} %stack.26.pos_ref.refs_0_, s32[4,128]{1,0:T(4,128)S(1)} %get-tuple-element.23.refs_1_, f32[8576,128]{1,0:T(8,128)S(1)} %get-tuple-element.24.refs_2_, f32[536,128]{1,0:T(8,128)S(1)} %get-tuple-element.25.refs_3_, s32[256,128]{1,0:T(8,128)S(1)} %get-tuple-element.32.refs_4_), custom_call_target="tpu_custom_call" | custom-call | flops 1000000 | bytes 1000000 | tf_op jit(solution)/shard_map/take_slots_10/pallas_call | solution.py:306
  25.2 0.0 collective-permute-done.1
  25.2 2.8 %take_slots_31.1 = f32[544,128]{1,0:T(8,128)S(1)} custom-call(s32[8]{0:T(128)S(1)} %stack.26.pos_ref.refs_0_, s32[4,128]{1,0:T(4,128)S(1)} %get-tuple-element.23.refs_1_, f32[8576,128]{1,0:T(8,128)S(1)} %get-tuple-element.24.refs_2_, f32[536,128]{1,0:T(8,128)S(1)} %get-tuple-element.25.refs_3_, s32[256,128]{1,0:T(8,128)S(1)} %get-tuple-element.32.refs_4_), custom_call_target="tpu_custom_call" | custom-call | flops 1000000 | bytes 1000000 | tf_op jit(solution)/shard_map/take_slots_31/pallas_call | solution.py:306
  28.0 0.8 %collective-permute-start.3 = (f32[544,128]{1,0:T(8,128)S(1)}, f32[544,128]{1,0:T(8,128)S(1)}, u32[]{:S(2)}, u32[]{:S(2)}) collective-permute-start(f32[544,128]{1,0:T(8,128)S(1)} %take_slots_31.1), channel_id=1, source_target_pairs={{0,4},{1,5},{2,6},{3,7},{4,0},{5,1},{6,2},{7,3},{8,12},{9,13},{10,... | collective-permute-start | bytes 835592 | tf_op jit(solution)/shard_map/ppermute | solution.py:428
  28.8 0.4 collective-permute-start.4
  29.3 0.0 collective-permute-done.2.refs_2_
  29.3 2.8 %take_slots_30.1 = f32[544,128]{1,0:T(8,128)S(1)} custom-call(s32[8]{0:T(128)S(1)} %stack.26.pos_ref.refs_0_, s32[4,128]{1,0:T(4,128)S(1)} %get-tuple-element.23.refs_1_, f32[8576,128]{1,0:T(8,128)S(1)} %get-tuple-element.24.refs_2_, f32[536,128]{1,0:T(8,128)S(1)} %get-tuple-element.25.refs_3_, s32[256,128]{1,0:T(8,128)S(1)} %get-tuple-element.32.refs_4_), custom_call_target="tpu_custom_call" | custom-call | flops 1000000 | bytes 1000000 | tf_op jit(solution)/shard_map/take_slots_30/pallas_call | solution.py:306
  32.1 0.0 copy-start
  32.1 0.0 collective-permute-done.3
  32.1 1.1 %collective-permute-start.5 = (f32[544,128]{1,0:T(8,128)S(1)}, f32[544,128]{1,0:T(8,128)S(1)}, u32[]{:S(2)}, u32[]{:S(2)}) collective-permute-start(f32[544,128]{1,0:T(8,128)S(1)} %add.30), channel_id=1, source_target_pairs={{0,3},{1,0},{2,1},{3,2},{4,5},{5,6},{6,7},{7,4},{8,11},{9,8},{10,9... | collective-permute-start | bytes 835592 | tf_op jit(solution)/shard_map/ppermute | solution.py:428
  33.2 5.0 %take_slots_001.1 = (f32[544,128]{1,0:T(8,128)S(1)}, f32[544,128]{1,0:T(8,128)S(1)}) custom-call(s32[8]{0:T(128)S(1)} %stack.26.pos_ref.refs_0_, s32[4,128]{1,0:T(4,128)S(1)} %get-tuple-element.23.refs_1_, f32[8576,128]{1,0:T(8,128)S(1)} %get-tuple-element.24.refs_2_, f32[536,128]{1,0:T(8,128)S(1)} %get-tuple-element.25.refs_3_, ...), custom_call_target="tpu_custom_call" | custom-call | flops 1000000 | bytes 1000000 | tf_op jit(solution)/shard_map/take_slots_001/pallas_call | solution.py:306
  38.3 3.3 %collective-permute-start.6 = (f32[544,128]{1,0:T(8,128)S(1)}, f32[544,128]{1,0:T(8,128)S(1)}, u32[]{:S(2)}, u32[]{:S(2)}) collective-permute-start(f32[544,128]{1,0:T(8,128)S(1)} %get-tuple-element.35), channel_id=1, source_target_pairs={{0,4},{1,5},{2,6},{3,7},{4,0},{5,1},{6,2},{7,3},{8,12},{9,13},{10,... | collective-permute-start | bytes 835592 | tf_op jit(solution)/shard_map/ppermute | solution.py:428
  41.6 0.0 collective-permute-done.4.refs_3_
  41.6 0.0 collective-permute-done.5.refs_4_
  41.6 1.2 %collective-permute-done.6 = f32[544,128]{1,0:T(8,128)S(1)} collective-permute-done((f32[544,128]{1,0:T(8,128)S(1)}, f32[544,128]{1,0:T(8,128)S(1)}, u32[]{:S(2)}, u32[]{:S(2)}) %collective-permute-start.6) | collective-permute-done | bytes 278560 | tf_op jit(solution)/shard_map/ppermute | solution.py:428
  42.8 2.6 %given_order_far.1 = (f32[544,128]{1,0:T(8,128)S(1)}, f32[136,128]{1,0:T(8,128)S(1)}, f32[136,128]{1,0:T(8,128)S(1)}, f32[136,128]{1,0:T(8,128)S(1)}) custom-call(s32[8]{0:T(128)S(1)} %stack.26.pos_ref.refs_0_, s32[128,128]{1,0:T(8,128)S(1)} %get-tuple-element.34.refs_1_, f32[544,128]{1,0:T(8,128)S(1)} %collective-permute-done.2.refs_2_, ...), custom_call_target="tpu_custom_call" | custom-call | flops 1000000 | bytes 1000000 | tf_op jit(solution)/shard_map/given_order_far/pallas_call | solution.py:353
  45.4 3.0 %collective-permute-start.7 = (f32[136,128]{1,0:T(8,128)S(1)}, f32[136,128]{1,0:T(8,128)S(1)}, u32[]{:S(2)}, u32[]{:S(2)}) collective-permute-start(f32[136,128]{1,0:T(8,128)S(1)} %get-tuple-element.37), channel_id=1, source_target_pairs={{0,64},{1,65},{2,66},{3,67},{4,68},{5,69},{6,70},{7,71},{8,72},{9,... | collective-permute-start | bytes 208904 | tf_op jit(solution)/shard_map/ppermute | solution.py:428
  48.4 0.8 collective-permute-start.8
  49.2 0.7 collective-permute-start.9
  49.9 1.3 %given_order_own.1 = f32[136,128]{1,0:T(8,128)S(1)} custom-call(s32[8]{0:T(128)S(1)} %stack.26.pos_ref.refs_0_, s32[128,128]{1,0:T(8,128)S(1)} %get-tuple-element.34.refs_1_, f32[544,128]{1,0:T(8,128)S(1)} %get-tuple-element.36.refs_2_), custom_call_target="tpu_custom_call" | custom-call | flops 1000000 | bytes 1000000 | tf_op jit(solution)/shard_map/given_order_own/pallas_call | solution.py:353
  51.2 0.0 collective-permute-done.7
  51.2 0.9 %collective-permute-done.8 = f32[136,128]{1,0:T(8,128)S(1)} collective-permute-done((f32[136,128]{1,0:T(8,128)S(1)}, f32[136,128]{1,0:T(8,128)S(1)}, u32[]{:S(2)}, u32[]{:S(2)}) %collective-permute-start.8) | collective-permute-done | bytes 69664 | tf_op jit(solution)/shard_map/ppermute | solution.py:428
  52.1 2.2 %collective-permute-done.9 = f32[136,128]{1,0:T(8,128)S(1)} collective-permute-done((f32[136,128]{1,0:T(8,128)S(1)}, f32[136,128]{1,0:T(8,128)S(1)}, u32[]{:S(2)}, u32[]{:S(2)}) %collective-permute-start.9) | collective-permute-done | bytes 69664 | tf_op jit(solution)/shard_map/ppermute | solution.py:428
  54.3 1.3 %collective-permute-start.12 = (f32[136,128]{1,0:T(8,128)S(1)}, f32[136,128]{1,0:T(8,128)S(1)}, u32[]{:S(2)}, u32[]{:S(2)}) collective-permute-start(f32[136,128]{1,0:T(8,128)S(1)} %add_add_fusion.refs_2_), channel_id=1, source_target_pairs={{0,24},{1,25},{2,26},{3,27},{4,12},{5,13},{6,14},{7,15},{8,0},{9,1... | collective-permute-start | bytes 208904 | tf_op jit(solution)/shard_map/ppermute | solution.py:428
  55.6 1.5 %collective-permute-start.11 = (f32[136,128]{1,0:T(8,128)S(1)}, f32[136,128]{1,0:T(8,128)S(1)}, u32[]{:S(2)}, u32[]{:S(2)}) collective-permute-start(f32[136,128]{1,0:T(8,128)S(1)} %add_add_fusion.refs_2_), channel_id=1, source_target_pairs={{0,8},{1,9},{2,10},{3,11},{4,28},{5,29},{6,30},{7,31},{8,16},{9,17... | collective-permute-start | bytes 208904 | tf_op jit(solution)/shard_map/ppermute | solution.py:428
  57.0 1.5 %collective-permute-start.10 = (f32[136,128]{1,0:T(8,128)S(1)}, f32[136,128]{1,0:T(8,128)S(1)}, u32[]{:S(2)}, u32[]{:S(2)}) collective-permute-start(f32[136,128]{1,0:T(8,128)S(1)} %add_add_fusion.refs_2_), channel_id=1, source_target_pairs={{0,16},{1,17},{2,18},{3,19},{4,20},{5,21},{6,22},{7,23},{8,24},{9,... | collective-permute-start | bytes 208904 | tf_op jit(solution)/shard_map/ppermute | solution.py:428
  58.6 0.2 collective-permute-done.12.refs_5_
  58.7 1.0 %collective-permute-done.11.refs_4_ = f32[136,128]{1,0:T(8,128)S(1)} collective-permute-done((f32[136,128]{1,0:T(8,128)S(1)}, f32[136,128]{1,0:T(8,128)S(1)}, u32[]{:S(2)}, u32[]{:S(2)}) %collective-permute-start.11) | collective-permute-done | bytes 69664 | tf_op jit(solution)/shard_map/ppermute | solution.py:428
  59.8 2.6 %collective-permute-done.10.refs_3_ = f32[136,128]{1,0:T(8,128)S(1)} collective-permute-done((f32[136,128]{1,0:T(8,128)S(1)}, f32[136,128]{1,0:T(8,128)S(1)}, u32[]{:S(2)}, u32[]{:S(2)}) %collective-permute-start.10) | collective-permute-done | bytes 69664 | tf_op jit(solution)/shard_map/ppermute | solution.py:428
  62.4 0.0 copy-done
  62.4 1.4 %rows_and_gram.1 = (f32[17,256]{1,0:T(8,128)}, f32[4,8,128]{2,1,0:T(8,128)S(1)}) custom-call(s32[8]{0:T(128)S(1)} %stack.26.pos_ref.refs_0_, s32[16,2,8,128]{3,2,1,0:T(8,128)S(1)} %bitcast.15, f32[136,128]{1,0:T(8,128)S(1)} %add_add_fusion.refs_2_, f32[136,128]{1,0:T(8,128)S(1)} %collective-permute-done.10.refs_3_, ...), custom_call_target="tpu_custom_call" | custom-call | tf_op jit(solution)/shard_map/rows_and_gram/pallas_call | solution.py:395
  63.8 2.0 %collective-permute-start.13 = (f32[4,8,128]{2,1,0:T(8,128)S(1)}, f32[4,8,128]{2,1,0:T(8,128)S(1)}, u32[]{:S(2)}, u32[]{:S(2)}) collective-permute-start(f32[4,8,128]{2,1,0:T(8,128)S(1)} %get-tuple-element.41), channel_id=1, source_target_pairs={{0,4},{1,5},{2,6},{3,7},{4,0},{5,1},{6,2},{7,3},{8,12},{9,13},{10,... | collective-permute-start | bytes 49160 | tf_op jit(solution)/shard_map/ppermute | solution.py:428
  65.7 0.8 %collective-permute-done.13 = f32[4,8,128]{2,1,0:T(8,128)S(1)} collective-permute-done((f32[4,8,128]{2,1,0:T(8,128)S(1)}, f32[4,8,128]{2,1,0:T(8,128)S(1)}, u32[]{:S(2)}, u32[]{:S(2)}) %collective-permute-start.13) | collective-permute-done | bytes 16416 | tf_op jit(solution)/shard_map/ppermute | solution.py:428
  66.6 10.4 %all_to_all.5.messages = f32[16,8,128]{2,1,0:T(8,128)S(1)} all-to-all(f32[16,8,128]{2,1,0:T(8,128)S(1)} %pad_maximum_fusion), channel_id=1, replica_groups={{0,1,2,3,32,33,34,35,64,65,66,67,96,97,98,99},{4,5,6,7,36,37,38,39,68,6..., dimensions={0} | all-to-all | bytes 131072 | tf_op jit(solution)/shard_map/all_to_all | solution.py:483
  77.0 0.8 own_gram.1
  (7 shorter events, 0.2 us)
Async XLA Ops:
  14.2 4.4 %collective-permute-start = (f32[544,128]{1,0:T(8,128)S(1)}, f32[544,128]{1,0:T(8,128)S(1)}, u32[]{:S(2)}, u32[]{:S(2)}) collective-permute-start(f32[544,128]{1,0:T(8,128)S(1)} %get-tuple-element.28), channel_id=1, source_target_pairs={{0,4},{1,5},{2,6},{3,7},{4,0},{5,1},{6,2},{7,3},{8,12},{9,13},{10,... | collective-permute-start | bytes 835592 | tf_op jit(solution)/shard_map/ppermute | solution.py:428
  18.5 6.7 %collective-permute-start.1 = (f32[544,128]{1,0:T(8,128)S(1)}, f32[544,128]{1,0:T(8,128)S(1)}, u32[]{:S(2)}, u32[]{:S(2)}) collective-permute-start(f32[544,128]{1,0:T(8,128)S(1)} %take_slots_11.1), channel_id=1, source_target_pairs={{0,4},{1,5},{2,6},{3,7},{4,0},{5,1},{6,2},{7,3},{8,12},{9,13},{10,... | collective-permute-start | bytes 835592 | tf_op jit(solution)/shard_map/ppermute | solution.py:428
  18.6 10.7 %collective-permute-start.2 = (f32[544,128]{1,0:T(8,128)S(1)}, f32[544,128]{1,0:T(8,128)S(1)}, u32[]{:S(2)}, u32[]{:S(2)}) collective-permute-start(f32[544,128]{1,0:T(8,128)S(1)} %add.28), channel_id=1, source_target_pairs={{0,2},{1,3},{2,0},{3,1},{4,6},{5,7},{6,4},{7,5},{8,10},{9,11},{10,... | collective-permute-start | bytes 835592 | tf_op jit(solution)/shard_map/ppermute | solution.py:428
  28.0 4.1 %collective-permute-start.3 = (f32[544,128]{1,0:T(8,128)S(1)}, f32[544,128]{1,0:T(8,128)S(1)}, u32[]{:S(2)}, u32[]{:S(2)}) collective-permute-start(f32[544,128]{1,0:T(8,128)S(1)} %take_slots_31.1), channel_id=1, source_target_pairs={{0,4},{1,5},{2,6},{3,7},{4,0},{5,1},{6,2},{7,3},{8,12},{9,13},{10,... | collective-permute-start | bytes 835592 | tf_op jit(solution)/shard_map/ppermute | solution.py:428
  28.8 12.7 %collective-permute-start.4 = (f32[544,128]{1,0:T(8,128)S(1)}, f32[544,128]{1,0:T(8,128)S(1)}, u32[]{:S(2)}, u32[]{:S(2)}) collective-permute-start(f32[544,128]{1,0:T(8,128)S(1)} %add.29), channel_id=1, source_target_pairs={{0,1},{1,2},{2,3},{3,0},{4,7},{5,4},{6,5},{7,6},{8,9},{9,10},{10,1... | collective-permute-start | bytes 835592 | tf_op jit(solution)/shard_map/ppermute | solution.py:428
  32.1 30.3 %copy-start = (s32[32768]{0:T(1024)S(1)}, s32[32768]{0:T(1024)}, u32[]{:S(2)}) copy-start(s32[32768]{0:T(1024)} %param.9) | copy-start | bytes 393220
  32.1 9.4 %collective-permute-start.5 = (f32[544,128]{1,0:T(8,128)S(1)}, f32[544,128]{1,0:T(8,128)S(1)}, u32[]{:S(2)}, u32[]{:S(2)}) collective-permute-start(f32[544,128]{1,0:T(8,128)S(1)} %add.30), channel_id=1, source_target_pairs={{0,3},{1,0},{2,1},{3,2},{4,5},{5,6},{6,7},{7,4},{8,11},{9,8},{10,9... | collective-permute-start | bytes 835592 | tf_op jit(solution)/shard_map/ppermute | solution.py:428
  38.3 4.5 %collective-permute-start.6 = (f32[544,128]{1,0:T(8,128)S(1)}, f32[544,128]{1,0:T(8,128)S(1)}, u32[]{:S(2)}, u32[]{:S(2)}) collective-permute-start(f32[544,128]{1,0:T(8,128)S(1)} %get-tuple-element.35), channel_id=1, source_target_pairs={{0,4},{1,5},{2,6},{3,7},{4,0},{5,1},{6,2},{7,3},{8,12},{9,13},{10,... | collective-permute-start | bytes 835592 | tf_op jit(solution)/shard_map/ppermute | solution.py:428
  45.4 5.7 %collective-permute-start.7 = (f32[136,128]{1,0:T(8,128)S(1)}, f32[136,128]{1,0:T(8,128)S(1)}, u32[]{:S(2)}, u32[]{:S(2)}) collective-permute-start(f32[136,128]{1,0:T(8,128)S(1)} %get-tuple-element.37), channel_id=1, source_target_pairs={{0,64},{1,65},{2,66},{3,67},{4,68},{5,69},{6,70},{7,71},{8,72},{9,... | collective-permute-start | bytes 208904 | tf_op jit(solution)/shard_map/ppermute | solution.py:428
  48.4 3.7 %collective-permute-start.8 = (f32[136,128]{1,0:T(8,128)S(1)}, f32[136,128]{1,0:T(8,128)S(1)}, u32[]{:S(2)}, u32[]{:S(2)}) collective-permute-start(f32[136,128]{1,0:T(8,128)S(1)} %get-tuple-element.38), channel_id=1, source_target_pairs={{0,32},{1,33},{2,34},{3,35},{4,100},{5,101},{6,102},{7,103},{8,40}... | collective-permute-start | bytes 208904 | tf_op jit(solution)/shard_map/ppermute | solution.py:428
  49.2 5.1 %collective-permute-start.9 = (f32[136,128]{1,0:T(8,128)S(1)}, f32[136,128]{1,0:T(8,128)S(1)}, u32[]{:S(2)}, u32[]{:S(2)}) collective-permute-start(f32[136,128]{1,0:T(8,128)S(1)} %get-tuple-element.39), channel_id=1, source_target_pairs={{0,96},{1,97},{2,98},{3,99},{4,36},{5,37},{6,38},{7,39},{8,104},{9... | collective-permute-start | bytes 208904 | tf_op jit(solution)/shard_map/ppermute | solution.py:428
  54.3 4.4 %collective-permute-start.12 = (f32[136,128]{1,0:T(8,128)S(1)}, f32[136,128]{1,0:T(8,128)S(1)}, u32[]{:S(2)}, u32[]{:S(2)}) collective-permute-start(f32[136,128]{1,0:T(8,128)S(1)} %add_add_fusion.refs_2_), channel_id=1, source_target_pairs={{0,24},{1,25},{2,26},{3,27},{4,12},{5,13},{6,14},{7,15},{8,0},{9,1... | collective-permute-start | bytes 208904 | tf_op jit(solution)/shard_map/ppermute | solution.py:428
  55.6 4.2 %collective-permute-start.11 = (f32[136,128]{1,0:T(8,128)S(1)}, f32[136,128]{1,0:T(8,128)S(1)}, u32[]{:S(2)}, u32[]{:S(2)}) collective-permute-start(f32[136,128]{1,0:T(8,128)S(1)} %add_add_fusion.refs_2_), channel_id=1, source_target_pairs={{0,8},{1,9},{2,10},{3,11},{4,28},{5,29},{6,30},{7,31},{8,16},{9,17... | collective-permute-start | bytes 208904 | tf_op jit(solution)/shard_map/ppermute | solution.py:428
  57.0 5.4 %collective-permute-start.10 = (f32[136,128]{1,0:T(8,128)S(1)}, f32[136,128]{1,0:T(8,128)S(1)}, u32[]{:S(2)}, u32[]{:S(2)}) collective-permute-start(f32[136,128]{1,0:T(8,128)S(1)} %add_add_fusion.refs_2_), channel_id=1, source_target_pairs={{0,16},{1,17},{2,18},{3,19},{4,20},{5,21},{6,22},{7,23},{8,24},{9,... | collective-permute-start | bytes 208904 | tf_op jit(solution)/shard_map/ppermute | solution.py:428
  63.8 2.8 %collective-permute-start.13 = (f32[4,8,128]{2,1,0:T(8,128)S(1)}, f32[4,8,128]{2,1,0:T(8,128)S(1)}, u32[]{:S(2)}, u32[]{:S(2)}) collective-permute-start(f32[4,8,128]{2,1,0:T(8,128)S(1)} %get-tuple-element.41), channel_id=1, source_target_pairs={{0,4},{1,5},{2,6},{3,7},{4,0},{5,1},{6,2},{7,3},{8,12},{9,13},{10,... | collective-permute-start | bytes 49160 | tf_op jit(solution)/shard_map/ppermute | solution.py:428

commit v7 on v6

--- a/solution.py
+++ b/solution.py
@@ -14,6 +14,7 @@
 SIDE = 256
 FETCHED = 36
 PEEL = 20
+OTHER = (0, 2, 3, 1)
 STEP = 4
 EIGHTHS = 4
 ROWS = 512
@@ -33,13 +34,13 @@
                     at = {"y": y, "x": x, "c": c, "z": z}
                     size = 2 if axis == "c" else 4
                     to = dict(at)
-                    to[axis] = (at[axis] + (-off if c else off)) % size
+                    to[axis] = (at[axis] + (OTHER[off] if c and axis != "c" else off)) % size
                     pairs.append((number(**at), number(**to)))
     return pairs
 
 
 def away(core, off):
-    return jnp.where(core == 0, off, -off)
+    return jnp.where(core == 0, off, OTHER[off])
 
 
 def fold(v):

time: 78.3 us -> 77.8 us (level)
  waiting for transfers between devices: 8.94 us -> 8.1 us
    ppermute x14, waiting for transfers between devices: 8.94 us -> 8.1 us  [send(): return lax.ppermute(v, AXES, shift(axis, off))]
  transfers between devices with their start and end apart: 14 -> 14, of which waited for: 7 -> 7; matrix products, arithmetic and copies ran while one was open for 0% -> 0% of each run, Pallas kernels for 22% -> 23%
where the time goes in v7:
time: 77.8 us; the launch traced here: 77.2 us
  Pallas kernels  35.9 us (46%)
  starting transfers between devices  21.2 us (27%)
  blocking collectives  11 us (14%)
  waiting for transfers between devices  8.1 us (10%)
  between operations  0.78 us (1%)
    pallas_call x6, Pallas kernels, slots_call(): pl.pallas_call(lambda *refs: slots_kernel(scale, off, cores, *refs), out_...  21.4 us
    ppermute x14, starting transfers between devices, send(): return lax.ppermute(v, AXES, shift(axis, off))  21.2 us
    all_to_all x1, blocking collectives, shards(): lax.all_to_all(gram, AXES, 0, 0, tiled=True, axis_index_groups=planes())  11 us
    pallas_call x1, Pallas kernels, prepare_call(): pl.pallas_call(prepare_kernel, out_shape=(jax.ShapeDtypeStruct((256, LANE...  8.41 us
    ppermute x14, waiting for transfers between devices, send(): return lax.ppermute(v, AXES, shift(axis, off))  8.1 us
    pallas_call x2, Pallas kernels, order_call(): pl.pallas_call(lambda *refs: kernel(rel, *refs), out_shape=(table,) + (ou...  3.9 us
  transfers between devices with their start and end apart: 14, of which 7 were waited for; matrix products, arithmetic and copies ran while one was open for 0% of the time, Pallas kernels for 23%

profile of v7, /device:TPU:1, one launch (start us, length us, event | category | flops | bytes accessed | tf_op | source)
XLA Modules:
  0.0 77.2 jit_solution(11084165278277117433)
XLA Ops:
  0.6 0.1 stack.26.pos_ref.refs_0_
  0.7 8.4 %sort_and_walsh.1 = (s32[256,128]{1,0:T(8,128)S(1)}, s32[4,128]{1,0:T(4,128)S(1)}, s32[128,128]{1,0:T(8,128)S(1)}, f32[8576,128]{1,0:T(8,128)S(1)}, f32[536,128]{1,0:T(8,128)S(1)}) custom-call(s32[8]{0:T(128)S(1)} %stack.26.pos_ref.refs_0_, s32[16,2,8,128]{3,2,1,0:T(8,128)} %bitcast.19, f32[8192,128]{1,0:T(8,128)} %bitcast.16, f32[512,128]{1,0:T(8,128)} %bitcast.17, ...), custom_call_target="tpu_custom_call" | custom-call | flops 1000000 | bytes 1000000 | tf_op jit(solution)/shard_map/sort_and_walsh/pallas_call | solution.py:218
  9.1 5.1 %take_slots_201.1 = (f32[544,128]{1,0:T(8,128)S(1)}, f32[544,128]{1,0:T(8,128)S(1)}) custom-call(s32[8]{0:T(128)S(1)} %stack.26.pos_ref.refs_0_, s32[4,128]{1,0:T(4,128)S(1)} %get-tuple-element.23.refs_1_, f32[8576,128]{1,0:T(8,128)S(1)} %get-tuple-element.24.refs_2_, f32[536,128]{1,0:T(8,128)S(1)} %get-tuple-element.25.refs_3_, ...), custom_call_target="tpu_custom_call" | custom-call | flops 1000000 | bytes 1000000 | tf_op jit(solution)/shard_map/take_slots_201/pallas_call | solution.py:307
  14.3 1.5 %collective-permute-start = (f32[544,128]{1,0:T(8,128)S(1)}, f32[544,128]{1,0:T(8,128)S(1)}, u32[]{:S(2)}, u32[]{:S(2)}) collective-permute-start(f32[544,128]{1,0:T(8,128)S(1)} %get-tuple-element.28), channel_id=1, source_target_pairs={{0,4},{1,5},{2,6},{3,7},{4,0},{5,1},{6,2},{7,3},{8,12},{9,13},{10,... | collective-permute-start | bytes 835592 | tf_op jit(solution)/shard_map/ppermute | solution.py:429
  15.8 2.8 %take_slots_11.1 = f32[544,128]{1,0:T(8,128)S(1)} custom-call(s32[8]{0:T(128)S(1)} %stack.26.pos_ref.refs_0_, s32[4,128]{1,0:T(4,128)S(1)} %get-tuple-element.23.refs_1_, f32[8576,128]{1,0:T(8,128)S(1)} %get-tuple-element.24.refs_2_, f32[536,128]{1,0:T(8,128)S(1)} %get-tuple-element.25.refs_3_, s32[256,128]{1,0:T(8,128)S(1)} %get-tuple-element.32.refs_4_), custom_call_target="tpu_custom_call" | custom-call | flops 1000000 | bytes 1000000 | tf_op jit(solution)/shard_map/take_slots_11/pallas_call | solution.py:307
  18.6 0.1 collective-permute-start.1
  18.7 0.0 collective-permute-done
  18.7 3.8 %collective-permute-start.2 = (f32[544,128]{1,0:T(8,128)S(1)}, f32[544,128]{1,0:T(8,128)S(1)}, u32[]{:S(2)}, u32[]{:S(2)}) collective-permute-start(f32[544,128]{1,0:T(8,128)S(1)} %add.28), channel_id=1, source_target_pairs={{0,2},{1,3},{2,0},{3,1},{4,7},{5,4},{6,5},{7,6},{8,10},{9,11},{10,... | collective-permute-start | bytes 835592 | tf_op jit(solution)/shard_map/ppermute | solution.py:429
  22.5 2.8 %take_slots_10.1 = f32[544,128]{1,0:T(8,128)S(1)} custom-call(s32[8]{0:T(128)S(1)} %stack.26.pos_ref.refs_0_, s32[4,128]{1,0:T(4,128)S(1)} %get-tuple-element.23.refs_1_, f32[8576,128]{1,0:T(8,128)S(1)} %get-tuple-element.24.refs_2_, f32[536,128]{1,0:T(8,128)S(1)} %get-tuple-element.25.refs_3_, s32[256,128]{1,0:T(8,128)S(1)} %get-tuple-element.32.refs_4_), custom_call_target="tpu_custom_call" | custom-call | flops 1000000 | bytes 1000000 | tf_op jit(solution)/shard_map/take_slots_10/pallas_call | solution.py:307
  25.3 0.0 collective-permute-done.1
  25.4 2.8 %take_slots_31.1 = f32[544,128]{1,0:T(8,128)S(1)} custom-call(s32[8]{0:T(128)S(1)} %stack.26.pos_ref.refs_0_, s32[4,128]{1,0:T(4,128)S(1)} %get-tuple-element.23.refs_1_, f32[8576,128]{1,0:T(8,128)S(1)} %get-tuple-element.24.refs_2_, f32[536,128]{1,0:T(8,128)S(1)} %get-tuple-element.25.refs_3_, s32[256,128]{1,0:T(8,128)S(1)} %get-tuple-element.32.refs_4_), custom_call_target="tpu_custom_call" | custom-call | flops 1000000 | bytes 1000000 | tf_op jit(solution)/shard_map/take_slots_31/pallas_call | solution.py:307
  28.2 0.7 collective-permute-start.3
  28.8 0.0 collective-permute-start.4
  28.8 0.1 collective-permute-done.2.refs_2_
  29.0 2.8 %take_slots_30.1 = f32[544,128]{1,0:T(8,128)S(1)} custom-call(s32[8]{0:T(128)S(1)} %stack.26.pos_ref.refs_0_, s32[4,128]{1,0:T(4,128)S(1)} %get-tuple-element.23.refs_1_, f32[8576,128]{1,0:T(8,128)S(1)} %get-tuple-element.24.refs_2_, f32[536,128]{1,0:T(8,128)S(1)} %get-tuple-element.25.refs_3_, s32[256,128]{1,0:T(8,128)S(1)} %get-tuple-element.32.refs_4_), custom_call_target="tpu_custom_call" | custom-call | flops 1000000 | bytes 1000000 | tf_op jit(solution)/shard_map/take_slots_30/pallas_call | solution.py:307
  31.8 0.0 copy-start
  31.8 0.0 collective-permute-done.3
  31.8 1.2 %collective-permute-start.5 = (f32[544,128]{1,0:T(8,128)S(1)}, f32[544,128]{1,0:T(8,128)S(1)}, u32[]{:S(2)}, u32[]{:S(2)}) collective-permute-start(f32[544,128]{1,0:T(8,128)S(1)} %add.30), channel_id=1, source_target_pairs={{0,3},{1,0},{2,1},{3,2},{4,5},{5,6},{6,7},{7,4},{8,11},{9,8},{10,9... | collective-permute-start | bytes 835592 | tf_op jit(solution)/shard_map/ppermute | solution.py:429
  33.0 5.1 %take_slots_001.1 = (f32[544,128]{1,0:T(8,128)S(1)}, f32[544,128]{1,0:T(8,128)S(1)}) custom-call(s32[8]{0:T(128)S(1)} %stack.26.pos_ref.refs_0_, s32[4,128]{1,0:T(4,128)S(1)} %get-tuple-element.23.refs_1_, f32[8576,128]{1,0:T(8,128)S(1)} %get-tuple-element.24.refs_2_, f32[536,128]{1,0:T(8,128)S(1)} %get-tuple-element.25.refs_3_, ...), custom_call_target="tpu_custom_call" | custom-call | flops 1000000 | bytes 1000000 | tf_op jit(solution)/shard_map/take_slots_001/pallas_call | solution.py:307
  38.2 2.3 %collective-permute-start.6 = (f32[544,128]{1,0:T(8,128)S(1)}, f32[544,128]{1,0:T(8,128)S(1)}, u32[]{:S(2)}, u32[]{:S(2)}) collective-permute-start(f32[544,128]{1,0:T(8,128)S(1)} %get-tuple-element.35), channel_id=1, source_target_pairs={{0,4},{1,5},{2,6},{3,7},{4,0},{5,1},{6,2},{7,3},{8,12},{9,13},{10,... | collective-permute-start | bytes 835592 | tf_op jit(solution)/shard_map/ppermute | solution.py:429
  40.5 0.0 collective-permute-done.4.refs_3_
  40.5 1.3 %collective-permute-done.5.refs_4_ = f32[544,128]{1,0:T(8,128)S(1)} collective-permute-done((f32[544,128]{1,0:T(8,128)S(1)}, f32[544,128]{1,0:T(8,128)S(1)}, u32[]{:S(2)}, u32[]{:S(2)}) %collective-permute-start.5) | collective-permute-done | bytes 278560 | tf_op jit(solution)/shard_map/ppermute | solution.py:429
  41.8 0.0 collective-permute-done.6
  41.8 2.6 %given_order_far.1 = (f32[544,128]{1,0:T(8,128)S(1)}, f32[136,128]{1,0:T(8,128)S(1)}, f32[136,128]{1,0:T(8,128)S(1)}, f32[136,128]{1,0:T(8,128)S(1)}) custom-call(s32[8]{0:T(128)S(1)} %stack.26.pos_ref.refs_0_, s32[128,128]{1,0:T(8,128)S(1)} %get-tuple-element.34.refs_1_, f32[544,128]{1,0:T(8,128)S(1)} %collective-permute-done.2.refs_2_, ...), custom_call_target="tpu_custom_call" | custom-call | flops 1000000 | bytes 1000000 | tf_op jit(solution)/shard_map/given_order_far/pallas_call | solution.py:354
  44.5 2.8 %collective-permute-start.7 = (f32[136,128]{1,0:T(8,128)S(1)}, f32[136,128]{1,0:T(8,128)S(1)}, u32[]{:S(2)}, u32[]{:S(2)}) collective-permute-start(f32[136,128]{1,0:T(8,128)S(1)} %get-tuple-element.37), channel_id=1, source_target_pairs={{0,64},{1,65},{2,66},{3,67},{4,100},{5,101},{6,102},{7,103},{8,72}... | collective-permute-start | bytes 208904 | tf_op jit(solution)/shard_map/ppermute | solution.py:429
  47.3 0.4 collective-permute-start.8
  47.6 0.7 collective-permute-start.9
  48.3 1.3 %given_order_own.1 = f32[136,128]{1,0:T(8,128)S(1)} custom-call(s32[8]{0:T(128)S(1)} %stack.26.pos_ref.refs_0_, s32[128,128]{1,0:T(8,128)S(1)} %get-tuple-element.34.refs_1_, f32[544,128]{1,0:T(8,128)S(1)} %get-tuple-element.36.refs_2_), custom_call_target="tpu_custom_call" | custom-call | flops 1000000 | bytes 1000000 | tf_op jit(solution)/shard_map/given_order_own/pallas_call | solution.py:354
  49.6 0.0 collective-permute-done.7
  49.6 2.9 %collective-permute-done.8 = f32[136,128]{1,0:T(8,128)S(1)} collective-permute-done((f32[136,128]{1,0:T(8,128)S(1)}, f32[136,128]{1,0:T(8,128)S(1)}, u32[]{:S(2)}, u32[]{:S(2)}) %collective-permute-start.8) | collective-permute-done | bytes 69664 | tf_op jit(solution)/shard_map/ppermute | solution.py:429
  52.5 0.9 %collective-permute-done.9 = f32[136,128]{1,0:T(8,128)S(1)} collective-permute-done((f32[136,128]{1,0:T(8,128)S(1)}, f32[136,128]{1,0:T(8,128)S(1)}, u32[]{:S(2)}, u32[]{:S(2)}) %collective-permute-start.9) | collective-permute-done | bytes 69664 | tf_op jit(solution)/shard_map/ppermute | solution.py:429
  53.4 1.3 %collective-permute-start.12 = (f32[136,128]{1,0:T(8,128)S(1)}, f32[136,128]{1,0:T(8,128)S(1)}, u32[]{:S(2)}, u32[]{:S(2)}) collective-permute-start(f32[136,128]{1,0:T(8,128)S(1)} %add_add_fusion.refs_2_), channel_id=1, source_target_pairs={{0,24},{1,25},{2,26},{3,27},{4,12},{5,13},{6,14},{7,15},{8,0},{9,1... | collective-permute-start | bytes 208904 | tf_op jit(solution)/shard_map/ppermute | solution.py:429
  54.7 2.5 %collective-permute-start.11 = (f32[136,128]{1,0:T(8,128)S(1)}, f32[136,128]{1,0:T(8,128)S(1)}, u32[]{:S(2)}, u32[]{:S(2)}) collective-permute-start(f32[136,128]{1,0:T(8,128)S(1)} %add_add_fusion.refs_2_), channel_id=1, source_target_pairs={{0,8},{1,9},{2,10},{3,11},{4,20},{5,21},{6,22},{7,23},{8,16},{9,17... | collective-permute-start | bytes 208904 | tf_op jit(solution)/shard_map/ppermute | solution.py:429
  57.1 1.2 %collective-permute-start.10 = (f32[136,128]{1,0:T(8,128)S(1)}, f32[136,128]{1,0:T(8,128)S(1)}, u32[]{:S(2)}, u32[]{:S(2)}) collective-permute-start(f32[136,128]{1,0:T(8,128)S(1)} %add_add_fusion.refs_2_), channel_id=1, source_target_pairs={{0,16},{1,17},{2,18},{3,19},{4,28},{5,29},{6,30},{7,31},{8,24},{9,... | collective-permute-start | bytes 208904 | tf_op jit(solution)/shard_map/ppermute | solution.py:429
  58.3 0.0 collective-permute-done.12.refs_5_
  58.3 1.3 %collective-permute-done.11.refs_4_ = f32[136,128]{1,0:T(8,128)S(1)} collective-permute-done((f32[136,128]{1,0:T(8,128)S(1)}, f32[136,128]{1,0:T(8,128)S(1)}, u32[]{:S(2)}, u32[]{:S(2)}) %collective-permute-start.11) | collective-permute-done | bytes 69664 | tf_op jit(solution)/shard_map/ppermute | solution.py:429
  59.6 0.7 collective-permute-done.10.refs_3_
  60.3 0.0 copy-done
  60.3 1.4 %rows_and_gram.1 = (f32[17,256]{1,0:T(8,128)}, f32[4,8,128]{2,1,0:T(8,128)S(1)}) custom-call(s32[8]{0:T(128)S(1)} %stack.26.pos_ref.refs_0_, s32[16,2,8,128]{3,2,1,0:T(8,128)S(1)} %bitcast.15, f32[136,128]{1,0:T(8,128)S(1)} %add_add_fusion.refs_2_, f32[136,128]{1,0:T(8,128)S(1)} %collective-permute-done.10.refs_3_, ...), custom_call_target="tpu_custom_call" | custom-call | tf_op jit(solution)/shard_map/rows_and_gram/pallas_call | solution.py:396
  61.7 2.9 %collective-permute-start.13 = (f32[4,8,128]{2,1,0:T(8,128)S(1)}, f32[4,8,128]{2,1,0:T(8,128)S(1)}, u32[]{:S(2)}, u32[]{:S(2)}) collective-permute-start(f32[4,8,128]{2,1,0:T(8,128)S(1)} %get-tuple-element.41), channel_id=1, source_target_pairs={{0,4},{1,5},{2,6},{3,7},{4,0},{5,1},{6,2},{7,3},{8,12},{9,13},{10,... | collective-permute-start | bytes 49160 | tf_op jit(solution)/shard_map/ppermute | solution.py:429
  64.6 0.8 %collective-permute-done.13 = f32[4,8,128]{2,1,0:T(8,128)S(1)} collective-permute-done((f32[4,8,128]{2,1,0:T(8,128)S(1)}, f32[4,8,128]{2,1,0:T(8,128)S(1)}, u32[]{:S(2)}, u32[]{:S(2)}) %collective-permute-start.13) | collective-permute-done | bytes 16416 | tf_op jit(solution)/shard_map/ppermute | solution.py:429
  65.5 11.0 %all_to_all.5.messages = f32[16,8,128]{2,1,0:T(8,128)S(1)} all-to-all(f32[16,8,128]{2,1,0:T(8,128)S(1)} %pad_maximum_fusion), channel_id=1, replica_groups={{0,1,2,3,32,33,34,35,64,65,66,67,96,97,98,99},{4,5,6,7,36,37,38,39,68,6..., dimensions={0} | all-to-all | bytes 131072 | tf_op jit(solution)/shard_map/all_to_all | solution.py:484
  76.5 0.8 own_gram.1
  (7 shorter events, 0.2 us)
Async XLA Ops:
  14.3 4.4 %collective-permute-start = (f32[544,128]{1,0:T(8,128)S(1)}, f32[544,128]{1,0:T(8,128)S(1)}, u32[]{:S(2)}, u32[]{:S(2)}) collective-permute-start(f32[544,128]{1,0:T(8,128)S(1)} %get-tuple-element.28), channel_id=1, source_target_pairs={{0,4},{1,5},{2,6},{3,7},{4,0},{5,1},{6,2},{7,3},{8,12},{9,13},{10,... | collective-permute-start | bytes 835592 | tf_op jit(solution)/shard_map/ppermute | solution.py:429
  18.6 6.7 %collective-permute-start.1 = (f32[544,128]{1,0:T(8,128)S(1)}, f32[544,128]{1,0:T(8,128)S(1)}, u32[]{:S(2)}, u32[]{:S(2)}) collective-permute-start(f32[544,128]{1,0:T(8,128)S(1)} %take_slots_11.1), channel_id=1, source_target_pairs={{0,4},{1,5},{2,6},{3,7},{4,0},{5,1},{6,2},{7,3},{8,12},{9,13},{10,... | collective-permute-start | bytes 835592 | tf_op jit(solution)/shard_map/ppermute | solution.py:429
  18.7 10.3 %collective-permute-start.2 = (f32[544,128]{1,0:T(8,128)S(1)}, f32[544,128]{1,0:T(8,128)S(1)}, u32[]{:S(2)}, u32[]{:S(2)}) collective-permute-start(f32[544,128]{1,0:T(8,128)S(1)} %add.28), channel_id=1, source_target_pairs={{0,2},{1,3},{2,0},{3,1},{4,7},{5,4},{6,5},{7,6},{8,10},{9,11},{10,... | collective-permute-start | bytes 835592 | tf_op jit(solution)/shard_map/ppermute | solution.py:429
  28.2 3.6 %collective-permute-start.3 = (f32[544,128]{1,0:T(8,128)S(1)}, f32[544,128]{1,0:T(8,128)S(1)}, u32[]{:S(2)}, u32[]{:S(2)}) collective-permute-start(f32[544,128]{1,0:T(8,128)S(1)} %take_slots_31.1), channel_id=1, source_target_pairs={{0,4},{1,5},{2,6},{3,7},{4,0},{5,1},{6,2},{7,3},{8,12},{9,13},{10,... | collective-permute-start | bytes 835592 | tf_op jit(solution)/shard_map/ppermute | solution.py:429
  28.8 11.7 %collective-permute-start.4 = (f32[544,128]{1,0:T(8,128)S(1)}, f32[544,128]{1,0:T(8,128)S(1)}, u32[]{:S(2)}, u32[]{:S(2)}) collective-permute-start(f32[544,128]{1,0:T(8,128)S(1)} %add.29), channel_id=1, source_target_pairs={{0,1},{1,2},{2,3},{3,0},{4,6},{5,7},{6,4},{7,5},{8,9},{9,10},{10,1... | collective-permute-start | bytes 835592 | tf_op jit(solution)/shard_map/ppermute | solution.py:429
  31.8 28.5 %copy-start = (s32[32768]{0:T(1024)S(1)}, s32[32768]{0:T(1024)}, u32[]{:S(2)}) copy-start(s32[32768]{0:T(1024)} %param.9) | copy-start | bytes 393220
  31.8 10.0 %collective-permute-start.5 = (f32[544,128]{1,0:T(8,128)S(1)}, f32[544,128]{1,0:T(8,128)S(1)}, u32[]{:S(2)}, u32[]{:S(2)}) collective-permute-start(f32[544,128]{1,0:T(8,128)S(1)} %add.30), channel_id=1, source_target_pairs={{0,3},{1,0},{2,1},{3,2},{4,5},{5,6},{6,7},{7,4},{8,11},{9,8},{10,9... | collective-permute-start | bytes 835592 | tf_op jit(solution)/shard_map/ppermute | solution.py:429
  38.2 3.6 %collective-permute-start.6 = (f32[544,128]{1,0:T(8,128)S(1)}, f32[544,128]{1,0:T(8,128)S(1)}, u32[]{:S(2)}, u32[]{:S(2)}) collective-permute-start(f32[544,128]{1,0:T(8,128)S(1)} %get-tuple-element.35), channel_id=1, source_target_pairs={{0,4},{1,5},{2,6},{3,7},{4,0},{5,1},{6,2},{7,3},{8,12},{9,13},{10,... | collective-permute-start | bytes 835592 | tf_op jit(solution)/shard_map/ppermute | solution.py:429
  44.5 5.1 %collective-permute-start.7 = (f32[136,128]{1,0:T(8,128)S(1)}, f32[136,128]{1,0:T(8,128)S(1)}, u32[]{:S(2)}, u32[]{:S(2)}) collective-permute-start(f32[136,128]{1,0:T(8,128)S(1)} %get-tuple-element.37), channel_id=1, source_target_pairs={{0,64},{1,65},{2,66},{3,67},{4,100},{5,101},{6,102},{7,103},{8,72}... | collective-permute-start | bytes 208904 | tf_op jit(solution)/shard_map/ppermute | solution.py:429
  47.3 5.2 %collective-permute-start.8 = (f32[136,128]{1,0:T(8,128)S(1)}, f32[136,128]{1,0:T(8,128)S(1)}, u32[]{:S(2)}, u32[]{:S(2)}) collective-permute-start(f32[136,128]{1,0:T(8,128)S(1)} %get-tuple-element.38), channel_id=1, source_target_pairs={{0,32},{1,33},{2,34},{3,35},{4,68},{5,69},{6,70},{7,71},{8,40},{9,... | collective-permute-start | bytes 208904 | tf_op jit(solution)/shard_map/ppermute | solution.py:429
  47.6 5.8 %collective-permute-start.9 = (f32[136,128]{1,0:T(8,128)S(1)}, f32[136,128]{1,0:T(8,128)S(1)}, u32[]{:S(2)}, u32[]{:S(2)}) collective-permute-start(f32[136,128]{1,0:T(8,128)S(1)} %get-tuple-element.39), channel_id=1, source_target_pairs={{0,96},{1,97},{2,98},{3,99},{4,36},{5,37},{6,38},{7,39},{8,104},{9... | collective-permute-start | bytes 208904 | tf_op jit(solution)/shard_map/ppermute | solution.py:429
  53.4 4.9 %collective-permute-start.12 = (f32[136,128]{1,0:T(8,128)S(1)}, f32[136,128]{1,0:T(8,128)S(1)}, u32[]{:S(2)}, u32[]{:S(2)}) collective-permute-start(f32[136,128]{1,0:T(8,128)S(1)} %add_add_fusion.refs_2_), channel_id=1, source_target_pairs={{0,24},{1,25},{2,26},{3,27},{4,12},{5,13},{6,14},{7,15},{8,0},{9,1... | collective-permute-start | bytes 208904 | tf_op jit(solution)/shard_map/ppermute | solution.py:429
  54.7 4.9 %collective-permute-start.11 = (f32[136,128]{1,0:T(8,128)S(1)}, f32[136,128]{1,0:T(8,128)S(1)}, u32[]{:S(2)}, u32[]{:S(2)}) collective-permute-start(f32[136,128]{1,0:T(8,128)S(1)} %add_add_fusion.refs_2_), channel_id=1, source_target_pairs={{0,8},{1,9},{2,10},{3,11},{4,20},{5,21},{6,22},{7,23},{8,16},{9,17... | collective-permute-start | bytes 208904 | tf_op jit(solution)/shard_map/ppermute | solution.py:429
  57.1 3.2 %collective-permute-start.10 = (f32[136,128]{1,0:T(8,128)S(1)}, f32[136,128]{1,0:T(8,128)S(1)}, u32[]{:S(2)}, u32[]{:S(2)}) collective-permute-start(f32[136,128]{1,0:T(8,128)S(1)} %add_add_fusion.refs_2_), channel_id=1, source_target_pairs={{0,16},{1,17},{2,18},{3,19},{4,28},{5,29},{6,30},{7,31},{8,24},{9,... | collective-permute-start | bytes 208904 | tf_op jit(solution)/shard_map/ppermute | solution.py:429
  61.7 3.8 %collective-permute-start.13 = (f32[4,8,128]{2,1,0:T(8,128)S(1)}, f32[4,8,128]{2,1,0:T(8,128)S(1)}, u32[]{:S(2)}, u32[]{:S(2)}) collective-permute-start(f32[4,8,128]{2,1,0:T(8,128)S(1)} %get-tuple-element.41), channel_id=1, source_target_pairs={{0,4},{1,5},{2,6},{3,7},{4,0},{5,1},{6,2},{7,3},{8,12},{9,13},{10,... | collective-permute-start | bytes 49160 | tf_op jit(solution)/shard_map/ppermute | solution.py:429

commit v8 on v7

--- a/solution.py
+++ b/solution.py
@@ -470,8 +470,11 @@
     part1 = send(both1, "z", 1)
     part3 = send(both3, "z", 3)
     keys = after(keys, both3)
-    keep, give = take(0, 0, 1)
-    both0 = keep + send(give, "c", 1)
+    give, = take(0, 1)
+    got0 = send(give, "c", 1)
+    keys = after(keys, give)
+    keep, = take(0, 0)
+    both0 = keep + got0
     rank = after(rank, keep, part1, part3)
     parts = [part2, part1, part3, both0]
     rels = (2, 1, 3)

time: 77.8 us -> 77.4 us (level)
    pallas_call x6 -> x7, Pallas kernels: 21.4 us -> 22 us  [slots_call(): pl.pallas_call(lambda *refs: slots_kernel(scale, off, cores, *refs), out_...]
  transfers between devices with their start and end apart: 14 -> 14, of which waited for: 7 -> 8; matrix products, arithmetic and copies ran while one was open for 0% -> 0% of each run, Pallas kernels for 23% -> 24%
where the time goes in v8:
time: 77.4 us; the launch traced here: 76.8 us
  Pallas kernels  36.4 us (47%)
  starting transfers between devices  21 us (27%)
  blocking collectives  10.5 us (14%)
  waiting for transfers between devices  7.81 us (10%)
  between operations  0.8 us (1%)
    pallas_call x7, Pallas kernels, slots_call(): pl.pallas_call(lambda *refs: slots_kernel(scale, off, cores, *refs), out_...  22 us
    ppermute x14, starting transfers between devices, send(): return lax.ppermute(v, AXES, shift(axis, off))  21 us
    all_to_all x1, blocking collectives, shards(): lax.all_to_all(gram, AXES, 0, 0, tiled=True, axis_index_groups=planes())  10.5 us
    pallas_call x1, Pallas kernels, prepare_call(): pl.pallas_call(prepare_kernel, out_shape=(jax.ShapeDtypeStruct((256, LANE...  8.41 us
    ppermute x14, waiting for transfers between devices, send(): return lax.ppermute(v, AXES, shift(axis, off))  7.81 us
    pallas_call x2, Pallas kernels, order_call(): pl.pallas_call(lambda *refs: kernel(rel, *refs), out_shape=(table,) + (ou...  3.87 us
  transfers between devices with their start and end apart: 14, of which 8 were waited for; matrix products, arithmetic and copies ran while one was open for 0% of the time, Pallas kernels for 24%

profile of v8, /device:TPU:1, one launch (start us, length us, event | category | flops | bytes accessed | tf_op | source)
XLA Modules:
  0.0 76.8 jit_solution(17865946892187872447)
XLA Ops:
  0.6 0.1 stack.26.pos_ref.refs_0_
  0.7 8.4 %sort_and_walsh.1 = (s32[256,128]{1,0:T(8,128)S(1)}, s32[4,128]{1,0:T(4,128)S(1)}, s32[128,128]{1,0:T(8,128)S(1)}, f32[8576,128]{1,0:T(8,128)S(1)}, f32[536,128]{1,0:T(8,128)S(1)}) custom-call(s32[8]{0:T(128)S(1)} %stack.26.pos_ref.refs_0_, s32[16,2,8,128]{3,2,1,0:T(8,128)} %bitcast.19, f32[8192,128]{1,0:T(8,128)} %bitcast.16, f32[512,128]{1,0:T(8,128)} %bitcast.17, ...), custom_call_target="tpu_custom_call" | custom-call | flops 1000000 | bytes 1000000 | tf_op jit(solution)/shard_map/sort_and_walsh/pallas_call | solution.py:218
  9.1 5.0 %take_slots_201.1 = (f32[544,128]{1,0:T(8,128)S(1)}, f32[544,128]{1,0:T(8,128)S(1)}) custom-call(s32[8]{0:T(128)S(1)} %stack.26.pos_ref.refs_0_, s32[4,128]{1,0:T(4,128)S(1)} %get-tuple-element.22.refs_1_, f32[8576,128]{1,0:T(8,128)S(1)} %get-tuple-element.23.refs_2_, f32[536,128]{1,0:T(8,128)S(1)} %get-tuple-element.24.refs_3_, ...), custom_call_target="tpu_custom_call" | custom-call | flops 1000000 | bytes 1000000 | tf_op jit(solution)/shard_map/take_slots_201/pallas_call | solution.py:307
  14.2 1.5 %collective-permute-start = (f32[544,128]{1,0:T(8,128)S(1)}, f32[544,128]{1,0:T(8,128)S(1)}, u32[]{:S(2)}, u32[]{:S(2)}) collective-permute-start(f32[544,128]{1,0:T(8,128)S(1)} %get-tuple-element.27), channel_id=1, source_target_pairs={{0,4},{1,5},{2,6},{3,7},{4,0},{5,1},{6,2},{7,3},{8,12},{9,13},{10,... | collective-permute-start | bytes 835592 | tf_op jit(solution)/shard_map/ppermute | solution.py:429
  15.7 2.9 %take_slots_11.1 = f32[544,128]{1,0:T(8,128)S(1)} custom-call(s32[8]{0:T(128)S(1)} %stack.26.pos_ref.refs_0_, s32[4,128]{1,0:T(4,128)S(1)} %get-tuple-element.22.refs_1_, f32[8576,128]{1,0:T(8,128)S(1)} %get-tuple-element.23.refs_2_, f32[536,128]{1,0:T(8,128)S(1)} %get-tuple-element.24.refs_3_, s32[256,128]{1,0:T(8,128)S(1)} %get-tuple-element.32.refs_4_), custom_call_target="tpu_custom_call" | custom-call | flops 1000000 | bytes 1000000 | tf_op jit(solution)/shard_map/take_slots_11/pallas_call | solution.py:307
  18.6 0.1 collective-permute-start.1
  18.7 0.0 collective-permute-done
  18.7 4.0 %collective-permute-start.2 = (f32[544,128]{1,0:T(8,128)S(1)}, f32[544,128]{1,0:T(8,128)S(1)}, u32[]{:S(2)}, u32[]{:S(2)}) collective-permute-start(f32[544,128]{1,0:T(8,128)S(1)} %add.28), channel_id=1, source_target_pairs={{0,2},{1,3},{2,0},{3,1},{4,7},{5,4},{6,5},{7,6},{8,10},{9,11},{10,... | collective-permute-start | bytes 835592 | tf_op jit(solution)/shard_map/ppermute | solution.py:429
  22.8 2.8 %take_slots_10.1 = f32[544,128]{1,0:T(8,128)S(1)} custom-call(s32[8]{0:T(128)S(1)} %stack.26.pos_ref.refs_0_, s32[4,128]{1,0:T(4,128)S(1)} %get-tuple-element.22.refs_1_, f32[8576,128]{1,0:T(8,128)S(1)} %get-tuple-element.23.refs_2_, f32[536,128]{1,0:T(8,128)S(1)} %get-tuple-element.24.refs_3_, s32[256,128]{1,0:T(8,128)S(1)} %get-tuple-element.32.refs_4_), custom_call_target="tpu_custom_call" | custom-call | flops 1000000 | bytes 1000000 | tf_op jit(solution)/shard_map/take_slots_10/pallas_call | solution.py:307
  25.6 0.0 collective-permute-done.1
  25.6 2.8 %take_slots_31.1 = f32[544,128]{1,0:T(8,128)S(1)} custom-call(s32[8]{0:T(128)S(1)} %stack.26.pos_ref.refs_0_, s32[4,128]{1,0:T(4,128)S(1)} %get-tuple-element.22.refs_1_, f32[8576,128]{1,0:T(8,128)S(1)} %get-tuple-element.23.refs_2_, f32[536,128]{1,0:T(8,128)S(1)} %get-tuple-element.24.refs_3_, s32[256,128]{1,0:T(8,128)S(1)} %get-tuple-element.32.refs_4_), custom_call_target="tpu_custom_call" | custom-call | flops 1000000 | bytes 1000000 | tf_op jit(solution)/shard_map/take_slots_31/pallas_call | solution.py:307
  28.4 0.7 collective-permute-start.3
  29.1 0.0 collective-permute-start.4
  29.1 0.1 collective-permute-done.2.refs_2_
  29.2 2.8 %take_slots_30.1 = f32[544,128]{1,0:T(8,128)S(1)} custom-call(s32[8]{0:T(128)S(1)} %stack.26.pos_ref.refs_0_, s32[4,128]{1,0:T(4,128)S(1)} %get-tuple-element.22.refs_1_, f32[8576,128]{1,0:T(8,128)S(1)} %get-tuple-element.23.refs_2_, f32[536,128]{1,0:T(8,128)S(1)} %get-tuple-element.24.refs_3_, s32[256,128]{1,0:T(8,128)S(1)} %get-tuple-element.32.refs_4_), custom_call_target="tpu_custom_call" | custom-call | flops 1000000 | bytes 1000000 | tf_op jit(solution)/shard_map/take_slots_30/pallas_call | solution.py:307
  32.0 0.0 collective-permute-done.3
  32.1 0.8 %collective-permute-start.5 = (f32[544,128]{1,0:T(8,128)S(1)}, f32[544,128]{1,0:T(8,128)S(1)}, u32[]{:S(2)}, u32[]{:S(2)}) collective-permute-start(f32[544,128]{1,0:T(8,128)S(1)} %add.30), channel_id=1, source_target_pairs={{0,3},{1,0},{2,1},{3,2},{4,5},{5,6},{6,7},{7,4},{8,11},{9,8},{10,9... | collective-permute-start | bytes 835592 | tf_op jit(solution)/shard_map/ppermute | solution.py:429
  32.9 2.9 %take_slots_01.1 = f32[544,128]{1,0:T(8,128)S(1)} custom-call(s32[8]{0:T(128)S(1)} %stack.26.pos_ref.refs_0_, s32[4,128]{1,0:T(4,128)S(1)} %get-tuple-element.22.refs_1_, f32[8576,128]{1,0:T(8,128)S(1)} %get-tuple-element.23.refs_2_, f32[536,128]{1,0:T(8,128)S(1)} %get-tuple-element.24.refs_3_, s32[256,128]{1,0:T(8,128)S(1)} %get-tuple-element.32.refs_4_), custom_call_target="tpu_custom_call" | custom-call | flops 1000000 | bytes 1000000 | tf_op jit(solution)/shard_map/take_slots_01/pallas_call | solution.py:307
  35.8 0.0 copy-start
  35.8 2.6 %collective-permute-start.6 = (f32[544,128]{1,0:T(8,128)S(1)}, f32[544,128]{1,0:T(8,128)S(1)}, u32[]{:S(2)}, u32[]{:S(2)}) collective-permute-start(f32[544,128]{1,0:T(8,128)S(1)} %take_slots_01.1), channel_id=1, source_target_pairs={{0,4},{1,5},{2,6},{3,7},{4,0},{5,1},{6,2},{7,3},{8,12},{9,13},{10,... | collective-permute-start | bytes 835592 | tf_op jit(solution)/shard_map/ppermute | solution.py:429
  38.4 2.8 %take_slots_00.1 = f32[544,128]{1,0:T(8,128)S(1)} custom-call(s32[8]{0:T(128)S(1)} %stack.26.pos_ref.refs_0_, s32[4,128]{1,0:T(4,128)S(1)} %get-tuple-element.22.refs_1_, f32[8576,128]{1,0:T(8,128)S(1)} %get-tuple-element.23.refs_2_, f32[536,128]{1,0:T(8,128)S(1)} %get-tuple-element.24.refs_3_, s32[256,128]{1,0:T(8,128)S(1)} %get-tuple-element.32.refs_4_), custom_call_target="tpu_custom_call" | custom-call | flops 1000000 | bytes 1000000 | tf_op jit(solution)/shard_map/take_slots_00/pallas_call | solution.py:307
  41.2 0.0 collective-permute-done.4.refs_3_
  41.2 0.9 %collective-permute-done.5.refs_4_ = f32[544,128]{1,0:T(8,128)S(1)} collective-permute-done((f32[544,128]{1,0:T(8,128)S(1)}, f32[544,128]{1,0:T(8,128)S(1)}, u32[]{:S(2)}, u32[]{:S(2)}) %collective-permute-start.5) | collective-permute-done | bytes 278560 | tf_op jit(solution)/shard_map/ppermute | solution.py:429
  42.1 0.0 collective-permute-done.6
  42.1 2.6 %given_order_far.1 = (f32[544,128]{1,0:T(8,128)S(1)}, f32[136,128]{1,0:T(8,128)S(1)}, f32[136,128]{1,0:T(8,128)S(1)}, f32[136,128]{1,0:T(8,128)S(1)}) custom-call(s32[8]{0:T(128)S(1)} %stack.26.pos_ref.refs_0_, s32[128,128]{1,0:T(8,128)S(1)} %get-tuple-element.33.refs_1_, f32[544,128]{1,0:T(8,128)S(1)} %collective-permute-done.2.refs_2_, ...), custom_call_target="tpu_custom_call" | custom-call | flops 1000000 | bytes 1000000 | tf_op jit(solution)/shard_map/given_order_far/pallas_call | solution.py:354
  44.7 2.8 %collective-permute-start.7 = (f32[136,128]{1,0:T(8,128)S(1)}, f32[136,128]{1,0:T(8,128)S(1)}, u32[]{:S(2)}, u32[]{:S(2)}) collective-permute-start(f32[136,128]{1,0:T(8,128)S(1)} %get-tuple-element.35), channel_id=1, source_target_pairs={{0,64},{1,65},{2,66},{3,67},{4,100},{5,101},{6,102},{7,103},{8,72}... | collective-permute-start | bytes 208904 | tf_op jit(solution)/shard_map/ppermute | solution.py:429
  47.5 0.4 collective-permute-start.8
  47.9 0.7 collective-permute-start.9
  48.6 1.3 %given_order_own.1 = f32[136,128]{1,0:T(8,128)S(1)} custom-call(s32[8]{0:T(128)S(1)} %stack.26.pos_ref.refs_0_, s32[128,128]{1,0:T(8,128)S(1)} %get-tuple-element.33.refs_1_, f32[544,128]{1,0:T(8,128)S(1)} %get-tuple-element.34.refs_2_), custom_call_target="tpu_custom_call" | custom-call | flops 1000000 | bytes 1000000 | tf_op jit(solution)/shard_map/given_order_own/pallas_call | solution.py:354
  49.8 0.4 collective-permute-done.7
  50.3 2.0 %collective-permute-done.8 = f32[136,128]{1,0:T(8,128)S(1)} collective-permute-done((f32[136,128]{1,0:T(8,128)S(1)}, f32[136,128]{1,0:T(8,128)S(1)}, u32[]{:S(2)}, u32[]{:S(2)}) %collective-permute-start.8) | collective-permute-done | bytes 69664 | tf_op jit(solution)/shard_map/ppermute | solution.py:429
  52.3 1.5 %collective-permute-done.9 = f32[136,128]{1,0:T(8,128)S(1)} collective-permute-done((f32[136,128]{1,0:T(8,128)S(1)}, f32[136,128]{1,0:T(8,128)S(1)}, u32[]{:S(2)}, u32[]{:S(2)}) %collective-permute-start.9) | collective-permute-done | bytes 69664 | tf_op jit(solution)/shard_map/ppermute | solution.py:429
  53.8 1.3 %collective-permute-start.12 = (f32[136,128]{1,0:T(8,128)S(1)}, f32[136,128]{1,0:T(8,128)S(1)}, u32[]{:S(2)}, u32[]{:S(2)}) collective-permute-start(f32[136,128]{1,0:T(8,128)S(1)} %add_add_fusion.refs_2_), channel_id=1, source_target_pairs={{0,24},{1,25},{2,26},{3,27},{4,12},{5,13},{6,14},{7,15},{8,0},{9,1... | collective-permute-start | bytes 208904 | tf_op jit(solution)/shard_map/ppermute | solution.py:429
  55.1 2.4 %collective-permute-start.11 = (f32[136,128]{1,0:T(8,128)S(1)}, f32[136,128]{1,0:T(8,128)S(1)}, u32[]{:S(2)}, u32[]{:S(2)}) collective-permute-start(f32[136,128]{1,0:T(8,128)S(1)} %add_add_fusion.refs_2_), channel_id=1, source_target_pairs={{0,8},{1,9},{2,10},{3,11},{4,20},{5,21},{6,22},{7,23},{8,16},{9,17... | collective-permute-start | bytes 208904 | tf_op jit(solution)/shard_map/ppermute | solution.py:429
  57.5 1.2 %collective-permute-start.10 = (f32[136,128]{1,0:T(8,128)S(1)}, f32[136,128]{1,0:T(8,128)S(1)}, u32[]{:S(2)}, u32[]{:S(2)}) collective-permute-start(f32[136,128]{1,0:T(8,128)S(1)} %add_add_fusion.refs_2_), channel_id=1, source_target_pairs={{0,16},{1,17},{2,18},{3,19},{4,28},{5,29},{6,30},{7,31},{8,24},{9,... | collective-permute-start | bytes 208904 | tf_op jit(solution)/shard_map/ppermute | solution.py:429
  58.7 0.0 collective-permute-done.12.refs_5_
  58.7 1.3 %collective-permute-done.11.refs_4_ = f32[136,128]{1,0:T(8,128)S(1)} collective-permute-done((f32[136,128]{1,0:T(8,128)S(1)}, f32[136,128]{1,0:T(8,128)S(1)}, u32[]{:S(2)}, u32[]{:S(2)}) %collective-permute-start.11) | collective-permute-done | bytes 69664 | tf_op jit(solution)/shard_map/ppermute | solution.py:429
  60.0 0.7 collective-permute-done.10.refs_3_
  60.7 0.0 copy-done
  60.7 1.4 %rows_and_gram.1 = (f32[17,256]{1,0:T(8,128)}, f32[4,8,128]{2,1,0:T(8,128)S(1)}) custom-call(s32[8]{0:T(128)S(1)} %stack.26.pos_ref.refs_0_, s32[16,2,8,128]{3,2,1,0:T(8,128)S(1)} %bitcast.15, f32[136,128]{1,0:T(8,128)S(1)} %add_add_fusion.refs_2_, f32[136,128]{1,0:T(8,128)S(1)} %collective-permute-done.10.refs_3_, ...), custom_call_target="tpu_custom_call" | custom-call | tf_op jit(solution)/shard_map/rows_and_gram/pallas_call | solution.py:396
  62.1 2.6 %collective-permute-start.13 = (f32[4,8,128]{2,1,0:T(8,128)S(1)}, f32[4,8,128]{2,1,0:T(8,128)S(1)}, u32[]{:S(2)}, u32[]{:S(2)}) collective-permute-start(f32[4,8,128]{2,1,0:T(8,128)S(1)} %get-tuple-element.39), channel_id=1, source_target_pairs={{0,4},{1,5},{2,6},{3,7},{4,0},{5,1},{6,2},{7,3},{8,12},{9,13},{10,... | collective-permute-start | bytes 49160 | tf_op jit(solution)/shard_map/ppermute | solution.py:429
  64.7 0.8 %collective-permute-done.13 = f32[4,8,128]{2,1,0:T(8,128)S(1)} collective-permute-done((f32[4,8,128]{2,1,0:T(8,128)S(1)}, f32[4,8,128]{2,1,0:T(8,128)S(1)}, u32[]{:S(2)}, u32[]{:S(2)}) %collective-permute-start.13) | collective-permute-done | bytes 16416 | tf_op jit(solution)/shard_map/ppermute | solution.py:429
  65.5 10.5 %all_to_all.5.messages = f32[16,8,128]{2,1,0:T(8,128)S(1)} all-to-all(f32[16,8,128]{2,1,0:T(8,128)S(1)} %pad_maximum_fusion), channel_id=1, replica_groups={{0,1,2,3,32,33,34,35,64,65,66,67,96,97,98,99},{4,5,6,7,36,37,38,39,68,6..., dimensions={0} | all-to-all | bytes 131072 | tf_op jit(solution)/shard_map/all_to_all | solution.py:487
  76.0 0.8 own_gram.1
  (7 shorter events, 0.2 us)
Async XLA Ops:
  14.2 4.5 %collective-permute-start = (f32[544,128]{1,0:T(8,128)S(1)}, f32[544,128]{1,0:T(8,128)S(1)}, u32[]{:S(2)}, u32[]{:S(2)}) collective-permute-start(f32[544,128]{1,0:T(8,128)S(1)} %get-tuple-element.27), channel_id=1, source_target_pairs={{0,4},{1,5},{2,6},{3,7},{4,0},{5,1},{6,2},{7,3},{8,12},{9,13},{10,... | collective-permute-start | bytes 835592 | tf_op jit(solution)/shard_map/ppermute | solution.py:429
  18.6 7.0 %collective-permute-start.1 = (f32[544,128]{1,0:T(8,128)S(1)}, f32[544,128]{1,0:T(8,128)S(1)}, u32[]{:S(2)}, u32[]{:S(2)}) collective-permute-start(f32[544,128]{1,0:T(8,128)S(1)} %take_slots_11.1), channel_id=1, source_target_pairs={{0,4},{1,5},{2,6},{3,7},{4,0},{5,1},{6,2},{7,3},{8,12},{9,13},{10,... | collective-permute-start | bytes 835592 | tf_op jit(solution)/shard_map/ppermute | solution.py:429
  18.7 10.5 %collective-permute-start.2 = (f32[544,128]{1,0:T(8,128)S(1)}, f32[544,128]{1,0:T(8,128)S(1)}, u32[]{:S(2)}, u32[]{:S(2)}) collective-permute-start(f32[544,128]{1,0:T(8,128)S(1)} %add.28), channel_id=1, source_target_pairs={{0,2},{1,3},{2,0},{3,1},{4,7},{5,4},{6,5},{7,6},{8,10},{9,11},{10,... | collective-permute-start | bytes 835592 | tf_op jit(solution)/shard_map/ppermute | solution.py:429
  28.4 3.6 %collective-permute-start.3 = (f32[544,128]{1,0:T(8,128)S(1)}, f32[544,128]{1,0:T(8,128)S(1)}, u32[]{:S(2)}, u32[]{:S(2)}) collective-permute-start(f32[544,128]{1,0:T(8,128)S(1)} %take_slots_31.1), channel_id=1, source_target_pairs={{0,4},{1,5},{2,6},{3,7},{4,0},{5,1},{6,2},{7,3},{8,12},{9,13},{10,... | collective-permute-start | bytes 835592 | tf_op jit(solution)/shard_map/ppermute | solution.py:429
  29.1 12.1 %collective-permute-start.4 = (f32[544,128]{1,0:T(8,128)S(1)}, f32[544,128]{1,0:T(8,128)S(1)}, u32[]{:S(2)}, u32[]{:S(2)}) collective-permute-start(f32[544,128]{1,0:T(8,128)S(1)} %add.29), channel_id=1, source_target_pairs={{0,1},{1,2},{2,3},{3,0},{4,6},{5,7},{6,4},{7,5},{8,9},{9,10},{10,1... | collective-permute-start | bytes 835592 | tf_op jit(solution)/shard_map/ppermute | solution.py:429
  32.1 10.0 %collective-permute-start.5 = (f32[544,128]{1,0:T(8,128)S(1)}, f32[544,128]{1,0:T(8,128)S(1)}, u32[]{:S(2)}, u32[]{:S(2)}) collective-permute-start(f32[544,128]{1,0:T(8,128)S(1)} %add.30), channel_id=1, source_target_pairs={{0,3},{1,0},{2,1},{3,2},{4,5},{5,6},{6,7},{7,4},{8,11},{9,8},{10,9... | collective-permute-start | bytes 835592 | tf_op jit(solution)/shard_map/ppermute | solution.py:429
  35.8 24.9 %copy-start = (s32[32768]{0:T(1024)S(1)}, s32[32768]{0:T(1024)}, u32[]{:S(2)}) copy-start(s32[32768]{0:T(1024)} %param.9) | copy-start | bytes 393220
  35.8 6.3 %collective-permute-start.6 = (f32[544,128]{1,0:T(8,128)S(1)}, f32[544,128]{1,0:T(8,128)S(1)}, u32[]{:S(2)}, u32[]{:S(2)}) collective-permute-start(f32[544,128]{1,0:T(8,128)S(1)} %take_slots_01.1), channel_id=1, source_target_pairs={{0,4},{1,5},{2,6},{3,7},{4,0},{5,1},{6,2},{7,3},{8,12},{9,13},{10,... | collective-permute-start | bytes 835592 | tf_op jit(solution)/shard_map/ppermute | solution.py:429
  44.7 5.5 %collective-permute-start.7 = (f32[136,128]{1,0:T(8,128)S(1)}, f32[136,128]{1,0:T(8,128)S(1)}, u32[]{:S(2)}, u32[]{:S(2)}) collective-permute-start(f32[136,128]{1,0:T(8,128)S(1)} %get-tuple-element.35), channel_id=1, source_target_pairs={{0,64},{1,65},{2,66},{3,67},{4,100},{5,101},{6,102},{7,103},{8,72}... | collective-permute-start | bytes 208904 | tf_op jit(solution)/shard_map/ppermute | solution.py:429
  47.5 4.8 %collective-permute-start.8 = (f32[136,128]{1,0:T(8,128)S(1)}, f32[136,128]{1,0:T(8,128)S(1)}, u32[]{:S(2)}, u32[]{:S(2)}) collective-permute-start(f32[136,128]{1,0:T(8,128)S(1)} %get-tuple-element.36), channel_id=1, source_target_pairs={{0,32},{1,33},{2,34},{3,35},{4,68},{5,69},{6,70},{7,71},{8,40},{9,... | collective-permute-start | bytes 208904 | tf_op jit(solution)/shard_map/ppermute | solution.py:429
  47.9 5.9 %collective-permute-start.9 = (f32[136,128]{1,0:T(8,128)S(1)}, f32[136,128]{1,0:T(8,128)S(1)}, u32[]{:S(2)}, u32[]{:S(2)}) collective-permute-start(f32[136,128]{1,0:T(8,128)S(1)} %get-tuple-element.37), channel_id=1, source_target_pairs={{0,96},{1,97},{2,98},{3,99},{4,36},{5,37},{6,38},{7,39},{8,104},{9... | collective-permute-start | bytes 208904 | tf_op jit(solution)/shard_map/ppermute | solution.py:429
  53.8 4.9 %collective-permute-start.12 = (f32[136,128]{1,0:T(8,128)S(1)}, f32[136,128]{1,0:T(8,128)S(1)}, u32[]{:S(2)}, u32[]{:S(2)}) collective-permute-start(f32[136,128]{1,0:T(8,128)S(1)} %add_add_fusion.refs_2_), channel_id=1, source_target_pairs={{0,24},{1,25},{2,26},{3,27},{4,12},{5,13},{6,14},{7,15},{8,0},{9,1... | collective-permute-start | bytes 208904 | tf_op jit(solution)/shard_map/ppermute | solution.py:429
  55.1 4.9 %collective-permute-start.11 = (f32[136,128]{1,0:T(8,128)S(1)}, f32[136,128]{1,0:T(8,128)S(1)}, u32[]{:S(2)}, u32[]{:S(2)}) collective-permute-start(f32[136,128]{1,0:T(8,128)S(1)} %add_add_fusion.refs_2_), channel_id=1, source_target_pairs={{0,8},{1,9},{2,10},{3,11},{4,20},{5,21},{6,22},{7,23},{8,16},{9,17... | collective-permute-start | bytes 208904 | tf_op jit(solution)/shard_map/ppermute | solution.py:429
  57.5 3.2 %collective-permute-start.10 = (f32[136,128]{1,0:T(8,128)S(1)}, f32[136,128]{1,0:T(8,128)S(1)}, u32[]{:S(2)}, u32[]{:S(2)}) collective-permute-start(f32[136,128]{1,0:T(8,128)S(1)} %add_add_fusion.refs_2_), channel_id=1, source_target_pairs={{0,16},{1,17},{2,18},{3,19},{4,28},{5,29},{6,30},{7,31},{8,24},{9,... | collective-permute-start | bytes 208904 | tf_op jit(solution)/shard_map/ppermute | solution.py:429
  62.1 3.4 %collective-permute-start.13 = (f32[4,8,128]{2,1,0:T(8,128)S(1)}, f32[4,8,128]{2,1,0:T(8,128)S(1)}, u32[]{:S(2)}, u32[]{:S(2)}) collective-permute-start(f32[4,8,128]{2,1,0:T(8,128)S(1)} %get-tuple-element.39), channel_id=1, source_target_pairs={{0,4},{1,5},{2,6},{3,7},{4,0},{5,1},{6,2},{7,3},{8,12},{9,13},{10,... | collective-permute-start | bytes 49160 | tf_op jit(solution)/shard_map/ppermute | solution.py:429
